TPU v7x, 512 devices: a whole 4x4x16 slice. The times are simulated.
512 devices in a mesh: atom: 32 (over z, core), energy: 16 (over y, x).
Axes of the slice: x: 4, y: 4, z: 16, core: 2. Of those that a mesh axis runs over, the one named last changes fastest.
Arguments:
- green: bfloat16 [256, 200, 2048], P('atom', None, 'energy'), may hold values from -6 to 6
- coupling: bfloat16 [512, 800], P('atom'), may hold values from -0.625 to 0.625
- pairs: int32 [512, 2], P('atom'), may hold values from 0 to 255, as said below
- counts: int32 [32], P('atom'), may hold values from 8 to 16, as said below
- occupation: float32 [8], replicated, may hold values from 0.05 to 2
- offsets: int32 [8], replicated, may hold values from 1 to 64, as said below
Outputs:
- sigma: bfloat16 [256, 200, 2048], P('atom', None, 'energy')
Inputs may be any that keep to these rules, and one draw needn't show every extreme that they name: `pairs`: slot s lies in partition p = s // 16; its first atom is one of partition p, atoms p * 8 to (p + 1) * 8 - 1. Its second atom is another atom of partition p, or one of the first 2 atoms of partition p + 1 (then its first atom is one of the last 2 atoms of partition p), or one of the last 2 atoms of partition p - 1 (then its first atom is one of the first 2 atoms of partition p); in every partition that has such a neighbour some live slot bonds to the farthest of those 2 atoms. `counts`: some partition has all its slots live. `offsets`: some mode has the largest offset.
All inputs are finite; a program needn't handle non-finite values.
Results may differ from a plain program's by a relative error of at most 0.012.
Values may be sent and summed in bfloat16 or wider, within the bound.
No kernel may reach another device: no remote copies, remote signals or barrier semaphores. Data moves between devices by JAX's collectives and lax.ppermute only.
A program may use at most 192 MiB of HBM per device.

v0:
```python
import functools

import jax
import jax.numpy as jnp
from jax import lax
from jax.experimental import pallas as pl
from jax.experimental.pallas import tpu as pltpu
from jax.sharding import PartitionSpec as P

NORB = 10
MODES = 8
KMAX = 64
SQ = NORB * NORB
ROWS = 104
LANES = 128
DEPTH = MODES * LANES
BF = jnp.bfloat16
F32 = jnp.float32
VMEM = pl.BlockSpec(memory_space=pltpu.VMEM)
SMEM = pl.BlockSpec(memory_space=pltpu.SMEM)


def iota(shape, dim):
    return lax.broadcasted_iota(jnp.int32, shape, dim)


def build_kernel(occ_ref, off_ref, cnt_ref, coup_ref, t_ref, tt_ref, s_ref, cm, v, c12):
    slots = coup_ref.shape[0]
    coup = coup_ref[...].astype(F32)
    width = 7 * LANES
    coup = jnp.concatenate([coup, jnp.zeros((slots, width - MODES * SQ), F32)], axis=1)
    lane = iota((slots, LANES), 1)
    for m in range(MODES):
        part = coup if m == 0 else pltpu.roll(coup, width - m * SQ, 1)
        cm[m * slots : (m + 1) * slots, :] = jnp.where(lane < SQ, part[:, :LANES], 0.0)

    ij = iota((LANES, LANES), 0)
    jk = iota((LANES, LANES), 1)
    valid = (ij < SQ) & (jk < SQ)
    i_of, j_of = ij // NORB, ij % NORB
    j_to, k_to = jk // NORB, jk % NORB
    row = iota((16, LANES), 0) % NORB
    col = iota((16, LANES), 1)
    sub = iota((8, LANES), 0)

    def expand(masked, keep, other, out_ref):
        spread = jnp.concatenate(
            [
                jnp.where(valid & (other == j_to), 1.0, 0.0),
                jnp.where(valid & (other == k_to), 1.0, 0.0),
            ],
            axis=1,
        ).astype(BF)
        keep = jnp.where(keep == row, 1.0, 0.0)

        def fill(s, carry):
            for m in range(MODES):
                line = cm[pl.ds(m * slots + s, 1), :]
                v[pl.ds(pl.multiple_of(s * (16 * MODES) + m * 16, 16), 16), :] = (
                    jnp.broadcast_to(line, (16, LANES)) * keep
                ).astype(BF)
            return carry

        lax.fori_loop(0, cnt_ref[0], fill, 0)
        for part in range(slots // 2):
            at = part * 32 * MODES
            c12[at : at + 32 * MODES, :] = jnp.dot(
                v[at : at + 32 * MODES, :], spread, preferred_element_type=F32
            )

        def product(s, carry):
            for m in range(MODES):
                base = pl.multiple_of(s * (16 * MODES) + m * 16, 16)
                first = c12[pl.ds(base, 16), :LANES]
                second = c12[pl.ds(base, 16), LANES:]
                turns = [
                    second[0:8],
                    second[8:16],
                    pltpu.roll(second, 10, 0)[0:8],
                    pltpu.roll(second, 12, 0)[0:8],
                    pltpu.roll(second, 14, 0)[0:8],
                ]
                spreads = [jnp.broadcast_to(first[i : i + 1], (8, LANES)) for i in range(NORB)]
                rows = []
                for g in range(ROWS // 8):
                    lo = 8 * g // NORB
                    hi = min((8 * g + 7) // NORB, NORB - 1)
                    left = spreads[lo]
                    if hi != lo:
                        left = jnp.where(sub < NORB * hi - 8 * g, left, spreads[hi])
                    rows.append(left * turns[g % 5])
                out_ref[s, :, m * LANES : (m + 1) * LANES] = jnp.concatenate(rows, axis=0).astype(BF)
            return carry

        lax.fori_loop(0, cnt_ref[0], product, 0)

    v[...] = jnp.zeros(v.shape, BF)
    expand(cm, col // NORB, j_of, t_ref)
    expand(cm, col % NORB, i_of, tt_ref)

    e_in = iota((2 * LANES, LANES), 0)
    e_out = iota((2 * LANES, LANES), 1)
    low = jnp.where(e_in < 128, e_in, jnp.where(e_in < 192, e_in - 192, e_in - 64))
    high = jnp.where(e_in < 128, e_in, jnp.where(e_in < 192, e_in, e_in - 256))
    for m in range(MODES):
        occ = occ_ref[m]
        step = off_ref[m]
        for which, e_of in enumerate((low, high)):
            s_ref[which, :, m * LANES : (m + 1) * LANES] = jnp.where(
                e_of == e_out - step, occ, jnp.where(e_of == e_out + step, occ + 1.0, 0.0)
            ).astype(BF)


def shift_atom(center, halo, s_ref, which, gf, store):
    gf[0:200, :LANES] = center.astype(F32)
    gf[0:200, LANES:] = halo.astype(F32)
    lhs = jnp.concatenate([gf[0:104, :], gf[100:204, :]], axis=0).astype(BF)
    for t in range(MODES // 2):
        out = jnp.dot(lhs, s_ref[which, :, t * 256 : (t + 1) * 256], preferred_element_type=F32)
        for mm in range(2):
            for r in range(2):
                store(
                    2 * t + mm,
                    r,
                    out[r * ROWS : (r + 1) * ROWS, mm * LANES : (mm + 1) * LANES].astype(BF),
                )


def halo_of(fr_ref, fl_ref, x):
    left = iota((200, LANES), 1) < 64
    a = fr_ref[x % 4]
    b = fl_ref[x % 4]
    return jnp.where(left, a, b) if x < 4 else jnp.where(left, b, a)


def prepare(x_ref, gf, count):
    gf[200:208, :] = jnp.zeros((8, 256), F32)
    for x in range(count):
        for m in range(MODES):
            x_ref[x, m * LANES + 96 : (m + 1) * LANES, :] = jnp.zeros((32, 256), BF)


def store_in(x_ref, at):
    def store(m, r, value):
        x_ref[at, m * LANES : m * LANES + ROWS, r * LANES : (r + 1) * LANES] = value

    return store


def pack_rows(total, gf):
    gf[0:ROWS, :LANES] = total[:, :LANES]
    gf[SQ : SQ + ROWS, :LANES] = total[:, LANES:]
    return gf[0:200, :LANES].astype(BF)


def rim_kernel(
    cnt_ref, fst_ref, snd_ref, odd_ref, g_ref, fr_ref, fl_ref, s_ref, tt_ref, cross_ref, near_ref, x, part, gf
):
    prepare(x, gf, 4)
    rims = (0, 1, 6, 7)
    halos = []
    for at, atom in enumerate(rims):
        halo = halo_of(fr_ref, fl_ref, atom)
        halos.append(halo)
        shift_atom(g_ref[atom], halo, s_ref, atom // 4, gf, store_in(x, at))
    part[...] = jnp.zeros(part.shape, F32)

    def visit(s, carry):
        second = snd_ref[s]
        first = fst_ref[s]

        @pl.when((second < 0) | (second >= 8))
        def _():
            to = jnp.where(second < 0, second + 2, second - 6)
            of = jnp.where(first >= 4, first - 4, first)
            part[to] = part[to] + jnp.dot(tt_ref[s], x[of], preferred_element_type=F32)

        return carry

    lax.fori_loop(0, cnt_ref[0], visit, 0)
    odd = odd_ref[0]

    def fill(ref, side):
        for j in range(2):
            ref[j] = g_ref[6 * side + j]
            ref[2 + j] = halos[2 * side + j]
            ref[4 + j] = pack_rows(part[2 * side + j], gf)

    @pl.when(odd == 1)
    def _():
        fill(cross_ref, 1)
        fill(near_ref, 0)

    @pl.when(odd == 0)
    def _():
        fill(cross_ref, 0)
        fill(near_ref, 1)


def local_kernel(cnt_ref, fst_ref, snd_ref, g_ref, fr_ref, fl_ref, s_ref, t_ref, tt_ref, acc, x, gf):
    prepare(x, gf, 8)
    for atom in range(8):
        shift_atom(g_ref[atom], halo_of(fr_ref, fl_ref, atom), s_ref, atom // 4, gf, store_in(x, atom))
    acc[...] = jnp.zeros(acc.shape, F32)

    def visit(s, carry):
        second = snd_ref[s]
        first = fst_ref[s]

        @pl.when((second >= 0) & (second < 8))
        def _():
            acc[first] = acc[first] + jnp.dot(t_ref[s], x[second], preferred_element_type=F32)
            acc[second] = acc[second] + jnp.dot(tt_ref[s], x[first], preferred_element_type=F32)

        return carry

    lax.fori_loop(0, cnt_ref[0], visit, 0)


def final_kernel(
    cnt_ref, fst_ref, snd_ref, odd_ref, cross_ref, near_ref, s_ref, t_ref, acc_ref, out_ref, x, acc, gf
):
    prepare(x, gf, 4)
    odd = odd_ref[0]

    def take(ref, side):
        for j in range(2):
            shift_atom(ref[j], ref[2 + j], s_ref, 1 - side, gf, store_in(x, 2 * side + j))

    @pl.when(odd == 1)
    def _():
        take(cross_ref, 1)
        take(near_ref, 0)

    @pl.when(odd == 0)
    def _():
        take(cross_ref, 0)
        take(near_ref, 1)

    acc[...] = acc_ref[...]

    def visit(s, carry):
        second = snd_ref[s]
        first = fst_ref[s]

        @pl.when((second < 0) | (second >= 8))
        def _():
            of = jnp.where(second < 0, second + 2, second - 6)
            acc[first] = acc[first] + jnp.dot(t_ref[s], x[of], preferred_element_type=F32)

        return carry

    lax.fori_loop(0, cnt_ref[0], visit, 0)
    for atom in range(8):
        gf[0:ROWS, :LANES] = acc[atom, :, :LANES]
        gf[SQ : SQ + ROWS, :LANES] = acc[atom, :, LANES:]
        total = gf[0:200, :LANES]
        if atom in (0, 1, 6, 7):
            side = atom // 4
            j = atom - 6 * side
            got = jnp.where(odd == side, cross_ref[4 + j].astype(F32), near_ref[4 + j].astype(F32))
            total = total + got
        out_ref[atom] = total.astype(BF)


def swap(value, axis, start):
    count = lax.axis_size(axis)
    pairs = [(i, i + 1) for i in range(start, count - 1, 2)]
    return lax.ppermute(value, axis, pairs + [(b, a) for a, b in pairs])


def step_of(value, axis, by):
    count = lax.axis_size(axis)
    return lax.ppermute(value, axis, [(i, i + by) for i in range(count) if 0 <= i + by < count])


def call(kernel, outs, scratch, flops, moved, specs):
    return pl.pallas_call(
        kernel,
        out_shape=outs,
        in_specs=specs,
        out_specs=jax.tree.map(lambda _: VMEM, outs),
        scratch_shapes=scratch,
        compiler_params=pltpu.CompilerParams(vmem_limit_bytes=40 * 1024 * 1024),
        cost_estimate=pl.CostEstimate(flops=flops, bytes_accessed=moved, transcendentals=0),
    )


def per_device(green, coupling, pairs, counts, occupation, offsets):
    atoms, slab, e_dev = green.shape
    slots = pairs.shape[0]
    part = lax.axis_index("atom")
    rel = pairs - part * atoms
    first, second = rel[:, 0], rel[:, 1]
    odd = jnp.reshape(part % 2, (1,)).astype(jnp.int32)
    half = atoms // 2
    to_right = jnp.concatenate([green[:half, :, KMAX:], green[half:, :, KMAX:]], axis=2)
    to_left = jnp.concatenate([green[half:, :, :KMAX], green[:half, :, :KMAX]], axis=2)
    fr = step_of(to_right, "energy", 1)
    fl = step_of(to_left, "energy", -1)

    shape = jax.ShapeDtypeStruct
    tens = shape((slots, ROWS, DEPTH), BF)
    gf = pltpu.VMEM((208, 256), F32)
    t, tt, s = call(
        build_kernel,
        (tens, tens, shape((2, 256, DEPTH), BF)),
        [
            pltpu.VMEM((MODES * slots, LANES), F32),
            pltpu.VMEM((MODES * slots * 16, LANES), BF),
            pltpu.VMEM((MODES * slots * 16, 256), F32),
        ],
        int(3e9),
        int(8e6),
        [SMEM, SMEM, SMEM, VMEM],
    )(occupation, offsets, counts, coupling)

    payload = shape((6, slab, e_dev), BF)
    cross, near = call(
        rim_kernel,
        (payload, payload),
        [pltpu.VMEM((4, DEPTH, 256), BF), pltpu.VMEM((4, ROWS, 256), F32), gf],
        int(1e9),
        int(1e6),
        [SMEM] * 4 + [VMEM] * 5,
    )(counts, first, second, odd, green, fr, fl, s, tt)
    cross = swap(cross, "atom", 1)
    near = swap(near, "atom", 0)

    acc = call(
        local_kernel,
        shape((atoms, ROWS, 256), F32),
        [pltpu.VMEM((8, DEPTH, 256), BF), gf],
        int(3e9),
        int(1e6),
        [SMEM] * 3 + [VMEM] * 6,
    )(counts, first, second, green, fr, fl, s, t, tt)

    return call(
        final_kernel,
        shape((atoms, slab, e_dev), BF),
        [pltpu.VMEM((4, DEPTH, 256), BF), pltpu.VMEM((atoms, ROWS, 256), F32), gf],
        int(1e9),
        int(1e6),
        [SMEM] * 4 + [VMEM] * 5,
    )(counts, first, second, odd, cross, near, s, t, acc)


def solution(mesh):
    placed = (P("atom", None, "energy"), P("atom", None), P("atom", None), P("atom"), P(), P())
    return jax.shard_map(
        per_device, mesh=mesh, in_specs=placed, out_specs=P("atom", None, "energy"), check_vma=False
    )
```

profile of v0, /device:TPU:249, one launch (start us, length us, event | category | flops | bytes accessed | tf_op | source)
XLA Modules:
  0.0 36.3 jit_solution(9377236286285449111)
XLA Ops:
  0.0 1.4 %fusion = (bf16[4,200,64]{2,1,0:T(8,128)(2,1)S(1)}, bf16[4,200,64]{2,1,0:T(8,128)(2,1)S(1)}, bf16[4,200,64]{2,1,0:T(8,128)(2,1)S(1)}, bf16[4,200,64]{2,1,0:T(8,128)(2,1)S(1)}) fusion(bf16[8,200,128]{2,1,0:T(8,128)(2,1)} %g_ref.3), kind=kLoop, calls=%fused_computation.5 | loop fusion | bytes 819200 | tf_op jit(solution)/shard_map/slice | solution.py:298
  1.4 0.1 pad_maximum_fusion.1
  1.5 4.6 %collective-permute-start.1 = (bf16[4,200,128]{2,1,0:T(8,128)(2,1)S(1)}, bf16[4,200,128]{2,1,0:T(8,128)(2,1)S(1)}, u32[]{:S(2)}, u32[]{:S(2)}) collective-permute-start(bf16[4,200,128]{2,1,0:T(8,128)(2,1)S(1)} %pad_maximum_fusion.1), channel_id=1, source_target_pairs={{1,0},{2,1},{3,2},{4,3},{5,4},{6,5},{7,6},{8,7},{9,8},{10,9},{11,1... | collective-permute-start | bytes 614408 | tf_op jit(solution)/shard_map/ppermute | solution.py:274
  6.1 0.1 pad_maximum_fusion
  6.3 1.9 %collective-permute-start = (bf16[4,200,128]{2,1,0:T(8,128)(2,1)S(1)}, bf16[4,200,128]{2,1,0:T(8,128)(2,1)S(1)}, u32[]{:S(2)}, u32[]{:S(2)}) collective-permute-start(bf16[4,200,128]{2,1,0:T(8,128)(2,1)S(1)} %pad_maximum_fusion), channel_id=1, source_target_pairs={{0,1},{1,2},{2,3},{3,4},{4,5},{5,6},{6,7},{7,8},{8,9},{9,10},{10,1... | collective-permute-start | bytes 614408 | tf_op jit(solution)/shard_map/ppermute | solution.py:274
  8.8 0.7 %broadcast_subtract_fusion = s32[16,2]{0,1:T(2,128)S(1)} fusion(s32[16,2]{0,1:T(2,128)} %param.8, s32[]{:T(128)S(6)} %mul.3), kind=kLoop, calls=%fused_computation.4 | loop fusion | flops 32 | bytes 260 | tf_op jit(solution)/shard_map/sub | solution.py:293
  9.5 0.0 copy-start.1
  9.5 0.7 %copy-done.1 = bf16[16,800]{1,0:T(8,128)(2,1)S(1)} copy-done((bf16[16,800]{1,0:T(8,128)(2,1)S(1)}, bf16[16,800]{1,0:T(8,128)(2,1)}, u32[]{:S(2)}) %copy-start.1) | copy-done | bytes 25624
  10.3 0.0 copy-start.2
  10.3 0.7 %copy-done.2 = f32[8]{0:T(128)S(1)} copy-done((f32[8]{0:T(128)S(1)}, f32[8]{0:T(128)}, u32[]{:S(2)}) %copy-start.2) | copy-done | bytes 56
  10.9 0.0 copy-start.3
  10.9 0.7 %copy-done.3 = s32[8]{0:T(128)S(1)} copy-done((s32[8]{0:T(128)S(1)}, s32[8]{0:T(128)}, u32[]{:S(2)}) %copy-start.3) | copy-done | bytes 56
  11.6 0.0 copy-start
  11.6 4.1 %shard_map.64 = (bf16[16,104,1024]{2,1,0:T(8,128)(2,1)S(1)}, bf16[16,104,1024]{2,1,0:T(8,128)(2,1)S(1)}, bf16[2,256,1024]{2,1,0:T(8,128)(2,1)S(1)}) custom-call(f32[8]{0:T(128)S(1)} %copy-done.2, s32[8]{0:T(128)S(1)} %copy-done.3, s32[1]{0:T(128)S(6)} %copy.7.cnt_ref, bf16[16,800]{1,0:T(8,128)(2,1)S(1)} %copy-done.1), custom_call_target="tpu_custom_call" | custom-call | flops 3000000000 | bytes 8000000 | tf_op jit(solution)/shard_map/pallas_call | solution.py:305
  15.7 0.0 collective-permute-done.1.fl_ref
  15.8 0.1 collective-permute-done.fr_ref
  15.9 0.0 copy-done
  15.9 3.4 %shard_map.65 = (bf16[6,200,128]{2,1,0:T(8,128)(2,1)S(1)}, bf16[6,200,128]{2,1,0:T(8,128)(2,1)S(1)}) custom-call(s32[1]{0:T(128)S(6)} %copy.7.cnt_ref, s32[16]{0:T(128)S(1)} %get-tuple-element.20.fst_ref, s32[16]{0:T(128)S(1)} %get-tuple-element.19.snd_ref, s32[1]{0:T(128)} %bitcast.2.odd_ref, bf16[8,200,128]{2,1,0:T(8,128)(2,1)S(1)} %copy-done, ...), custom_call_target="tpu_custom_call" | custom-call | flops 1000000000 | bytes 1000000 | tf_op jit(solution)/shard_map/pallas_call | solution.py:319
  19.3 6.2 %collective-permute-start.2 = (bf16[6,200,128]{2,1,0:T(8,128)(2,1)S(1)}, bf16[6,200,128]{2,1,0:T(8,128)(2,1)S(1)}, u32[]{:S(2)}, u32[]{:S(2)}) collective-permute-start(bf16[6,200,128]{2,1,0:T(8,128)(2,1)S(1)} %get-tuple-element.12), channel_id=1, source_target_pairs={{16,32},{48,64},{80,96},{112,128},{144,160},{176,192},{208,224},{2... | collective-permute-start | bytes 921608 | tf_op jit(solution)/shard_map/ppermute | solution.py:269
  25.4 1.9 %collective-permute-start.3 = (bf16[6,200,128]{2,1,0:T(8,128)(2,1)S(1)}, bf16[6,200,128]{2,1,0:T(8,128)(2,1)S(1)}, u32[]{:S(2)}, u32[]{:S(2)}) collective-permute-start(bf16[6,200,128]{2,1,0:T(8,128)(2,1)S(1)} %get-tuple-element.13), channel_id=1, source_target_pairs={{0,16},{32,48},{64,80},{96,112},{128,144},{160,176},{192,208},{224... | collective-permute-start | bytes 921608 | tf_op jit(solution)/shard_map/ppermute | solution.py:269
  27.4 4.7 %shard_map.66.acc_ref = f32[8,104,256]{2,1,0:T(8,128)S(1)} custom-call(s32[1]{0:T(128)S(6)} %copy.7.cnt_ref, s32[16]{0:T(128)S(1)} %get-tuple-element.20.fst_ref, s32[16]{0:T(128)S(1)} %get-tuple-element.19.snd_ref, bf16[8,200,128]{2,1,0:T(8,128)(2,1)S(1)} %copy-done, bf16[4,200,128]{2,1,0:T(8,128)(2,1)S(1)} %collective-permute-done.fr_ref, ...), custom_call_target="tpu_custom_call" | custom-call | flops 3000000000 | bytes 1000000 | tf_op jit(solution)/shard_map/pallas_call | solution.py:330
  32.0 0.0 collective-permute-done.2.cross_ref
  32.0 0.0 collective-permute-done.3.near_ref
  32.1 4.2 %shard_map.67 = bf16[8,200,128]{2,1,0:T(8,128)(2,1)} custom-call(s32[1]{0:T(128)S(6)} %copy.7.cnt_ref, s32[16]{0:T(128)S(1)} %get-tuple-element.20.fst_ref, s32[16]{0:T(128)S(1)} %get-tuple-element.19.snd_ref, s32[1]{0:T(128)} %bitcast.2.odd_ref, bf16[6,200,128]{2,1,0:T(8,128)(2,1)S(1)} %collective-permute-done.2.cross_ref, ...), custom_call_target="tpu_custom_call" | custom-call | flops 1000000000 | bytes 1000000 | tf_op jit(solution)/shard_map/pallas_call | solution.py:339
  (1 shorter events, 0.0 us)
Async XLA Ops:
  1.5 14.2 %collective-permute-start.1 = (bf16[4,200,128]{2,1,0:T(8,128)(2,1)S(1)}, bf16[4,200,128]{2,1,0:T(8,128)(2,1)S(1)}, u32[]{:S(2)}, u32[]{:S(2)}) collective-permute-start(bf16[4,200,128]{2,1,0:T(8,128)(2,1)S(1)} %pad_maximum_fusion.1), channel_id=1, source_target_pairs={{1,0},{2,1},{3,2},{4,3},{5,4},{6,5},{7,6},{8,7},{9,8},{10,9},{11,1... | collective-permute-start | bytes 614408 | tf_op jit(solution)/shard_map/ppermute | solution.py:274
  6.3 9.6 %collective-permute-start = (bf16[4,200,128]{2,1,0:T(8,128)(2,1)S(1)}, bf16[4,200,128]{2,1,0:T(8,128)(2,1)S(1)}, u32[]{:S(2)}, u32[]{:S(2)}) collective-permute-start(bf16[4,200,128]{2,1,0:T(8,128)(2,1)S(1)} %pad_maximum_fusion), channel_id=1, source_target_pairs={{0,1},{1,2},{2,3},{3,4},{4,5},{5,6},{6,7},{7,8},{8,9},{9,10},{10,1... | collective-permute-start | bytes 614408 | tf_op jit(solution)/shard_map/ppermute | solution.py:274
  9.5 0.7 %copy-start.1 = (bf16[16,800]{1,0:T(8,128)(2,1)S(1)}, bf16[16,800]{1,0:T(8,128)(2,1)}, u32[]{:S(2)}) copy-start(bf16[16,800]{1,0:T(8,128)(2,1)} %coup_ref.1) | copy-start | bytes 76804
  10.3 0.7 %copy-start.2 = (f32[8]{0:T(128)S(1)}, f32[8]{0:T(128)}, u32[]{:S(2)}) copy-start(f32[8]{0:T(128)} %occ_ref.1) | copy-start | bytes 100
  10.9 0.7 %copy-start.3 = (s32[8]{0:T(128)S(1)}, s32[8]{0:T(128)}, u32[]{:S(2)}) copy-start(s32[8]{0:T(128)} %off_ref.1) | copy-start | bytes 100
  11.6 4.3 %copy-start = (bf16[8,200,128]{2,1,0:T(8,128)(2,1)S(1)}, bf16[8,200,128]{2,1,0:T(8,128)(2,1)}, u32[]{:S(2)}) copy-start(bf16[8,200,128]{2,1,0:T(8,128)(2,1)} %g_ref.3) | copy-start | bytes 1228804
  19.3 12.8 %collective-permute-start.2 = (bf16[6,200,128]{2,1,0:T(8,128)(2,1)S(1)}, bf16[6,200,128]{2,1,0:T(8,128)(2,1)S(1)}, u32[]{:S(2)}, u32[]{:S(2)}) collective-permute-start(bf16[6,200,128]{2,1,0:T(8,128)(2,1)S(1)} %get-tuple-element.12), channel_id=1, source_target_pairs={{16,32},{48,64},{80,96},{112,128},{144,160},{176,192},{208,224},{2... | collective-permute-start | bytes 921608 | tf_op jit(solution)/shard_map/ppermute | solution.py:269
  25.4 6.6 %collective-permute-start.3 = (bf16[6,200,128]{2,1,0:T(8,128)(2,1)S(1)}, bf16[6,200,128]{2,1,0:T(8,128)(2,1)S(1)}, u32[]{:S(2)}, u32[]{:S(2)}) collective-permute-start(bf16[6,200,128]{2,1,0:T(8,128)(2,1)S(1)} %get-tuple-element.13), channel_id=1, source_target_pairs={{0,16},{32,48},{64,80},{96,112},{128,144},{160,176},{192,208},{224... | collective-permute-start | bytes 921608 | tf_op jit(solution)/shard_map/ppermute | solution.py:269
where the time goes:
time: 36.6 us; the launch traced here: 36.3 us
  Pallas kernels  16.4 us (45%)
  starting transfers between devices  14.6 us (40%)
  local copies, waits for them, and re-layouts  3.47 us (9%)
  other arithmetic  0.94 us (3%)
  between operations  0.76 us (2%)
    ppermute x2, starting transfers between devices, swap(): return lax.ppermute(value, axis, pairs + [(b, a) for a, b in pairs])  8.1 us
    ppermute x2, starting transfers between devices, step_of(): lax.ppermute(value, axis, [(i, i + by) for i in range(count) if 0 <= i +...  6.49 us
    pallas_call x1, Pallas kernels, per_device(): call(local_kernel, shape((atoms, ROWS, 256), F32), [pltpu.VMEM((8, DEPTH,...  4.66 us
    pallas_call x1, Pallas kernels, per_device(): call(final_kernel, shape((atoms, slab, e_dev), BF), [pltpu.VMEM((4, DEPTH...  4.2 us
    pallas_call x1, Pallas kernels, per_device(): call(build_kernel, (tens, tens, shape((2, 256, DEPTH), BF)), [pltpu.VMEM(...  4.14 us
    pallas_call x1, Pallas kernels, per_device(): call(rim_kernel, (payload, payload), [pltpu.VMEM((4, DEPTH, 256), BF), pl...  3.36 us
    unnamed x8, local copies, waits for them, and re-layouts  2.06 us
    slice x1, local copies, waits for them, and re-layouts, per_device(): green[half:, :, :KMAX]  1.41 us
  transfers between devices with their start and end apart: 4, of which 1 were waited for; matrix products, arithmetic and copies ran while one was open for 2% of the time, Pallas kernels for 24%

commit v1 on v0

v1 whole, which is shorter than its diff:
```python
import jax
import jax.numpy as jnp
from jax import lax
from jax.experimental import pallas as pl
from jax.experimental.pallas import tpu as pltpu
from jax.sharding import PartitionSpec as P

NORB = 10
MODES = 8
KMAX = 64
SQ = NORB * NORB
ROWS = 104
PITCH = 112
LANES = 128
DEPTH = MODES * LANES
SLOTS = 16
ATOMS = 8
SLAB = 2 * SQ
LISTS = 48
BF = jnp.bfloat16
F32 = jnp.float32
I32 = jnp.int32
VMEM = pl.BlockSpec(memory_space=pltpu.VMEM)
SMEM = pl.BlockSpec(memory_space=pltpu.SMEM)
HBM = pl.BlockSpec(memory_space=pltpu.HBM)


def iota(shape, dim):
    return lax.broadcasted_iota(I32, shape, dim)


def pack_kernel(
    g_ref, coup_ref, pairs_hbm, occ_hbm, off_hbm, to_a, to_b, g, coup, ints, occ, pairs_ref, off_ref, sems
):
    moves = (
        (g_ref, g),
        (pairs_hbm, pairs_ref),
        (occ_hbm, occ),
        (off_hbm, off_ref),
        (coup_ref, coup),
    )
    copies = [pltpu.make_async_copy(src, dst, sems.at[i]) for i, (src, dst) in enumerate(moves)]
    for copy in copies:
        copy.start()
    for copy in copies[1:4]:
        copy.wait()
    base = lax.axis_index("atom") * ATOMS
    for s in range(SLOTS):
        ints[s] = pairs_ref[0, s] - base
        ints[SLOTS + s] = pairs_ref[1, s] - base
    for m in range(MODES):
        ints[2 * SLOTS + m] = off_ref[m]
    odd = lax.axis_index("energy") % 2
    half = ATOMS // 2
    low = jnp.where(odd == 0, 1, 0)
    pick = (iota((SLAB, LANES), 1) // KMAX) == odd
    copies[0].wait()
    for x in range(half):
        turned = pltpu.roll(g[x + half * odd].astype(F32), KMAX, 1)
        kept = g[x + half * low].astype(F32)
        to_a[x] = jnp.where(pick, turned, kept).astype(BF)
        to_b[x] = jnp.where(pick, kept, turned).astype(BF)
    copies[4].wait()


def build_kernel(cnt_ref, occ_ref, ints_ref, coup_ref, t_ref, s_ref, jobs_ref, cm, v, c12):
    count = cnt_ref[0]

    def listed(s, carry):
        near, far = carry
        first = ints_ref[s]
        second = ints_ref[SLOTS + s]
        local = jnp.where((second >= 0) & (second < ATOMS), 1, 0)
        rim = jnp.where(first >= 4, first - 4, first)
        out = jnp.where(second < 0, second + 2, second - 6)
        jobs_ref[near] = s + 64 * second + 4096 * first
        jobs_ref[near + 1] = s + SLOTS + 64 * first + 4096 * second
        jobs_ref[LISTS + far] = s + SLOTS + 64 * rim + 4096 * out
        jobs_ref[2 * LISTS + far] = s + 64 * out + 4096 * rim
        return near + 2 * local, far + 1 - local

    near, far = lax.fori_loop(0, count, listed, (jnp.int32(0), jnp.int32(0)))
    for j in range(8):
        jobs_ref[near + j] = 4096 * ATOMS
        jobs_ref[LISTS + far + j] = 4096 * 4
        jobs_ref[2 * LISTS + far + j] = 4096 * 4
    jobs_ref[3 * LISTS] = near
    jobs_ref[3 * LISTS + 1] = far

    coup = coup_ref[...].astype(F32)
    width = 7 * LANES
    coup = jnp.concatenate([coup, jnp.zeros((SLOTS, width - MODES * SQ), F32)], axis=1)
    lane = iota((SLOTS, LANES), 1)
    for m in range(MODES):
        part = coup if m == 0 else pltpu.roll(coup, width - m * SQ, 1)
        cm[m * SLOTS : (m + 1) * SLOTS, :] = jnp.where(lane < SQ, part[:, :LANES], 0.0)

    ij = iota((LANES, LANES), 0)
    jk = iota((LANES, LANES), 1)
    valid = (ij < SQ) & (jk < SQ)
    row = iota((16, LANES), 0) % NORB
    col = iota((16, LANES), 1)
    sub = iota((8, LANES), 0)

    def expand(keep, other, at):
        spread = jnp.concatenate(
            [
                jnp.where(valid & (other == jk // NORB), 1.0, 0.0),
                jnp.where(valid & (other == jk % NORB), 1.0, 0.0),
            ],
            axis=1,
        ).astype(BF)
        keep = jnp.where(keep == row, 1.0, 0.0)

        def fill(s, carry):
            for m in range(MODES):
                line = cm[pl.ds(m * SLOTS + s, 1), :]
                v[pl.ds(pl.multiple_of(s * (16 * MODES) + m * 16, 16), 16), :] = (
                    jnp.broadcast_to(line, (16, LANES)) * keep
                ).astype(BF)
            return carry

        lax.fori_loop(0, count, fill, 0)
        for part in range(SLOTS // 2):
            lo = part * 32 * MODES
            c12[lo : lo + 32 * MODES, :] = jnp.dot(
                v[lo : lo + 32 * MODES, :], spread, preferred_element_type=F32
            )

        def product(s, carry):
            for m in range(MODES):
                base = pl.multiple_of(s * (16 * MODES) + m * 16, 16)
                first = c12[pl.ds(base, 16), :LANES]
                second = c12[pl.ds(base, 16), LANES:]
                turns = [
                    second[0:8],
                    second[8:16],
                    pltpu.roll(second, 10, 0)[0:8],
                    pltpu.roll(second, 12, 0)[0:8],
                    pltpu.roll(second, 14, 0)[0:8],
                ]
                spreads = [jnp.broadcast_to(first[i : i + 1], (8, LANES)) for i in range(NORB)]
                rows = []
                for g in range(ROWS // 8):
                    lo = 8 * g // NORB
                    hi = min((8 * g + 7) // NORB, NORB - 1)
                    left = spreads[lo]
                    if hi != lo:
                        left = jnp.where(sub < NORB * hi - 8 * g, left, spreads[hi])
                    rows.append(left * turns[g % 5])
                t_ref[at + s, :, m * LANES : (m + 1) * LANES] = jnp.concatenate(rows, axis=0).astype(BF)
            return carry

        lax.fori_loop(0, count, product, 0)

    expand(col // NORB, ij % NORB, 0)
    expand(col % NORB, ij // NORB, SLOTS)

    odd = lax.axis_index("energy") % 2
    e_in = iota((2 * LANES, LANES), 0)
    e_out = iota((2 * LANES, LANES), 1)
    left_first = jnp.where(e_in < 128, e_in, jnp.where(e_in < 192, e_in - 192, e_in - 64))
    right_first = jnp.where(e_in < 128, e_in, jnp.where(e_in < 192, e_in, e_in - 256))
    orders = (jnp.where(odd == 1, left_first, right_first), jnp.where(odd == 1, right_first, left_first))
    for m in range(MODES):
        occ = occ_ref[m]
        step = ints_ref[2 * SLOTS + m]
        for which in range(2):
            away = orders[which] - e_out
            s_ref[which, :, m * LANES : (m + 1) * LANES] = jnp.where(
                away == -step, occ, jnp.where(away == step, occ + 1.0, 0.0)
            ).astype(BF)


def shift_atom(center, halo, s_ref, which, lhs, low, store):
    lhs[0:ROWS, :LANES] = center[0:ROWS]
    lhs[0:ROWS, LANES:] = halo[0:ROWS]
    low[0:ROWS, :LANES] = center[96:SLAB].astype(F32)
    low[0:ROWS, LANES:] = halo[96:SLAB].astype(F32)
    lhs[PITCH : PITCH + ROWS, :] = low[4 : 4 + ROWS, :].astype(BF)
    for t in range(MODES // 2):
        out = jnp.dot(lhs[...], s_ref[which, :, t * 256 : (t + 1) * 256], preferred_element_type=F32)
        for mm in range(2):
            for r in range(2):
                store(
                    2 * t + mm,
                    r,
                    out[r * PITCH : r * PITCH + ROWS, mm * LANES : (mm + 1) * LANES].astype(BF),
                )


def halo_of(from_a, from_b, x):
    left = iota((SLAB, LANES), 1) < KMAX
    a = from_a[x % 4]
    b = from_b[x % 4]
    return jnp.where(left, a, b) if x < 4 else jnp.where(left, b, a)


def prepare(x_ref, lhs, low, count):
    low[:, ROWS:, :] = jnp.zeros((low.shape[0], 8, 256), F32)
    lhs[:, 96:PITCH, :] = jnp.zeros((lhs.shape[0], 16, 256), BF)
    lhs[:, PITCH + 96 :, :] = jnp.zeros((lhs.shape[0], 16, 256), BF)
    for x in range(count):
        for m in range(MODES):
            x_ref[x, m * LANES + 96 : (m + 1) * LANES, :] = jnp.zeros((32, 256), BF)


def store_in(x_ref, at):
    def store(m, r, value):
        x_ref[at, m * LANES : m * LANES + ROWS, r * LANES : (r + 1) * LANES] = value

    return store


def unfold(total, rows):
    rows[0:ROWS, :] = total[:, :LANES]
    rows[SQ : SQ + ROWS, :] = total[:, LANES:]
    return rows[0:SLAB, :]


def run_jobs(jobs_ref, at, count, chunk, t_ref, x_ref, acc):
    def step(i, carry):
        for j in range(chunk):
            job = jobs_ref[at + i * chunk + j]
            t, src, dst = job & 63, (job >> 6) & 63, job >> 12
            acc[dst] = acc[dst] + jnp.dot(t_ref[t], x_ref[src], preferred_element_type=F32)
        return carry

    lax.fori_loop(0, (count + chunk - 1) // chunk, step, 0)


def rim_kernel(jobs_ref, g_ref, from_a, from_b, s_ref, t_ref, cross_ref, near_ref, x, part, lhs, low, rows):
    prepare(x, lhs, low, 4)
    halos = []
    for at, atom in enumerate((0, 1, 6, 7)):
        halo = halo_of(from_a, from_b, atom)
        halos.append(halo)
        shift_atom(g_ref[atom], halo, s_ref, atom // 4, lhs.at[at], low.at[at], store_in(x, at))
    part[...] = jnp.zeros(part.shape, F32)
    run_jobs(jobs_ref, LISTS, jobs_ref[3 * LISTS + 1], 4, t_ref, x, part)
    odd = lax.axis_index("atom") % 2

    def fill(ref, side):
        for j in range(2):
            ref[j] = g_ref[6 * side + j]
            ref[2 + j] = halos[2 * side + j]
            ref[4 + j] = unfold(part[2 * side + j], rows).astype(BF)

    @pl.when(odd == 1)
    def _():
        fill(cross_ref, 1)
        fill(near_ref, 0)

    @pl.when(odd == 0)
    def _():
        fill(cross_ref, 0)
        fill(near_ref, 1)


def local_kernel(jobs_ref, g_ref, from_a, from_b, s_ref, t_ref, inner_ref, rim_ref, x, acc, lhs, low, rows):
    prepare(x, lhs, low, ATOMS)
    for atom in range(ATOMS):
        halo = halo_of(from_a, from_b, atom)
        shift_atom(g_ref[atom], halo, s_ref, atom // 4, lhs.at[atom], low.at[atom], store_in(x, atom))
    acc[...] = jnp.zeros(acc.shape, F32)
    run_jobs(jobs_ref, 0, jobs_ref[3 * LISTS], 8, t_ref, x, acc)
    for j in range(4):
        inner_ref[j] = unfold(acc[2 + j], rows).astype(BF)
        rim_ref[j] = acc[j if j < 2 else j + 4]


def final_kernel(
    jobs_ref, cross_ref, near_ref, s_ref, t_ref, inner_ref, rim_ref, out_ref, x, acc, done, lhs, low, rows, sems
):
    early = pltpu.make_async_copy(inner_ref, out_ref.at[2:6], sems.at[0])
    early.start()
    prepare(x, lhs, low, 4)
    odd = lax.axis_index("atom") % 2

    def take(ref, side):
        for j in range(2):
            at = 2 * side + j
            shift_atom(ref[j], ref[2 + j], s_ref, 1 - side, lhs.at[at], low.at[at], store_in(x, at))

    @pl.when(odd == 1)
    def _():
        take(cross_ref, 1)
        take(near_ref, 0)

    @pl.when(odd == 0)
    def _():
        take(cross_ref, 0)
        take(near_ref, 1)

    acc[0:4] = rim_ref[...]
    run_jobs(jobs_ref, 2 * LISTS, jobs_ref[3 * LISTS + 1], 4, t_ref, x, acc)
    for j in range(4):
        side = j // 2
        got = jnp.where(
            odd == side, cross_ref[4 + j % 2].astype(F32), near_ref[4 + j % 2].astype(F32)
        )
        done[j] = (unfold(acc[j], rows) + got).astype(BF)
    lower = pltpu.make_async_copy(done.at[0:2], out_ref.at[0:2], sems.at[1])
    upper = pltpu.make_async_copy(done.at[2:4], out_ref.at[6:8], sems.at[2])
    lower.start()
    upper.start()
    early.wait()
    lower.wait()
    upper.wait()


def swap(value, axis, start):
    count = lax.axis_size(axis)
    pairs = [(i, i + 1) for i in range(start, count - 1, 2)]
    return lax.ppermute(value, axis, pairs + [(b, a) for a, b in pairs])


def call(kernel, outs, scratch, flops, moved, specs, out_specs, grant=40):
    return pl.pallas_call(
        kernel,
        out_shape=outs,
        in_specs=specs,
        out_specs=out_specs,
        scratch_shapes=scratch,
        compiler_params=pltpu.CompilerParams(vmem_limit_bytes=grant * 1024 * 1024),
        cost_estimate=pl.CostEstimate(flops=flops, bytes_accessed=moved, transcendentals=0),
    )


def per_device(green, coupling, pairs, counts, occupation, offsets):
    atoms, slab, e_dev = green.shape
    shape = jax.ShapeDtypeStruct
    dma = pltpu.SemaphoreType.DMA

    half = shape((atoms // 2, slab, e_dev), BF)
    to_a, to_b, g, coup, ints, occ = call(
        pack_kernel,
        (half, half, shape(green.shape, BF), shape(coupling.shape, BF), shape((2 * SLOTS + MODES,), I32), shape((MODES,), F32)),
        [
            pltpu.SMEM((2, SLOTS), I32),
            pltpu.SMEM((MODES,), I32),
            dma((5,)),
        ],
        int(1e6),
        int(1e6),
        [HBM] * 5,
        (VMEM, VMEM, VMEM, VMEM, SMEM, SMEM),
    )(*[pltpu.with_memory_space_constraint(v, pltpu.HBM) for v in (green, coupling, pairs.T, occupation, offsets)])
    from_b = swap(to_b, "energy", 1)
    from_a = swap(to_a, "energy", 0)

    t, s, jobs = call(
        build_kernel,
        (shape((2 * SLOTS, ROWS, DEPTH), BF), shape((2, 256, DEPTH), BF), shape((3 * LISTS + 8,), I32)),
        [
            pltpu.VMEM((MODES * SLOTS, LANES), F32),
            pltpu.VMEM((MODES * SLOTS * 16, LANES), BF),
            pltpu.VMEM((MODES * SLOTS * 16, 256), F32),
        ],
        int(3e9),
        int(8e6),
        [SMEM, SMEM, SMEM, VMEM],
        (VMEM, VMEM, SMEM),
    )(counts, occ, ints, coup)

    def scratch(count, sums):
        return [
            pltpu.VMEM((count, DEPTH, 256), BF),
            pltpu.VMEM((sums, ROWS, 256), F32),
        ], [
            pltpu.VMEM((count, 2 * PITCH, 256), BF),
            pltpu.VMEM((count, PITCH, 256), F32),
            pltpu.VMEM((208, LANES), F32),
        ]

    payload = shape((6, slab, e_dev), BF)
    main, spare = scratch(4, 5)
    cross, near = call(
        rim_kernel, (payload, payload), main + spare, int(1e9), int(1e6), [SMEM] + [VMEM] * 5, (VMEM, VMEM)
    )(jobs, g, from_a, from_b, s, t)
    cross = swap(cross, "atom", 1)
    near = swap(near, "atom", 0)

    main, spare = scratch(8, 9)
    inner, rim = call(
        local_kernel,
        (shape((4, slab, e_dev), BF), shape((4, ROWS, 256), F32)),
        main + spare,
        int(3e9),
        int(1e6),
        [SMEM] + [VMEM] * 5,
        (VMEM, VMEM),
    )(jobs, g, from_a, from_b, s, t)

    main, spare = scratch(4, 5)
    return call(
        final_kernel,
        shape((atoms, slab, e_dev), BF),
        main + [pltpu.VMEM((4, slab, e_dev), BF)] + spare + [dma((3,))],
        int(1e9),
        int(1e6),
        [SMEM] + [VMEM] * 6,
        HBM,
    )(jobs, cross, near, s, t, inner, rim)


def solution(mesh):
    placed = (P("atom", None, "energy"), P("atom", None), P("atom", None), P("atom"), P(), P())
    return jax.shard_map(
        per_device, mesh=mesh, in_specs=placed, out_specs=P("atom", None, "energy"), check_vma=False
    )
```

time: 36.6 us -> 32.7 us (0.89)
  the two profiles are of different devices: /device:TPU:249 before, /device:TPU:240 now
where the time goes in v1:
time: 32.7 us; the launch traced here: 32.5 us
  Pallas kernels  16.1 us (49%)
  starting transfers between devices  14.3 us (44%)
  waiting for transfers between devices  1.4 us (4%)
  between operations  0.73 us (2%)
    ppermute x4, starting transfers between devices, swap(): return lax.ppermute(value, axis, pairs + [(b, a) for a, b in pairs])  14.3 us
    pallas_call x1, Pallas kernels, per_device(): call(build_kernel, (shape((2 * SLOTS, ROWS, DEPTH), BF), shape((2, 256, D...  4.59 us
    pallas_call x1, Pallas kernels, per_device(): call(local_kernel, (shape((4, slab, e_dev), BF), shape((4, ROWS, 256), F3...  4.32 us
    pallas_call x1, Pallas kernels, per_device(): call(final_kernel, shape((atoms, slab, e_dev), BF), main + [pltpu.VMEM((4...  3.02 us
    pallas_call x1, Pallas kernels, per_device(): call(rim_kernel, (payload, payload), main + spare, int(1000000000.0), int...  2.33 us
    pallas_call x1, Pallas kernels, per_device(): call(pack_kernel, (half, half, shape(green.shape, BF), shape(coupling.sha...  1.8 us
    ppermute x4, waiting for transfers between devices, swap(): return lax.ppermute(value, axis, pairs + [(b, a) for a, b in pairs])  1.4 us
  transfers between devices with their start and end apart: 4, of which 1 were waited for; matrix products, arithmetic and copies ran while one was open for 0% of the time, Pallas kernels for 27%

profile of v1, /device:TPU:240, one launch (start us, length us, event | category | flops | bytes accessed | tf_op | source)
XLA Modules:
  0.0 32.5 jit_solution(8570700684600722903)
XLA Ops:
  0.0 1.8 %shard_map.64 = (bf16[4,200,128]{2,1,0:T(8,128)(2,1)S(1)}, bf16[4,200,128]{2,1,0:T(8,128)(2,1)S(1)}, bf16[8,200,128]{2,1,0:T(8,128)(2,1)S(1)}, bf16[16,800]{1,0:...) custom-call(bf16[8,200,128]{2,1,0:T(8,128)(2,1)} %g_ref.1, bf16[16,800]{1,0:T(8,128)(2,1)} %coup_ref.1, s32[2,16]{1,0:T(2,128)} %bitcast.1, ...), custom_call_target="tpu_custom_call" | custom-call | flops 1000000 | bytes 1000000 | tf_op jit(solution)/shard_map/pallas_call | solution.py:336
  1.8 3.4 %collective-permute-start = (bf16[4,200,128]{2,1,0:T(8,128)(2,1)S(1)}, bf16[4,200,128]{2,1,0:T(8,128)(2,1)S(1)}, u32[]{:S(2)}, u32[]{:S(2)}) collective-permute-start(bf16[4,200,128]{2,1,0:T(8,128)(2,1)S(1)} %get-tuple-element.23), channel_id=1, source_target_pairs={{0,1},{2,3},{4,5},{6,7},{8,9},{10,11},{12,13},{14,15},{1,0},{3,2},... | collective-permute-start | bytes 614408 | tf_op jit(solution)/shard_map/ppermute | solution.py:315
  5.2 3.9 %collective-permute-start.1 = (bf16[4,200,128]{2,1,0:T(8,128)(2,1)S(1)}, bf16[4,200,128]{2,1,0:T(8,128)(2,1)S(1)}, u32[]{:S(2)}, u32[]{:S(2)}) collective-permute-start(bf16[4,200,128]{2,1,0:T(8,128)(2,1)S(1)} %get-tuple-element.24), channel_id=1, source_target_pairs={{1,2},{3,4},{5,6},{7,8},{9,10},{11,12},{13,14},{2,1},{4,3},{6,5},{... | collective-permute-start | bytes 614408 | tf_op jit(solution)/shard_map/ppermute | solution.py:315
  9.8 4.6 %shard_map.65 = (bf16[32,104,1024]{2,1,0:T(8,128)(2,1)S(1)}, bf16[2,256,1024]{2,1,0:T(8,128)(2,1)S(1)}, s32[152]{0:T(256)S(1)}) custom-call(s32[1]{0:T(128)S(6)} %copy.7.cnt_ref, f32[8]{0:T(128)S(1)} %get-tuple-element.18.occ_ref, s32[40]{0:T(128)S(1)} %get-tuple-element.19.ints_ref, bf16[16,800]{1,0:T(8,128)(2,1)S(1)} %get-tuple-element.20.coup_ref), custom_call_target="tpu_custom_call" | custom-call | flops 3000000000 | bytes 8000000 | tf_op jit(solution)/shard_map/pallas_call | solution.py:352
  14.4 0.0 collective-permute-done.from_a
  14.4 1.4 %collective-permute-done.1.from_b = bf16[4,200,128]{2,1,0:T(8,128)(2,1)S(1)} collective-permute-done((bf16[4,200,128]{2,1,0:T(8,128)(2,1)S(1)}, bf16[4,200,128]{2,1,0:T(8,128)(2,1)S(1)}, u32[]{:S(2)}, u32[]{:S(2)}) %collective-permute-start.1) | collective-permute-done | bytes 204832 | tf_op jit(solution)/shard_map/ppermute | solution.py:315
  15.8 2.3 %shard_map.66 = (bf16[6,200,128]{2,1,0:T(8,128)(2,1)S(1)}, bf16[6,200,128]{2,1,0:T(8,128)(2,1)S(1)}) custom-call(s32[152]{0:T(256)S(1)} %get-tuple-element.21.jobs_ref, bf16[8,200,128]{2,1,0:T(8,128)(2,1)S(1)} %get-tuple-element.22.g_ref, bf16[4,200,128]{2,1,0:T(8,128)(2,1)S(1)} %collective-permute-done.from_a, ...), custom_call_target="tpu_custom_call" | custom-call | flops 1000000000 | bytes 1000000 | tf_op jit(solution)/shard_map/pallas_call | solution.py:378
  18.1 1.9 %collective-permute-start.2 = (bf16[6,200,128]{2,1,0:T(8,128)(2,1)S(1)}, bf16[6,200,128]{2,1,0:T(8,128)(2,1)S(1)}, u32[]{:S(2)}, u32[]{:S(2)}) collective-permute-start(bf16[6,200,128]{2,1,0:T(8,128)(2,1)S(1)} %get-tuple-element.27), channel_id=1, source_target_pairs={{16,32},{48,64},{80,96},{112,128},{144,160},{176,192},{208,224},{2... | collective-permute-start | bytes 921608 | tf_op jit(solution)/shard_map/ppermute | solution.py:315
  20.0 5.1 %collective-permute-start.3 = (bf16[6,200,128]{2,1,0:T(8,128)(2,1)S(1)}, bf16[6,200,128]{2,1,0:T(8,128)(2,1)S(1)}, u32[]{:S(2)}, u32[]{:S(2)}) collective-permute-start(bf16[6,200,128]{2,1,0:T(8,128)(2,1)S(1)} %get-tuple-element.28), channel_id=1, source_target_pairs={{0,16},{32,48},{64,80},{96,112},{128,144},{160,176},{192,208},{224... | collective-permute-start | bytes 921608 | tf_op jit(solution)/shard_map/ppermute | solution.py:315
  25.2 4.3 %shard_map.67 = (bf16[4,200,128]{2,1,0:T(8,128)(2,1)S(1)}, f32[4,104,256]{2,1,0:T(8,128)S(1)}) custom-call(s32[152]{0:T(256)S(1)} %get-tuple-element.21.jobs_ref, bf16[8,200,128]{2,1,0:T(8,128)(2,1)S(1)} %get-tuple-element.22.g_ref, bf16[4,200,128]{2,1,0:T(8,128)(2,1)S(1)} %collective-permute-done.from_a, ...), custom_call_target="tpu_custom_call" | custom-call | flops 3000000000 | bytes 1000000 | tf_op jit(solution)/shard_map/pallas_call | solution.py:385
  29.5 0.0 collective-permute-done.2.cross_ref
  29.5 0.0 collective-permute-done.3.near_ref
  29.5 3.0 %shard_map.68 = bf16[8,200,128]{2,1,0:T(8,128)(2,1)} custom-call(s32[152]{0:T(256)S(1)} %get-tuple-element.21.jobs_ref, bf16[6,200,128]{2,1,0:T(8,128)(2,1)S(1)} %collective-permute-done.2.cross_ref, bf16[6,200,128]{2,1,0:T(8,128)(2,1)S(1)} %collective-permute-done.3.near_ref, bf16[2,256,1024]{2,1,0:T(8,128)(2,1)S(1)} %get-tuple-element.25.s_ref, ...), custom_call_target="tpu_custom_call" | custom-call | flops 1000000000 | bytes 1000000 | tf_op jit(solution)/shard_map/pallas_call | solution.py:396
Async XLA Ops:
  1.8 12.5 %collective-permute-start = (bf16[4,200,128]{2,1,0:T(8,128)(2,1)S(1)}, bf16[4,200,128]{2,1,0:T(8,128)(2,1)S(1)}, u32[]{:S(2)}, u32[]{:S(2)}) collective-permute-start(bf16[4,200,128]{2,1,0:T(8,128)(2,1)S(1)} %get-tuple-element.23), channel_id=1, source_target_pairs={{0,1},{2,3},{4,5},{6,7},{8,9},{10,11},{12,13},{14,15},{1,0},{3,2},... | collective-permute-start | bytes 614408 | tf_op jit(solution)/shard_map/ppermute | solution.py:315
  5.2 10.5 %collective-permute-start.1 = (bf16[4,200,128]{2,1,0:T(8,128)(2,1)S(1)}, bf16[4,200,128]{2,1,0:T(8,128)(2,1)S(1)}, u32[]{:S(2)}, u32[]{:S(2)}) collective-permute-start(bf16[4,200,128]{2,1,0:T(8,128)(2,1)S(1)} %get-tuple-element.24), channel_id=1, source_target_pairs={{1,2},{3,4},{5,6},{7,8},{9,10},{11,12},{13,14},{2,1},{4,3},{6,5},{... | collective-permute-start | bytes 614408 | tf_op jit(solution)/shard_map/ppermute | solution.py:315
  18.1 11.4 %collective-permute-start.2 = (bf16[6,200,128]{2,1,0:T(8,128)(2,1)S(1)}, bf16[6,200,128]{2,1,0:T(8,128)(2,1)S(1)}, u32[]{:S(2)}, u32[]{:S(2)}) collective-permute-start(bf16[6,200,128]{2,1,0:T(8,128)(2,1)S(1)} %get-tuple-element.27), channel_id=1, source_target_pairs={{16,32},{48,64},{80,96},{112,128},{144,160},{176,192},{208,224},{2... | collective-permute-start | bytes 921608 | tf_op jit(solution)/shard_map/ppermute | solution.py:315
  20.0 9.5 %collective-permute-start.3 = (bf16[6,200,128]{2,1,0:T(8,128)(2,1)S(1)}, bf16[6,200,128]{2,1,0:T(8,128)(2,1)S(1)}, u32[]{:S(2)}, u32[]{:S(2)}) collective-permute-start(bf16[6,200,128]{2,1,0:T(8,128)(2,1)S(1)} %get-tuple-element.28), channel_id=1, source_target_pairs={{0,16},{32,48},{64,80},{96,112},{128,144},{160,176},{192,208},{224... | collective-permute-start | bytes 921608 | tf_op jit(solution)/shard_map/ppermute | solution.py:315

commit v2 on v1

--- a/solution.py
+++ b/solution.py
@@ -29,53 +29,41 @@
     return lax.broadcasted_iota(I32, shape, dim)
 
 
-def pack_kernel(
-    g_ref, coup_ref, pairs_hbm, occ_hbm, off_hbm, to_a, to_b, g, coup, ints, occ, pairs_ref, off_ref, sems
-):
-    moves = (
-        (g_ref, g),
-        (pairs_hbm, pairs_ref),
-        (occ_hbm, occ),
-        (off_hbm, off_ref),
-        (coup_ref, coup),
-    )
+def pack_kernel(g_hbm, coup_hbm, pairs_hbm, occ_hbm, off_hbm, to_a, to_b, g, coup, pairs, occ, off, sems):
+    half = ATOMS // 2
+    moves = ((g_hbm, g), (coup_hbm, coup), (pairs_hbm, pairs), (occ_hbm, occ), (off_hbm, off))
     copies = [pltpu.make_async_copy(src, dst, sems.at[i]) for i, (src, dst) in enumerate(moves)]
     for copy in copies:
         copy.start()
-    for copy in copies[1:4]:
-        copy.wait()
-    base = lax.axis_index("atom") * ATOMS
-    for s in range(SLOTS):
-        ints[s] = pairs_ref[0, s] - base
-        ints[SLOTS + s] = pairs_ref[1, s] - base
-    for m in range(MODES):
-        ints[2 * SLOTS + m] = off_ref[m]
     odd = lax.axis_index("energy") % 2
-    half = ATOMS // 2
-    low = jnp.where(odd == 0, 1, 0)
     pick = (iota((SLAB, LANES), 1) // KMAX) == odd
     copies[0].wait()
     for x in range(half):
-        turned = pltpu.roll(g[x + half * odd].astype(F32), KMAX, 1)
-        kept = g[x + half * low].astype(F32)
-        to_a[x] = jnp.where(pick, turned, kept).astype(BF)
-        to_b[x] = jnp.where(pick, kept, turned).astype(BF)
-    copies[4].wait()
-
-
-def build_kernel(cnt_ref, occ_ref, ints_ref, coup_ref, t_ref, s_ref, jobs_ref, cm, v, c12):
+        turned = pltpu.roll(g[x + half * odd].astype(F32), KMAX, 1).astype(BF)
+        kept = g[x + half - half * odd]
+        to_a[x] = jnp.where(pick, turned, kept)
+        to_b[x] = jnp.where(pick, kept, turned)
+    for copy in copies[1:]:
+        copy.wait()
+
+
+def build_kernel(cnt_ref, pairs_ref, occ_ref, off_ref, coup_ref, t_ref, s_ref, jobs_ref, x_ref, cm, v, c12):
     count = cnt_ref[0]
+    base = lax.axis_index("atom") * ATOMS
+    for x in range(ATOMS):
+        for m in range(MODES):
+            x_ref[x, m * LANES + 96 : (m + 1) * LANES, :] = jnp.zeros((32, 256), BF)
 
     def listed(s, carry):
         near, far = carry
-        first = ints_ref[s]
-        second = ints_ref[SLOTS + s]
+        first = pairs_ref[0, s] - base
+        second = pairs_ref[1, s] - base
         local = jnp.where((second >= 0) & (second < ATOMS), 1, 0)
         rim = jnp.where(first >= 4, first - 4, first)
         out = jnp.where(second < 0, second + 2, second - 6)
         jobs_ref[near] = s + 64 * second + 4096 * first
         jobs_ref[near + 1] = s + SLOTS + 64 * first + 4096 * second
-        jobs_ref[LISTS + far] = s + SLOTS + 64 * rim + 4096 * out
+        jobs_ref[LISTS + far] = s + SLOTS + 64 * first + 4096 * out
         jobs_ref[2 * LISTS + far] = s + 64 * out + 4096 * rim
         return near + 2 * local, far + 1 - local
 
@@ -164,7 +152,7 @@
     orders = (jnp.where(odd == 1, left_first, right_first), jnp.where(odd == 1, right_first, left_first))
     for m in range(MODES):
         occ = occ_ref[m]
-        step = ints_ref[2 * SLOTS + m]
+        step = off_ref[m]
         for which in range(2):
             away = orders[which] - e_out
             s_ref[which, :, m * LANES : (m + 1) * LANES] = jnp.where(
@@ -177,6 +165,7 @@
     lhs[0:ROWS, LANES:] = halo[0:ROWS]
     low[0:ROWS, :LANES] = center[96:SLAB].astype(F32)
     low[0:ROWS, LANES:] = halo[96:SLAB].astype(F32)
+    low[ROWS:, :] = jnp.zeros((PITCH - ROWS, 256), F32)
     lhs[PITCH : PITCH + ROWS, :] = low[4 : 4 + ROWS, :].astype(BF)
     for t in range(MODES // 2):
         out = jnp.dot(lhs[...], s_ref[which, :, t * 256 : (t + 1) * 256], preferred_element_type=F32)
@@ -196,15 +185,6 @@
     return jnp.where(left, a, b) if x < 4 else jnp.where(left, b, a)
 
 
-def prepare(x_ref, lhs, low, count):
-    low[:, ROWS:, :] = jnp.zeros((low.shape[0], 8, 256), F32)
-    lhs[:, 96:PITCH, :] = jnp.zeros((lhs.shape[0], 16, 256), BF)
-    lhs[:, PITCH + 96 :, :] = jnp.zeros((lhs.shape[0], 16, 256), BF)
-    for x in range(count):
-        for m in range(MODES):
-            x_ref[x, m * LANES + 96 : (m + 1) * LANES, :] = jnp.zeros((32, 256), BF)
-
-
 def store_in(x_ref, at):
     def store(m, r, value):
         x_ref[at, m * LANES : m * LANES + ROWS, r * LANES : (r + 1) * LANES] = value
@@ -229,13 +209,14 @@
     lax.fori_loop(0, (count + chunk - 1) // chunk, step, 0)
 
 
-def rim_kernel(jobs_ref, g_ref, from_a, from_b, s_ref, t_ref, cross_ref, near_ref, x, part, lhs, low, rows):
-    prepare(x, lhs, low, 4)
+def rim_kernel(
+    jobs_ref, g_ref, from_b, from_a, s_ref, t_ref, x_old, cross_ref, near_ref, x, part, lhs, low, rows
+):
     halos = []
     for at, atom in enumerate((0, 1, 6, 7)):
         halo = halo_of(from_a, from_b, atom)
         halos.append(halo)
-        shift_atom(g_ref[atom], halo, s_ref, atom // 4, lhs.at[at], low.at[at], store_in(x, at))
+        shift_atom(g_ref[atom], halo, s_ref, atom // 4, lhs.at[at], low.at[at], store_in(x, atom))
     part[...] = jnp.zeros(part.shape, F32)
     run_jobs(jobs_ref, LISTS, jobs_ref[3 * LISTS + 1], 4, t_ref, x, part)
     odd = lax.axis_index("atom") % 2
@@ -257,11 +238,12 @@
         fill(near_ref, 1)
 
 
-def local_kernel(jobs_ref, g_ref, from_a, from_b, s_ref, t_ref, inner_ref, rim_ref, x, acc, lhs, low, rows):
-    prepare(x, lhs, low, ATOMS)
-    for atom in range(ATOMS):
+def local_kernel(
+    jobs_ref, g_ref, from_b, from_a, s_ref, t_ref, x_old, inner_ref, rim_ref, x, acc, lhs, low, rows
+):
+    for at, atom in enumerate((2, 3, 4, 5)):
         halo = halo_of(from_a, from_b, atom)
-        shift_atom(g_ref[atom], halo, s_ref, atom // 4, lhs.at[atom], low.at[atom], store_in(x, atom))
+        shift_atom(g_ref[atom], halo, s_ref, atom // 4, lhs.at[at], low.at[at], store_in(x, atom))
     acc[...] = jnp.zeros(acc.shape, F32)
     run_jobs(jobs_ref, 0, jobs_ref[3 * LISTS], 8, t_ref, x, acc)
     for j in range(4):
@@ -270,11 +252,10 @@
 
 
 def final_kernel(
-    jobs_ref, cross_ref, near_ref, s_ref, t_ref, inner_ref, rim_ref, out_ref, x, acc, done, lhs, low, rows, sems
+    jobs_ref, cross_ref, near_ref, s_ref, t_ref, inner_ref, rim_ref, x_old, out_ref, x, acc, done, lhs, low, rows, sems
 ):
     early = pltpu.make_async_copy(inner_ref, out_ref.at[2:6], sems.at[0])
     early.start()
-    prepare(x, lhs, low, 4)
     odd = lax.axis_index("atom") % 2
 
     def take(ref, side):
@@ -315,14 +296,15 @@
     return lax.ppermute(value, axis, pairs + [(b, a) for a, b in pairs])
 
 
-def call(kernel, outs, scratch, flops, moved, specs, out_specs, grant=40):
+def call(kernel, outs, scratch, flops, moved, specs, out_specs, aliases={}):
     return pl.pallas_call(
         kernel,
         out_shape=outs,
         in_specs=specs,
         out_specs=out_specs,
         scratch_shapes=scratch,
-        compiler_params=pltpu.CompilerParams(vmem_limit_bytes=grant * 1024 * 1024),
+        input_output_aliases=aliases,
+        compiler_params=pltpu.CompilerParams(vmem_limit_bytes=32 * 1024 * 1024),
         cost_estimate=pl.CostEstimate(flops=flops, bytes_accessed=moved, transcendentals=0),
     )
 
@@ -331,27 +313,26 @@
     atoms, slab, e_dev = green.shape
     shape = jax.ShapeDtypeStruct
     dma = pltpu.SemaphoreType.DMA
+    pairs = pairs.T
 
     half = shape((atoms // 2, slab, e_dev), BF)
-    to_a, to_b, g, coup, ints, occ = call(
+    taken = (green, coupling, pairs, occupation, offsets)
+    to_a, to_b, g, coup, pairs, occ, off = call(
         pack_kernel,
-        (half, half, shape(green.shape, BF), shape(coupling.shape, BF), shape((2 * SLOTS + MODES,), I32), shape((MODES,), F32)),
-        [
-            pltpu.SMEM((2, SLOTS), I32),
-            pltpu.SMEM((MODES,), I32),
-            dma((5,)),
-        ],
+        (half, half) + tuple(shape(v.shape, v.dtype) for v in taken),
+        [dma((5,))],
         int(1e6),
         int(1e6),
         [HBM] * 5,
-        (VMEM, VMEM, VMEM, VMEM, SMEM, SMEM),
-    )(*[pltpu.with_memory_space_constraint(v, pltpu.HBM) for v in (green, coupling, pairs.T, occupation, offsets)])
+        (VMEM,) * 7,
+    )(*[pltpu.with_memory_space_constraint(v, pltpu.HBM) for v in taken])
     from_b = swap(to_b, "energy", 1)
     from_a = swap(to_a, "energy", 0)
 
-    t, s, jobs = call(
+    shifted = shape((ATOMS, DEPTH, 256), BF)
+    t, s, jobs, x = call(
         build_kernel,
-        (shape((2 * SLOTS, ROWS, DEPTH), BF), shape((2, 256, DEPTH), BF), shape((3 * LISTS + 8,), I32)),
+        (shape((2 * SLOTS, ROWS, DEPTH), BF), shape((2, 256, DEPTH), BF), shape((3 * LISTS + 8,), I32), shifted),
         [
             pltpu.VMEM((MODES * SLOTS, LANES), F32),
             pltpu.VMEM((MODES * SLOTS * 16, LANES), BF),
@@ -359,49 +340,50 @@
         ],
         int(3e9),
         int(8e6),
-        [SMEM, SMEM, SMEM, VMEM],
-        (VMEM, VMEM, SMEM),
-    )(counts, occ, ints, coup)
-
-    def scratch(count, sums):
-        return [
-            pltpu.VMEM((count, DEPTH, 256), BF),
-            pltpu.VMEM((sums, ROWS, 256), F32),
-        ], [
-            pltpu.VMEM((count, 2 * PITCH, 256), BF),
-            pltpu.VMEM((count, PITCH, 256), F32),
-            pltpu.VMEM((208, LANES), F32),
-        ]
-
+        [SMEM] * 4 + [VMEM],
+        (VMEM, VMEM, SMEM, VMEM),
+    )(counts, pairs, occ, off, coup)
+
+    spare = [
+        pltpu.VMEM((4, 2 * PITCH, 256), BF),
+        pltpu.VMEM((4, PITCH, 256), F32),
+        pltpu.VMEM((208, LANES), F32),
+    ]
     payload = shape((6, slab, e_dev), BF)
-    main, spare = scratch(4, 5)
-    cross, near = call(
-        rim_kernel, (payload, payload), main + spare, int(1e9), int(1e6), [SMEM] + [VMEM] * 5, (VMEM, VMEM)
-    )(jobs, g, from_a, from_b, s, t)
+    cross, near, x = call(
+        rim_kernel,
+        (payload, payload, shifted),
+        [pltpu.VMEM((5, ROWS, 256), F32)] + spare,
+        int(1e9),
+        int(1e6),
+        [SMEM] + [VMEM] * 6,
+        (VMEM, VMEM, VMEM),
+        {6: 2},
+    )(jobs, g, from_b, from_a, s, t, x)
     cross = swap(cross, "atom", 1)
     near = swap(near, "atom", 0)
 
-    main, spare = scratch(8, 9)
-    inner, rim = call(
+    inner, rim, x = call(
         local_kernel,
-        (shape((4, slab, e_dev), BF), shape((4, ROWS, 256), F32)),
-        main + spare,
+        (shape((4, slab, e_dev), BF), shape((4, ROWS, 256), F32), shifted),
+        [pltpu.VMEM((9, ROWS, 256), F32)] + spare,
         int(3e9),
         int(1e6),
-        [SMEM] + [VMEM] * 5,
-        (VMEM, VMEM),
-    )(jobs, g, from_a, from_b, s, t)
-
-    main, spare = scratch(4, 5)
+        [SMEM] + [VMEM] * 6,
+        (VMEM, VMEM, VMEM),
+        {6: 2},
+    )(jobs, g, from_b, from_a, s, t, x)
+
     return call(
         final_kernel,
-        shape((atoms, slab, e_dev), BF),
-        main + [pltpu.VMEM((4, slab, e_dev), BF)] + spare + [dma((3,))],
+        (shape((atoms, slab, e_dev), BF), shifted),
+        [pltpu.VMEM((5, ROWS, 256), F32), pltpu.VMEM((4, slab, e_dev), BF)] + spare + [dma((3,))],
         int(1e9),
         int(1e6),
-        [SMEM] + [VMEM] * 6,
-        HBM,
-    )(jobs, cross, near, s, t, inner, rim)
+        [SMEM] + [VMEM] * 7,
+        (HBM, VMEM),
+        {7: 1},
+    )(jobs, cross, near, s, t, inner, rim, x)[0]
 
 
 def solution(mesh):

time: 32.7 us -> 30.4 us (0.930)
  the two profiles are of different devices: /device:TPU:240 before, /device:TPU:248 now
where the time goes in v2:
time: 30.4 us; the launch traced here: 30.2 us
  Pallas kernels  15.1 us (50%)
  starting transfers between devices  13.4 us (44%)
  waiting for transfers between devices  0.96 us (3%)
  between operations  0.73 us (2%)
    ppermute x4, starting transfers between devices, swap(): return lax.ppermute(value, axis, pairs + [(b, a) for a, b in pairs])  13.4 us
    pallas_call x1, Pallas kernels, per_device(): call(build_kernel, (shape((2 * SLOTS, ROWS, DEPTH), BF), shape((2, 256, D...  4.85 us
    pallas_call x1, Pallas kernels, per_device(): call(local_kernel, (shape((4, slab, e_dev), BF), shape((4, ROWS, 256), F3...  3.76 us
    pallas_call x1, Pallas kernels, per_device(): call(final_kernel, (shape((atoms, slab, e_dev), BF), shifted), [pltpu.VME...  3.02 us
    pallas_call x1, Pallas kernels, per_device(): call(rim_kernel, (payload, payload, shifted), [pltpu.VMEM((5, ROWS, 256),...  2.31 us
    pallas_call x1, Pallas kernels, per_device(): call(pack_kernel, (half, half) + tuple((shape(v.shape, v.dtype) for v in...  1.2 us
    ppermute x4, waiting for transfers between devices, swap(): return lax.ppermute(value, axis, pairs + [(b, a) for a, b in pairs])  0.96 us
  transfers between devices with their start and end apart: 4, of which 1 were waited for; matrix products, arithmetic and copies ran while one was open for 0% of the time, Pallas kernels for 29%

profile of v2, /device:TPU:248, one launch (start us, length us, event | category | flops | bytes accessed | tf_op | source)
XLA Modules:
  0.0 30.2 jit_solution(14325701854479927705)
XLA Ops:
  0.0 1.2 %shard_map.64 = (bf16[4,200,128]{2,1,0:T(8,128)(2,1)S(1)}, bf16[4,200,128]{2,1,0:T(8,128)(2,1)S(1)}, bf16[8,200,128]{2,1,0:T(8,128)(2,1)S(1)}, bf16[16,800]{1,0:...) custom-call(bf16[8,200,128]{2,1,0:T(8,128)(2,1)} %g_hbm.1, bf16[16,800]{1,0:T(8,128)(2,1)} %coup_hbm.1, ...), custom_call_target="tpu_custom_call" | custom-call | flops 1000000 | bytes 1000000 | tf_op jit(solution)/shard_map/pallas_call | solution.py:320
  1.2 4.8 %collective-permute-start = (bf16[4,200,128]{2,1,0:T(8,128)(2,1)S(1)}, bf16[4,200,128]{2,1,0:T(8,128)(2,1)S(1)}, u32[]{:S(2)}, u32[]{:S(2)}) collective-permute-start(bf16[4,200,128]{2,1,0:T(8,128)(2,1)S(1)} %get-tuple-element.29), channel_id=1, source_target_pairs={{1,2},{3,4},{5,6},{7,8},{9,10},{11,12},{13,14},{2,1},{4,3},{6,5},{... | collective-permute-start | bytes 614408 | tf_op jit(solution)/shard_map/ppermute | solution.py:296
  6.1 2.0 %collective-permute-start.1 = (bf16[4,200,128]{2,1,0:T(8,128)(2,1)S(1)}, bf16[4,200,128]{2,1,0:T(8,128)(2,1)S(1)}, u32[]{:S(2)}, u32[]{:S(2)}) collective-permute-start(bf16[4,200,128]{2,1,0:T(8,128)(2,1)S(1)} %get-tuple-element.30), channel_id=1, source_target_pairs={{0,1},{2,3},{4,5},{6,7},{8,9},{10,11},{12,13},{14,15},{1,0},{3,2},... | collective-permute-start | bytes 614408 | tf_op jit(solution)/shard_map/ppermute | solution.py:296
  8.7 4.9 %shard_map.65 = (bf16[32,104,1024]{2,1,0:T(8,128)(2,1)S(1)}, bf16[2,256,1024]{2,1,0:T(8,128)(2,1)S(1)}, s32[152]{0:T(256)S(1)}, bf16[8,1024,256]{2,1,0:T(8,128)(2,1)S(1)}) custom-call(s32[1]{0:T(128)S(6)} %copy.13.cnt_ref, s32[2,16]{1,0:T(2,128)S(1)} %get-tuple-element.23.pairs_ref, f32[8]{0:T(128)S(1)} %get-tuple-element.24.occ_ref, ...), custom_call_target="tpu_custom_call" | custom-call | flops 3000000000 | bytes 8000000 | tf_op jit(solution)/shard_map/pallas_call | solution.py:333
  13.5 0.0 collective-permute-done.from_b
  13.5 1.0 %collective-permute-done.1.from_a = bf16[4,200,128]{2,1,0:T(8,128)(2,1)S(1)} collective-permute-done((bf16[4,200,128]{2,1,0:T(8,128)(2,1)S(1)}, bf16[4,200,128]{2,1,0:T(8,128)(2,1)S(1)}, u32[]{:S(2)}, u32[]{:S(2)}) %collective-permute-start.1) | collective-permute-done | bytes 204832 | tf_op jit(solution)/shard_map/ppermute | solution.py:296
  14.5 2.3 %shard_map.66 = (bf16[6,200,128]{2,1,0:T(8,128)(2,1)S(1)}, bf16[6,200,128]{2,1,0:T(8,128)(2,1)S(1)}, bf16[8,1024,256]{2,1,0:T(8,128)(2,1)S(1)}) custom-call(s32[152]{0:T(256)S(1)} %get-tuple-element.27.jobs_ref, bf16[8,200,128]{2,1,0:T(8,128)(2,1)S(1)} %get-tuple-element.28.g_ref, ...), custom_call_target="tpu_custom_call", output_to_operand_aliasing={{2}: (6, {})} | custom-call | flops 1000000000 | bytes 1000000 | tf_op jit(solution)/shard_map/pallas_call | solution.py:353
  16.8 1.9 %collective-permute-start.2 = (bf16[6,200,128]{2,1,0:T(8,128)(2,1)S(1)}, bf16[6,200,128]{2,1,0:T(8,128)(2,1)S(1)}, u32[]{:S(2)}, u32[]{:S(2)}) collective-permute-start(bf16[6,200,128]{2,1,0:T(8,128)(2,1)S(1)} %get-tuple-element.34), channel_id=1, source_target_pairs={{16,32},{48,64},{80,96},{112,128},{144,160},{176,192},{208,224},{2... | collective-permute-start | bytes 921608 | tf_op jit(solution)/shard_map/ppermute | solution.py:296
  18.7 4.7 %collective-permute-start.3 = (bf16[6,200,128]{2,1,0:T(8,128)(2,1)S(1)}, bf16[6,200,128]{2,1,0:T(8,128)(2,1)S(1)}, u32[]{:S(2)}, u32[]{:S(2)}) collective-permute-start(bf16[6,200,128]{2,1,0:T(8,128)(2,1)S(1)} %get-tuple-element.35), channel_id=1, source_target_pairs={{0,16},{32,48},{64,80},{96,112},{128,144},{160,176},{192,208},{224... | collective-permute-start | bytes 921608 | tf_op jit(solution)/shard_map/ppermute | solution.py:296
  23.4 3.8 %shard_map.67 = (bf16[4,200,128]{2,1,0:T(8,128)(2,1)S(1)}, f32[4,104,256]{2,1,0:T(8,128)S(1)}, bf16[8,1024,256]{2,1,0:T(8,128)(2,1)S(1)}) custom-call(s32[152]{0:T(256)S(1)} %get-tuple-element.27.jobs_ref, bf16[8,200,128]{2,1,0:T(8,128)(2,1)S(1)} %get-tuple-element.28.g_ref, ...), custom_call_target="tpu_custom_call", output_to_operand_aliasing={{2}: (6, {})} | custom-call | flops 3000000000 | bytes 1000000 | tf_op jit(solution)/shard_map/pallas_call | solution.py:366
  27.2 0.0 collective-permute-done.2.cross_ref
  27.2 0.0 collective-permute-done.3.near_ref
  27.2 3.0 %shard_map.68 = (bf16[8,200,128]{2,1,0:T(8,128)(2,1)}, bf16[8,1024,256]{2,1,0:T(8,128)(2,1)S(1)}) custom-call(s32[152]{0:T(256)S(1)} %get-tuple-element.27.jobs_ref, bf16[6,200,128]{2,1,0:T(8,128)(2,1)S(1)} %collective-permute-done.2.cross_ref, bf16[6,200,128]{2,1,0:T(8,128)(2,1)S(1)} %collective-permute-done.3.near_ref, ...), custom_call_target="tpu_custom_call", output_to_operand_aliasing={{1}: (7, {})} | custom-call | flops 1000000000 | bytes 1000000 | tf_op jit(solution)/shard_map/pallas_call | solution.py:377
Async XLA Ops:
  1.2 12.3 %collective-permute-start = (bf16[4,200,128]{2,1,0:T(8,128)(2,1)S(1)}, bf16[4,200,128]{2,1,0:T(8,128)(2,1)S(1)}, u32[]{:S(2)}, u32[]{:S(2)}) collective-permute-start(bf16[4,200,128]{2,1,0:T(8,128)(2,1)S(1)} %get-tuple-element.29), channel_id=1, source_target_pairs={{1,2},{3,4},{5,6},{7,8},{9,10},{11,12},{13,14},{2,1},{4,3},{6,5},{... | collective-permute-start | bytes 614408 | tf_op jit(solution)/shard_map/ppermute | solution.py:296
  6.1 8.4 %collective-permute-start.1 = (bf16[4,200,128]{2,1,0:T(8,128)(2,1)S(1)}, bf16[4,200,128]{2,1,0:T(8,128)(2,1)S(1)}, u32[]{:S(2)}, u32[]{:S(2)}) collective-permute-start(bf16[4,200,128]{2,1,0:T(8,128)(2,1)S(1)} %get-tuple-element.30), channel_id=1, source_target_pairs={{0,1},{2,3},{4,5},{6,7},{8,9},{10,11},{12,13},{14,15},{1,0},{3,2},... | collective-permute-start | bytes 614408 | tf_op jit(solution)/shard_map/ppermute | solution.py:296
  16.8 10.4 %collective-permute-start.2 = (bf16[6,200,128]{2,1,0:T(8,128)(2,1)S(1)}, bf16[6,200,128]{2,1,0:T(8,128)(2,1)S(1)}, u32[]{:S(2)}, u32[]{:S(2)}) collective-permute-start(bf16[6,200,128]{2,1,0:T(8,128)(2,1)S(1)} %get-tuple-element.34), channel_id=1, source_target_pairs={{16,32},{48,64},{80,96},{112,128},{144,160},{176,192},{208,224},{2... | collective-permute-start | bytes 921608 | tf_op jit(solution)/shard_map/ppermute | solution.py:296
  18.7 8.4 %collective-permute-start.3 = (bf16[6,200,128]{2,1,0:T(8,128)(2,1)S(1)}, bf16[6,200,128]{2,1,0:T(8,128)(2,1)S(1)}, u32[]{:S(2)}, u32[]{:S(2)}) collective-permute-start(bf16[6,200,128]{2,1,0:T(8,128)(2,1)S(1)} %get-tuple-element.35), channel_id=1, source_target_pairs={{0,16},{32,48},{64,80},{96,112},{128,144},{160,176},{192,208},{224... | collective-permute-start | bytes 921608 | tf_op jit(solution)/shard_map/ppermute | solution.py:296

commit v3 on v2

--- a/solution.py
+++ b/solution.py
@@ -55,25 +55,24 @@
             x_ref[x, m * LANES + 96 : (m + 1) * LANES, :] = jnp.zeros((32, 256), BF)
 
     def listed(s, carry):
-        near, far = carry
+        near, far, down, up = carry
         first = pairs_ref[0, s] - base
         second = pairs_ref[1, s] - base
         local = jnp.where((second >= 0) & (second < ATOMS), 1, 0)
-        rim = jnp.where(first >= 4, first - 4, first)
+        below = jnp.where(second < 0, 1, 0)
         out = jnp.where(second < 0, second + 2, second - 6)
         jobs_ref[near] = s + 64 * second + 4096 * first
         jobs_ref[near + 1] = s + SLOTS + 64 * first + 4096 * second
         jobs_ref[LISTS + far] = s + SLOTS + 64 * first + 4096 * out
-        jobs_ref[2 * LISTS + far] = s + 64 * out + 4096 * rim
-        return near + 2 * local, far + 1 - local
-
-    near, far = lax.fori_loop(0, count, listed, (jnp.int32(0), jnp.int32(0)))
-    for j in range(8):
-        jobs_ref[near + j] = 4096 * ATOMS
-        jobs_ref[LISTS + far + j] = 4096 * 4
-        jobs_ref[2 * LISTS + far + j] = 4096 * 4
-    jobs_ref[3 * LISTS] = near
-    jobs_ref[3 * LISTS + 1] = far
+        jobs_ref[2 * LISTS + down] = s + 64 * out + 4096 * first
+        jobs_ref[3 * LISTS + up] = s + 64 * out + 4096 * (first - 6)
+        return near + 2 * local, far + 1 - local, down + below, up + 1 - local - below
+
+    counted = lax.fori_loop(0, count, listed, (jnp.int32(0),) * 4)
+    for kind, (many, spare) in enumerate(zip(counted, (ATOMS, 4, 2, 2))):
+        for j in range(8):
+            jobs_ref[kind * LISTS + many + j] = 4096 * spare
+        jobs_ref[4 * LISTS + kind] = many
 
     coup = coup_ref[...].astype(F32)
     width = 7 * LANES
@@ -198,10 +197,12 @@
     return rows[0:SLAB, :]
 
 
-def run_jobs(jobs_ref, at, count, chunk, t_ref, x_ref, acc):
+def run_jobs(jobs_ref, kind, chunk, t_ref, x_ref, acc):
+    count = jobs_ref[4 * LISTS + kind]
+
     def step(i, carry):
         for j in range(chunk):
-            job = jobs_ref[at + i * chunk + j]
+            job = jobs_ref[kind * LISTS + i * chunk + j]
             t, src, dst = job & 63, (job >> 6) & 63, job >> 12
             acc[dst] = acc[dst] + jnp.dot(t_ref[t], x_ref[src], preferred_element_type=F32)
         return carry
@@ -210,32 +211,19 @@
 
 
 def rim_kernel(
-    jobs_ref, g_ref, from_b, from_a, s_ref, t_ref, x_old, cross_ref, near_ref, x, part, lhs, low, rows
+    jobs_ref, g_ref, from_b, from_a, s_ref, t_ref, x_old, down_ref, up_ref, x, part, lhs, low, rows
 ):
-    halos = []
     for at, atom in enumerate((0, 1, 6, 7)):
+        ref = up_ref if atom >= 6 else down_ref
         halo = halo_of(from_a, from_b, atom)
-        halos.append(halo)
+        ref[at % 2] = g_ref[atom]
+        ref[2 + at % 2] = halo
         shift_atom(g_ref[atom], halo, s_ref, atom // 4, lhs.at[at], low.at[at], store_in(x, atom))
     part[...] = jnp.zeros(part.shape, F32)
-    run_jobs(jobs_ref, LISTS, jobs_ref[3 * LISTS + 1], 4, t_ref, x, part)
-    odd = lax.axis_index("atom") % 2
-
-    def fill(ref, side):
-        for j in range(2):
-            ref[j] = g_ref[6 * side + j]
-            ref[2 + j] = halos[2 * side + j]
-            ref[4 + j] = unfold(part[2 * side + j], rows).astype(BF)
-
-    @pl.when(odd == 1)
-    def _():
-        fill(cross_ref, 1)
-        fill(near_ref, 0)
-
-    @pl.when(odd == 0)
-    def _():
-        fill(cross_ref, 0)
-        fill(near_ref, 1)
+    run_jobs(jobs_ref, 1, 4, t_ref, x, part)
+    for at in range(4):
+        ref = up_ref if at >= 2 else down_ref
+        ref[4 + at % 2] = unfold(part[at], rows.at[at]).astype(BF)
 
 
 def local_kernel(
@@ -245,55 +233,51 @@
         halo = halo_of(from_a, from_b, atom)
         shift_atom(g_ref[atom], halo, s_ref, atom // 4, lhs.at[at], low.at[at], store_in(x, atom))
     acc[...] = jnp.zeros(acc.shape, F32)
-    run_jobs(jobs_ref, 0, jobs_ref[3 * LISTS], 8, t_ref, x, acc)
+    run_jobs(jobs_ref, 0, 8, t_ref, x, acc)
     for j in range(4):
-        inner_ref[j] = unfold(acc[2 + j], rows).astype(BF)
+        inner_ref[j] = unfold(acc[2 + j], rows.at[j]).astype(BF)
         rim_ref[j] = acc[j if j < 2 else j + 4]
 
 
-def final_kernel(
-    jobs_ref, cross_ref, near_ref, s_ref, t_ref, inner_ref, rim_ref, x_old, out_ref, x, acc, done, lhs, low, rows, sems
+def upper_kernel(jobs_ref, got_ref, s_ref, t_ref, rim_ref, x_old, out_ref, x, acc, lhs, low, rows):
+    for j in range(2):
+        shift_atom(got_ref[j], got_ref[2 + j], s_ref, 0, lhs.at[j], low.at[j], store_in(x, 2 + j))
+    acc[0:2] = rim_ref[2:4]
+    run_jobs(jobs_ref, 3, 4, t_ref, x, acc)
+    for j in range(2):
+        out_ref[j] = (unfold(acc[j], rows.at[j]) + got_ref[4 + j].astype(F32)).astype(BF)
+
+
+def lower_kernel(
+    jobs_ref, got_ref, s_ref, t_ref, rim_ref, inner_ref, upper_ref, x_old, out_ref, x, acc, done, lhs, low, rows, sems
 ):
-    early = pltpu.make_async_copy(inner_ref, out_ref.at[2:6], sems.at[0])
-    early.start()
-    odd = lax.axis_index("atom") % 2
-
-    def take(ref, side):
-        for j in range(2):
-            at = 2 * side + j
-            shift_atom(ref[j], ref[2 + j], s_ref, 1 - side, lhs.at[at], low.at[at], store_in(x, at))
-
-    @pl.when(odd == 1)
-    def _():
-        take(cross_ref, 1)
-        take(near_ref, 0)
-
-    @pl.when(odd == 0)
-    def _():
-        take(cross_ref, 0)
-        take(near_ref, 1)
-
-    acc[0:4] = rim_ref[...]
-    run_jobs(jobs_ref, 2 * LISTS, jobs_ref[3 * LISTS + 1], 4, t_ref, x, acc)
-    for j in range(4):
-        side = j // 2
-        got = jnp.where(
-            odd == side, cross_ref[4 + j % 2].astype(F32), near_ref[4 + j % 2].astype(F32)
-        )
-        done[j] = (unfold(acc[j], rows) + got).astype(BF)
-    lower = pltpu.make_async_copy(done.at[0:2], out_ref.at[0:2], sems.at[1])
-    upper = pltpu.make_async_copy(done.at[2:4], out_ref.at[6:8], sems.at[2])
-    lower.start()
-    upper.start()
-    early.wait()
-    lower.wait()
-    upper.wait()
+    copies = [
+        pltpu.make_async_copy(inner_ref, out_ref.at[2:6], sems.at[0]),
+        pltpu.make_async_copy(upper_ref, out_ref.at[6:8], sems.at[1]),
+        pltpu.make_async_copy(done, out_ref.at[0:2], sems.at[2]),
+    ]
+    copies[0].start()
+    copies[1].start()
+    for j in range(2):
+        shift_atom(got_ref[j], got_ref[2 + j], s_ref, 1, lhs.at[j], low.at[j], store_in(x, j))
+    acc[0:2] = rim_ref[0:2]
+    run_jobs(jobs_ref, 2, 4, t_ref, x, acc)
+    for j in range(2):
+        done[j] = (unfold(acc[j], rows.at[j]) + got_ref[4 + j].astype(F32)).astype(BF)
+    copies[2].start()
+    for copy in copies:
+        copy.wait()
 
 
 def swap(value, axis, start):
     count = lax.axis_size(axis)
     pairs = [(i, i + 1) for i in range(start, count - 1, 2)]
     return lax.ppermute(value, axis, pairs + [(b, a) for a, b in pairs])
+
+
+def step_of(value, axis, by):
+    count = lax.axis_size(axis)
+    return lax.ppermute(value, axis, [(i, i + by) for i in range(count) if 0 <= i + by < count])
 
 
 def call(kernel, outs, scratch, flops, moved, specs, out_specs, aliases={}):
@@ -332,7 +316,7 @@
     shifted = shape((ATOMS, DEPTH, 256), BF)
     t, s, jobs, x = call(
         build_kernel,
-        (shape((2 * SLOTS, ROWS, DEPTH), BF), shape((2, 256, DEPTH), BF), shape((3 * LISTS + 8,), I32), shifted),
+        (shape((2 * SLOTS, ROWS, DEPTH), BF), shape((2, 256, DEPTH), BF), shape((4 * LISTS + 4,), I32), shifted),
         [
             pltpu.VMEM((MODES * SLOTS, LANES), F32),
             pltpu.VMEM((MODES * SLOTS * 16, LANES), BF),
@@ -347,10 +331,10 @@
     spare = [
         pltpu.VMEM((4, 2 * PITCH, 256), BF),
         pltpu.VMEM((4, PITCH, 256), F32),
-        pltpu.VMEM((208, LANES), F32),
+        pltpu.VMEM((4, 208, LANES), F32),
     ]
     payload = shape((6, slab, e_dev), BF)
-    cross, near, x = call(
+    down, up, x = call(
         rim_kernel,
         (payload, payload, shifted),
         [pltpu.VMEM((5, ROWS, 256), F32)] + spare,
@@ -360,8 +344,8 @@
         (VMEM, VMEM, VMEM),
         {6: 2},
     )(jobs, g, from_b, from_a, s, t, x)
-    cross = swap(cross, "atom", 1)
-    near = swap(near, "atom", 0)
+    above = step_of(down, "atom", -1)
+    below = step_of(up, "atom", 1)
 
     inner, rim, x = call(
         local_kernel,
@@ -374,16 +358,28 @@
         {6: 2},
     )(jobs, g, from_b, from_a, s, t, x)
 
+    sums = pltpu.VMEM((3, ROWS, 256), F32)
+    upper, x = call(
+        upper_kernel,
+        (shape((2, slab, e_dev), BF), shifted),
+        [sums] + spare,
+        int(5e8),
+        int(1e6),
+        [SMEM] + [VMEM] * 5,
+        (VMEM, VMEM),
+        {5: 1},
+    )(jobs, above, s, t, rim, x)
+
     return call(
-        final_kernel,
+        lower_kernel,
         (shape((atoms, slab, e_dev), BF), shifted),
-        [pltpu.VMEM((5, ROWS, 256), F32), pltpu.VMEM((4, slab, e_dev), BF)] + spare + [dma((3,))],
-        int(1e9),
+        [sums, pltpu.VMEM((2, slab, e_dev), BF)] + spare + [dma((3,))],
+        int(5e8),
         int(1e6),
         [SMEM] + [VMEM] * 7,
         (HBM, VMEM),
         {7: 1},
-    )(jobs, cross, near, s, t, inner, rim, x)[0]
+    )(jobs, below, s, t, rim, inner, upper, x)[0]
 
 
 def solution(mesh):

time: 30.4 us -> 31.4 us (1.033)
  the two profiles are of different devices: /device:TPU:248 before, /device:TPU:408 now
where the time goes in v3:
time: 31.4 us; the launch traced here: 31.2 us
  Pallas kernels  13.6 us (43%)
  starting transfers between devices  11.1 us (35%)
  waiting for transfers between devices  5.75 us (18%)
  between operations  0.73 us (2%)
    ppermute x2, starting transfers between devices, swap(): return lax.ppermute(value, axis, pairs + [(b, a) for a, b in pairs])  6.8 us
    ppermute x2, starting transfers between devices, step_of(): lax.ppermute(value, axis, [(i, i + by) for i in range(count) if 0 <= i +...  4.33 us
    pallas_call x1, Pallas kernels, per_device(): call(build_kernel, (shape((2 * SLOTS, ROWS, DEPTH), BF), shape((2, 256, D...  3.89 us
    ppermute x2, waiting for transfers between devices, step_of(): lax.ppermute(value, axis, [(i, i + by) for i in range(count) if 0 <= i +...  3.83 us
    pallas_call x1, Pallas kernels, per_device(): call(lower_kernel, (shape((atoms, slab, e_dev), BF), shifted), [sums, plt...  2.64 us
    pallas_call x1, Pallas kernels, per_device(): call(rim_kernel, (payload, payload, shifted), [pltpu.VMEM((5, ROWS, 256),...  2.24 us
    pallas_call x1, Pallas kernels, per_device(): call(local_kernel, (shape((4, slab, e_dev), BF), shape((4, ROWS, 256), F3...  2.13 us
    ppermute x2, waiting for transfers between devices, swap(): return lax.ppermute(value, axis, pairs + [(b, a) for a, b in pairs])  1.92 us
  transfers between devices with their start and end apart: 4, of which 3 were waited for; matrix products, arithmetic and copies ran while one was open for 0% of the time, Pallas kernels for 24%

profile of v3, /device:TPU:408, one launch (start us, length us, event | category | flops | bytes accessed | tf_op | source)
XLA Modules:
  0.0 31.2 jit_solution(10364665960301527389)
XLA Ops:
  0.0 1.2 %shard_map.64 = (bf16[4,200,128]{2,1,0:T(8,128)(2,1)S(1)}, bf16[4,200,128]{2,1,0:T(8,128)(2,1)S(1)}, bf16[8,200,128]{2,1,0:T(8,128)(2,1)S(1)}, bf16[16,800]{1,0:...) custom-call(bf16[8,200,128]{2,1,0:T(8,128)(2,1)} %g_hbm.1, bf16[16,800]{1,0:T(8,128)(2,1)} %coup_hbm.1, ...), custom_call_target="tpu_custom_call" | custom-call | flops 1000000 | bytes 1000000 | tf_op jit(solution)/shard_map/pallas_call | solution.py:304
  1.2 4.8 %collective-permute-start = (bf16[4,200,128]{2,1,0:T(8,128)(2,1)S(1)}, bf16[4,200,128]{2,1,0:T(8,128)(2,1)S(1)}, u32[]{:S(2)}, u32[]{:S(2)}) collective-permute-start(bf16[4,200,128]{2,1,0:T(8,128)(2,1)S(1)} %get-tuple-element.31), channel_id=1, source_target_pairs={{1,2},{3,4},{5,6},{7,8},{9,10},{11,12},{13,14},{2,1},{4,3},{6,5},{... | collective-permute-start | bytes 614408 | tf_op jit(solution)/shard_map/ppermute | solution.py:275
  6.1 2.0 %collective-permute-start.1 = (bf16[4,200,128]{2,1,0:T(8,128)(2,1)S(1)}, bf16[4,200,128]{2,1,0:T(8,128)(2,1)S(1)}, u32[]{:S(2)}, u32[]{:S(2)}) collective-permute-start(bf16[4,200,128]{2,1,0:T(8,128)(2,1)S(1)} %get-tuple-element.32), channel_id=1, source_target_pairs={{0,1},{2,3},{4,5},{6,7},{8,9},{10,11},{12,13},{14,15},{1,0},{3,2},... | collective-permute-start | bytes 614408 | tf_op jit(solution)/shard_map/ppermute | solution.py:275
  8.7 3.9 %shard_map.65 = (bf16[32,104,1024]{2,1,0:T(8,128)(2,1)S(1)}, bf16[2,256,1024]{2,1,0:T(8,128)(2,1)S(1)}, s32[196]{0:T(256)S(1)}, bf16[8,1024,256]{2,1,0:T(8,128)(2,1)S(1)}) custom-call(s32[1]{0:T(128)S(6)} %copy.15.cnt_ref, s32[2,16]{1,0:T(2,128)S(1)} %get-tuple-element.25.pairs_ref, f32[8]{0:T(128)S(1)} %get-tuple-element.26.occ_ref, ...), custom_call_target="tpu_custom_call" | custom-call | flops 3000000000 | bytes 8000000 | tf_op jit(solution)/shard_map/pallas_call | solution.py:317
  12.6 0.0 collective-permute-done.from_b
  12.6 1.9 %collective-permute-done.1.from_a = bf16[4,200,128]{2,1,0:T(8,128)(2,1)S(1)} collective-permute-done((bf16[4,200,128]{2,1,0:T(8,128)(2,1)S(1)}, bf16[4,200,128]{2,1,0:T(8,128)(2,1)S(1)}, u32[]{:S(2)}, u32[]{:S(2)}) %collective-permute-start.1) | collective-permute-done | bytes 204832 | tf_op jit(solution)/shard_map/ppermute | solution.py:275
  14.5 2.2 %shard_map.66 = (bf16[6,200,128]{2,1,0:T(8,128)(2,1)S(1)}, bf16[6,200,128]{2,1,0:T(8,128)(2,1)S(1)}, bf16[8,1024,256]{2,1,0:T(8,128)(2,1)S(1)}) custom-call(s32[196]{0:T(256)S(1)} %get-tuple-element.29.jobs_ref, bf16[8,200,128]{2,1,0:T(8,128)(2,1)S(1)} %get-tuple-element.30.g_ref, ...), custom_call_target="tpu_custom_call", output_to_operand_aliasing={{2}: (6, {})} | custom-call | flops 1000000000 | bytes 1000000 | tf_op jit(solution)/shard_map/pallas_call | solution.py:337
  16.7 2.4 %collective-permute-start.3 = (bf16[6,200,128]{2,1,0:T(8,128)(2,1)S(1)}, bf16[6,200,128]{2,1,0:T(8,128)(2,1)S(1)}, u32[]{:S(2)}, u32[]{:S(2)}) collective-permute-start(bf16[6,200,128]{2,1,0:T(8,128)(2,1)S(1)} %get-tuple-element.40), channel_id=1, source_target_pairs={{16,0},{32,16},{48,32},{64,48},{80,64},{96,80},{112,96},{128,112},... | collective-permute-start | bytes 921608 | tf_op jit(solution)/shard_map/ppermute | solution.py:280
  19.1 1.9 %collective-permute-start.2 = (bf16[6,200,128]{2,1,0:T(8,128)(2,1)S(1)}, bf16[6,200,128]{2,1,0:T(8,128)(2,1)S(1)}, u32[]{:S(2)}, u32[]{:S(2)}) collective-permute-start(bf16[6,200,128]{2,1,0:T(8,128)(2,1)S(1)} %get-tuple-element.36), channel_id=1, source_target_pairs={{0,16},{16,32},{32,48},{48,64},{64,80},{80,96},{96,112},{112,128},... | collective-permute-start | bytes 921608 | tf_op jit(solution)/shard_map/ppermute | solution.py:280
  21.1 2.1 %shard_map.67 = (bf16[4,200,128]{2,1,0:T(8,128)(2,1)S(1)}, f32[4,104,256]{2,1,0:T(8,128)S(1)}, bf16[8,1024,256]{2,1,0:T(8,128)(2,1)S(1)}) custom-call(s32[196]{0:T(256)S(1)} %get-tuple-element.29.jobs_ref, bf16[8,200,128]{2,1,0:T(8,128)(2,1)S(1)} %get-tuple-element.30.g_ref, ...), custom_call_target="tpu_custom_call", output_to_operand_aliasing={{2}: (6, {})} | custom-call | flops 3000000000 | bytes 1000000 | tf_op jit(solution)/shard_map/pallas_call | solution.py:350
  23.2 0.3 collective-permute-done.3.got_ref
  23.5 1.5 %shard_map.68 = (bf16[2,200,128]{2,1,0:T(8,128)(2,1)S(1)}, bf16[8,1024,256]{2,1,0:T(8,128)(2,1)S(1)}) custom-call(s32[196]{0:T(256)S(1)} %get-tuple-element.29.jobs_ref, bf16[6,200,128]{2,1,0:T(8,128)(2,1)S(1)} %collective-permute-done.3.got_ref, bf16[2,256,1024]{2,1,0:T(8,128)(2,1)S(1)} %get-tuple-element.33.s_ref, ...), custom_call_target="tpu_custom_call", output_to_operand_aliasing={{1}: (5, {})} | custom-call | flops 500000000 | bytes 1000000 | tf_op jit(solution)/shard_map/pallas_call | solution.py:362
  25.0 3.6 %collective-permute-done.2.got_ref = bf16[6,200,128]{2,1,0:T(8,128)(2,1)S(1)} collective-permute-done((bf16[6,200,128]{2,1,0:T(8,128)(2,1)S(1)}, bf16[6,200,128]{2,1,0:T(8,128)(2,1)S(1)}, u32[]{:S(2)}, u32[]{:S(2)}) %collective-permute-start.2) | collective-permute-done | bytes 307232 | tf_op jit(solution)/shard_map/ppermute | solution.py:280
  28.5 2.6 %shard_map.69 = (bf16[8,200,128]{2,1,0:T(8,128)(2,1)}, bf16[8,1024,256]{2,1,0:T(8,128)(2,1)S(1)}) custom-call(s32[196]{0:T(256)S(1)} %get-tuple-element.29.jobs_ref, bf16[6,200,128]{2,1,0:T(8,128)(2,1)S(1)} %collective-permute-done.2.got_ref, bf16[2,256,1024]{2,1,0:T(8,128)(2,1)S(1)} %get-tuple-element.33.s_ref, ...), custom_call_target="tpu_custom_call", output_to_operand_aliasing={{1}: (7, {})} | custom-call | flops 500000000 | bytes 1000000 | tf_op jit(solution)/shard_map/pallas_call | solution.py:373
Async XLA Ops:
  1.2 11.4 %collective-permute-start = (bf16[4,200,128]{2,1,0:T(8,128)(2,1)S(1)}, bf16[4,200,128]{2,1,0:T(8,128)(2,1)S(1)}, u32[]{:S(2)}, u32[]{:S(2)}) collective-permute-start(bf16[4,200,128]{2,1,0:T(8,128)(2,1)S(1)} %get-tuple-element.31), channel_id=1, source_target_pairs={{1,2},{3,4},{5,6},{7,8},{9,10},{11,12},{13,14},{2,1},{4,3},{6,5},{... | collective-permute-start | bytes 614408 | tf_op jit(solution)/shard_map/ppermute | solution.py:275
  6.1 8.4 %collective-permute-start.1 = (bf16[4,200,128]{2,1,0:T(8,128)(2,1)S(1)}, bf16[4,200,128]{2,1,0:T(8,128)(2,1)S(1)}, u32[]{:S(2)}, u32[]{:S(2)}) collective-permute-start(bf16[4,200,128]{2,1,0:T(8,128)(2,1)S(1)} %get-tuple-element.32), channel_id=1, source_target_pairs={{0,1},{2,3},{4,5},{6,7},{8,9},{10,11},{12,13},{14,15},{1,0},{3,2},... | collective-permute-start | bytes 614408 | tf_op jit(solution)/shard_map/ppermute | solution.py:275
  16.7 6.7 %collective-permute-start.3 = (bf16[6,200,128]{2,1,0:T(8,128)(2,1)S(1)}, bf16[6,200,128]{2,1,0:T(8,128)(2,1)S(1)}, u32[]{:S(2)}, u32[]{:S(2)}) collective-permute-start(bf16[6,200,128]{2,1,0:T(8,128)(2,1)S(1)} %get-tuple-element.40), channel_id=1, source_target_pairs={{16,0},{32,16},{48,32},{64,48},{80,64},{96,80},{112,96},{128,112},... | collective-permute-start | bytes 921608 | tf_op jit(solution)/shard_map/ppermute | solution.py:280
  19.1 9.4 %collective-permute-start.2 = (bf16[6,200,128]{2,1,0:T(8,128)(2,1)S(1)}, bf16[6,200,128]{2,1,0:T(8,128)(2,1)S(1)}, u32[]{:S(2)}, u32[]{:S(2)}) collective-permute-start(bf16[6,200,128]{2,1,0:T(8,128)(2,1)S(1)} %get-tuple-element.36), channel_id=1, source_target_pairs={{0,16},{16,32},{32,48},{48,64},{64,80},{80,96},{96,112},{112,128},... | collective-permute-start | bytes 921608 | tf_op jit(solution)/shard_map/ppermute | solution.py:280

commit v4 on v3

--- a/solution.py
+++ b/solution.py
@@ -47,7 +47,13 @@
         copy.wait()
 
 
-def build_kernel(cnt_ref, pairs_ref, occ_ref, off_ref, coup_ref, t_ref, s_ref, jobs_ref, x_ref, cm, v, c12):
+def build_kernel(
+    cnt_ref, pairs_in, occ_in, off_in, coup_ref, t_ref, s_ref, jobs_out, x_ref, cm, v, c12, pairs_ref, occ_ref, off_ref, jobs_ref, sems
+):
+    moves = ((pairs_in, pairs_ref), (occ_in, occ_ref), (off_in, off_ref))
+    copies = [pltpu.make_async_copy(src, dst, sems.at[i]) for i, (src, dst) in enumerate(moves)]
+    for copy in copies:
+        copy.start()
     count = cnt_ref[0]
     base = lax.axis_index("atom") * ATOMS
     for x in range(ATOMS):
@@ -68,11 +74,15 @@
         jobs_ref[3 * LISTS + up] = s + 64 * out + 4096 * (first - 6)
         return near + 2 * local, far + 1 - local, down + below, up + 1 - local - below
 
+    for copy in copies:
+        copy.wait()
     counted = lax.fori_loop(0, count, listed, (jnp.int32(0),) * 4)
     for kind, (many, spare) in enumerate(zip(counted, (ATOMS, 4, 2, 2))):
         for j in range(8):
             jobs_ref[kind * LISTS + many + j] = 4096 * spare
         jobs_ref[4 * LISTS + kind] = many
+    send = pltpu.make_async_copy(jobs_ref, jobs_out, sems.at[3])
+    send.start()
 
     coup = coup_ref[...].astype(F32)
     width = 7 * LANES
@@ -157,6 +167,7 @@
             s_ref[which, :, m * LANES : (m + 1) * LANES] = jnp.where(
                 away == -step, occ, jnp.where(away == step, occ + 1.0, 0.0)
             ).astype(BF)
+    send.wait()
 
 
 def shift_atom(center, halo, s_ref, which, lhs, low, store):
@@ -197,6 +208,17 @@
     return rows[0:SLAB, :]
 
 
+class Lists:
+    def __init__(self, source, held, sem):
+        self.held = held
+        self.copy = pltpu.make_async_copy(source, held, sem)
+        self.copy.start()
+
+    def ready(self):
+        self.copy.wait()
+        return self.held
+
+
 def run_jobs(jobs_ref, kind, chunk, t_ref, x_ref, acc):
     count = jobs_ref[4 * LISTS + kind]
 
@@ -211,8 +233,9 @@
 
 
 def rim_kernel(
-    jobs_ref, g_ref, from_b, from_a, s_ref, t_ref, x_old, down_ref, up_ref, x, part, lhs, low, rows
+    jobs_ref, g_ref, from_b, from_a, s_ref, t_ref, x_old, down_ref, up_ref, x, part, lhs, low, rows, held, sem
 ):
+    lists = Lists(jobs_ref, held, sem)
     for at, atom in enumerate((0, 1, 6, 7)):
         ref = up_ref if atom >= 6 else down_ref
         halo = halo_of(from_a, from_b, atom)
@@ -220,37 +243,55 @@
         ref[2 + at % 2] = halo
         shift_atom(g_ref[atom], halo, s_ref, atom // 4, lhs.at[at], low.at[at], store_in(x, atom))
     part[...] = jnp.zeros(part.shape, F32)
-    run_jobs(jobs_ref, 1, 4, t_ref, x, part)
+    run_jobs(lists.ready(), 1, 4, t_ref, x, part)
     for at in range(4):
         ref = up_ref if at >= 2 else down_ref
         ref[4 + at % 2] = unfold(part[at], rows.at[at]).astype(BF)
 
 
-def local_kernel(
-    jobs_ref, g_ref, from_b, from_a, s_ref, t_ref, x_old, inner_ref, rim_ref, x, acc, lhs, low, rows
+def early_kernel(
+    jobs_ref, g_ref, from_b, from_a, s_ref, t_ref, x_old, up_old, inner_ref, rim_ref, x, up_ref, acc, lhs, low, rows, held, sem
 ):
+    @pl.when(lax.axis_index("atom") % 2 == 1)
+    def _():
+        lists = Lists(jobs_ref, held, sem)
+        local_terms(lists, g_ref, from_b, from_a, s_ref, t_ref, inner_ref, rim_ref, x, acc, lhs, low, rows)
+
+
+def late_kernel(
+    jobs_ref, g_ref, from_b, from_a, s_ref, t_ref, x_old, inner_old, rim_old, inner_ref, rim_ref, x, acc, lhs, low, rows, held, sem
+):
+    @pl.when(lax.axis_index("atom") % 2 == 0)
+    def _():
+        lists = Lists(jobs_ref, held, sem)
+        local_terms(lists, g_ref, from_b, from_a, s_ref, t_ref, inner_ref, rim_ref, x, acc, lhs, low, rows)
+
+
+def local_terms(lists, g_ref, from_b, from_a, s_ref, t_ref, inner_ref, rim_ref, x, acc, lhs, low, rows):
     for at, atom in enumerate((2, 3, 4, 5)):
         halo = halo_of(from_a, from_b, atom)
         shift_atom(g_ref[atom], halo, s_ref, atom // 4, lhs.at[at], low.at[at], store_in(x, atom))
     acc[...] = jnp.zeros(acc.shape, F32)
-    run_jobs(jobs_ref, 0, 8, t_ref, x, acc)
+    run_jobs(lists.ready(), 0, 8, t_ref, x, acc)
     for j in range(4):
         inner_ref[j] = unfold(acc[2 + j], rows.at[j]).astype(BF)
         rim_ref[j] = acc[j if j < 2 else j + 4]
 
 
-def upper_kernel(jobs_ref, got_ref, s_ref, t_ref, rim_ref, x_old, out_ref, x, acc, lhs, low, rows):
+def upper_kernel(jobs_ref, got_ref, s_ref, t_ref, rim_ref, x_old, out_ref, x, acc, lhs, low, rows, held, sem):
+    lists = Lists(jobs_ref, held, sem)
     for j in range(2):
         shift_atom(got_ref[j], got_ref[2 + j], s_ref, 0, lhs.at[j], low.at[j], store_in(x, 2 + j))
     acc[0:2] = rim_ref[2:4]
-    run_jobs(jobs_ref, 3, 4, t_ref, x, acc)
+    run_jobs(lists.ready(), 3, 4, t_ref, x, acc)
     for j in range(2):
         out_ref[j] = (unfold(acc[j], rows.at[j]) + got_ref[4 + j].astype(F32)).astype(BF)
 
 
 def lower_kernel(
-    jobs_ref, got_ref, s_ref, t_ref, rim_ref, inner_ref, upper_ref, x_old, out_ref, x, acc, done, lhs, low, rows, sems
+    jobs_ref, got_ref, s_ref, t_ref, rim_ref, inner_ref, upper_ref, x_old, out_ref, x, acc, done, lhs, low, rows, held, sem, sems
 ):
+    lists = Lists(jobs_ref, held, sem)
     copies = [
         pltpu.make_async_copy(inner_ref, out_ref.at[2:6], sems.at[0]),
         pltpu.make_async_copy(upper_ref, out_ref.at[6:8], sems.at[1]),
@@ -261,7 +302,7 @@
     for j in range(2):
         shift_atom(got_ref[j], got_ref[2 + j], s_ref, 1, lhs.at[j], low.at[j], store_in(x, j))
     acc[0:2] = rim_ref[0:2]
-    run_jobs(jobs_ref, 2, 4, t_ref, x, acc)
+    run_jobs(lists.ready(), 2, 4, t_ref, x, acc)
     for j in range(2):
         done[j] = (unfold(acc[j], rows.at[j]) + got_ref[4 + j].astype(F32)).astype(BF)
     copies[2].start()
@@ -321,17 +362,24 @@
             pltpu.VMEM((MODES * SLOTS, LANES), F32),
             pltpu.VMEM((MODES * SLOTS * 16, LANES), BF),
             pltpu.VMEM((MODES * SLOTS * 16, 256), F32),
+            pltpu.SMEM((2, SLOTS), I32),
+            pltpu.SMEM((MODES,), F32),
+            pltpu.SMEM((MODES,), I32),
+            pltpu.SMEM((4 * LISTS + 4,), I32),
+            dma((4,)),
         ],
         int(3e9),
         int(8e6),
-        [SMEM] * 4 + [VMEM],
-        (VMEM, VMEM, SMEM, VMEM),
+        [SMEM] + [VMEM] * 4,
+        (VMEM,) * 4,
     )(counts, pairs, occ, off, coup)
 
     spare = [
         pltpu.VMEM((4, 2 * PITCH, 256), BF),
         pltpu.VMEM((4, PITCH, 256), F32),
         pltpu.VMEM((4, 208, LANES), F32),
+        pltpu.SMEM((4 * LISTS + 4,), I32),
+        dma(()),
     ]
     payload = shape((6, slab, e_dev), BF)
     down, up, x = call(
@@ -340,23 +388,35 @@
         [pltpu.VMEM((5, ROWS, 256), F32)] + spare,
         int(1e9),
         int(1e6),
-        [SMEM] + [VMEM] * 6,
+        [VMEM] * 7,
         (VMEM, VMEM, VMEM),
         {6: 2},
     )(jobs, g, from_b, from_a, s, t, x)
     above = step_of(down, "atom", -1)
+    inner = shape((4, slab, e_dev), BF)
+    rim = shape((4, ROWS, 256), F32)
+    sums = pltpu.VMEM((9, ROWS, 256), F32)
+    inner, rim, x, up = call(
+        early_kernel,
+        (inner, rim, shifted, payload),
+        [sums] + spare,
+        int(3e9),
+        int(1e6),
+        [VMEM] * 8,
+        (VMEM,) * 4,
+        {6: 2, 7: 3},
+    )(jobs, g, from_b, from_a, s, t, x, up)
     below = step_of(up, "atom", 1)
-
     inner, rim, x = call(
-        local_kernel,
-        (shape((4, slab, e_dev), BF), shape((4, ROWS, 256), F32), shifted),
-        [pltpu.VMEM((9, ROWS, 256), F32)] + spare,
+        late_kernel,
+        (shape(inner.shape, BF), shape(rim.shape, F32), shifted),
+        [sums] + spare,
         int(3e9),
         int(1e6),
-        [SMEM] + [VMEM] * 6,
-        (VMEM, VMEM, VMEM),
-        {6: 2},
-    )(jobs, g, from_b, from_a, s, t, x)
+        [VMEM] * 9,
+        (VMEM,) * 3,
+        {7: 0, 8: 1, 6: 2},
+    )(jobs, g, from_b, from_a, s, t, x, inner, rim)
 
     sums = pltpu.VMEM((3, ROWS, 256), F32)
     upper, x = call(
@@ -365,7 +425,7 @@
         [sums] + spare,
         int(5e8),
         int(1e6),
-        [SMEM] + [VMEM] * 5,
+        [VMEM] * 6,
         (VMEM, VMEM),
         {5: 1},
     )(jobs, above, s, t, rim, x)
@@ -376,7 +436,7 @@
         [sums, pltpu.VMEM((2, slab, e_dev), BF)] + spare + [dma((3,))],
         int(5e8),
         int(1e6),
-        [SMEM] + [VMEM] * 7,
+        [VMEM] * 8,
         (HBM, VMEM),
         {7: 1},
     )(jobs, below, s, t, rim, inner, upper, x)[0]

time: 31.4 us -> 30.7 us (0.978)
  the two profiles are of different devices: /device:TPU:408 before, /device:TPU:344 now
where the time goes in v4:
time: 30.7 us; the launch traced here: 30.5 us
  starting transfers between devices  13.6 us (44%)
  Pallas kernels  12.4 us (40%)
  waiting for transfers between devices  3.77 us (12%)
  between operations  0.74 us (2%)
    ppermute x2, starting transfers between devices, step_of(): lax.ppermute(value, axis, [(i, i + by) for i in range(count) if 0 <= i +...  6.8 us
    ppermute x2, starting transfers between devices, swap(): return lax.ppermute(value, axis, pairs + [(b, a) for a, b in pairs])  6.8 us
    pallas_call x1, Pallas kernels, per_device(): call(build_kernel, (shape((2 * SLOTS, ROWS, DEPTH), BF), shape((2, 256, D...  4.04 us
    pallas_call x1, Pallas kernels, per_device(): call(late_kernel, (shape(inner.shape, BF), shape(rim.shape, F32), shifted...  2.51 us
    ppermute x2, waiting for transfers between devices, step_of(): lax.ppermute(value, axis, [(i, i + by) for i in range(count) if 0 <= i +...  2 us
    ppermute x2, waiting for transfers between devices, swap(): return lax.ppermute(value, axis, pairs + [(b, a) for a, b in pairs])  1.77 us
    pallas_call x1, Pallas kernels, per_device(): call(rim_kernel, (payload, payload, shifted), [pltpu.VMEM((5, ROWS, 256),...  1.76 us
    pallas_call x1, Pallas kernels, per_device(): call(lower_kernel, (shape((atoms, slab, e_dev), BF), shifted), [sums, plt...  1.76 us
  transfers between devices with their start and end apart: 4, of which 2 were waited for; matrix products, arithmetic and copies ran while one was open for 0% of the time, Pallas kernels for 25%

profile of v4, /device:TPU:344, one launch (start us, length us, event | category | flops | bytes accessed | tf_op | source)
XLA Modules:
  0.0 30.5 jit_solution(5357394150571066198)
XLA Ops:
  0.0 1.2 %shard_map.64 = (bf16[4,200,128]{2,1,0:T(8,128)(2,1)S(1)}, bf16[4,200,128]{2,1,0:T(8,128)(2,1)S(1)}, bf16[8,200,128]{2,1,0:T(8,128)(2,1)S(1)}, bf16[16,800]{1,0:...) custom-call(bf16[8,200,128]{2,1,0:T(8,128)(2,1)} %g_hbm.1, bf16[16,800]{1,0:T(8,128)(2,1)} %coup_hbm.1, ...), custom_call_target="tpu_custom_call" | custom-call | flops 1000000 | bytes 1000000 | tf_op jit(solution)/shard_map/pallas_call | solution.py:345
  1.2 4.8 %collective-permute-start = (bf16[4,200,128]{2,1,0:T(8,128)(2,1)S(1)}, bf16[4,200,128]{2,1,0:T(8,128)(2,1)S(1)}, u32[]{:S(2)}, u32[]{:S(2)}) collective-permute-start(bf16[4,200,128]{2,1,0:T(8,128)(2,1)S(1)} %get-tuple-element.35), channel_id=1, source_target_pairs={{1,2},{3,4},{5,6},{7,8},{9,10},{11,12},{13,14},{2,1},{4,3},{6,5},{... | collective-permute-start | bytes 614408 | tf_op jit(solution)/shard_map/ppermute | solution.py:316
  6.1 2.0 %collective-permute-start.1 = (bf16[4,200,128]{2,1,0:T(8,128)(2,1)S(1)}, bf16[4,200,128]{2,1,0:T(8,128)(2,1)S(1)}, u32[]{:S(2)}, u32[]{:S(2)}) collective-permute-start(bf16[4,200,128]{2,1,0:T(8,128)(2,1)S(1)} %get-tuple-element.36), channel_id=1, source_target_pairs={{0,1},{2,3},{4,5},{6,7},{8,9},{10,11},{12,13},{14,15},{1,0},{3,2},... | collective-permute-start | bytes 614408 | tf_op jit(solution)/shard_map/ppermute | solution.py:316
  8.7 4.0 %shard_map.65 = (bf16[32,104,1024]{2,1,0:T(8,128)(2,1)S(1)}, bf16[2,256,1024]{2,1,0:T(8,128)(2,1)S(1)}, s32[196]{0:T(256)S(1)}, bf16[8,1024,256]{2,1,0:T(8,128)(2,1)S(1)}) custom-call(s32[1]{0:T(128)S(6)} %copy.23.cnt_ref, s32[2,16]{1,0:T(2,128)S(1)} %get-tuple-element.29.pairs_in, f32[8]{0:T(128)S(1)} %get-tuple-element.30.occ_in, ...), custom_call_target="tpu_custom_call" | custom-call | flops 3000000000 | bytes 8000000 | tf_op jit(solution)/shard_map/pallas_call | solution.py:358
  12.7 0.0 collective-permute-done.from_b
  12.7 1.8 %collective-permute-done.1.from_a = bf16[4,200,128]{2,1,0:T(8,128)(2,1)S(1)} collective-permute-done((bf16[4,200,128]{2,1,0:T(8,128)(2,1)S(1)}, bf16[4,200,128]{2,1,0:T(8,128)(2,1)S(1)}, u32[]{:S(2)}, u32[]{:S(2)}) %collective-permute-start.1) | collective-permute-done | bytes 204832 | tf_op jit(solution)/shard_map/ppermute | solution.py:316
  14.5 1.8 %shard_map.66 = (bf16[6,200,128]{2,1,0:T(8,128)(2,1)S(1)}, bf16[6,200,128]{2,1,0:T(8,128)(2,1)S(1)}, bf16[8,1024,256]{2,1,0:T(8,128)(2,1)S(1)}) custom-call(s32[196]{0:T(256)S(1)} %get-tuple-element.33.jobs_ref, bf16[8,200,128]{2,1,0:T(8,128)(2,1)S(1)} %get-tuple-element.34.g_ref, ...), custom_call_target="tpu_custom_call", output_to_operand_aliasing={{2}: (6, {})} | custom-call | flops 1000000000 | bytes 1000000 | tf_op jit(solution)/shard_map/pallas_call | solution.py:385
  16.3 1.9 %collective-permute-start.3 = (bf16[6,200,128]{2,1,0:T(8,128)(2,1)S(1)}, bf16[6,200,128]{2,1,0:T(8,128)(2,1)S(1)}, u32[]{:S(2)}, u32[]{:S(2)}) collective-permute-start(bf16[6,200,128]{2,1,0:T(8,128)(2,1)S(1)} %get-tuple-element.48), channel_id=1, source_target_pairs={{16,0},{32,16},{48,32},{64,48},{80,64},{96,80},{112,96},{128,112},... | collective-permute-start | bytes 921608 | tf_op jit(solution)/shard_map/ppermute | solution.py:321
  18.2 4.9 %collective-permute-start.2 = (bf16[6,200,128]{2,1,0:T(8,128)(2,1)S(1)}, bf16[6,200,128]{2,1,0:T(8,128)(2,1)S(1)}, u32[]{:S(2)}, u32[]{:S(2)}) collective-permute-start(bf16[6,200,128]{2,1,0:T(8,128)(2,1)S(1)} %get-tuple-element.42), channel_id=1, source_target_pairs={{0,16},{16,32},{32,48},{48,64},{64,80},{80,96},{96,112},{112,128},... | collective-permute-start | bytes 921608 | tf_op jit(solution)/shard_map/ppermute | solution.py:321
  23.1 2.5 %shard_map.68 = (bf16[4,200,128]{2,1,0:T(8,128)(2,1)S(1)}, f32[4,104,256]{2,1,0:T(8,128)S(1)}, bf16[8,1024,256]{2,1,0:T(8,128)(2,1)S(1)}) custom-call(s32[196]{0:T(256)S(1)} %get-tuple-element.33.jobs_ref, bf16[8,200,128]{2,1,0:T(8,128)(2,1)S(1)} %get-tuple-element.34.g_ref, ...), custom_call_target="tpu_custom_call", output_to_operand_aliasing={{0}: (7, {}), {1}: (8, {}), {2}: (6, {})} | custom-call | flops 3000000000 | bytes 1000000 | tf_op jit(solution)/shard_map/pallas_call | solution.py:410
  25.6 0.0 collective-permute-done.3.got_ref
  25.6 1.1 %shard_map.69 = (bf16[2,200,128]{2,1,0:T(8,128)(2,1)S(1)}, bf16[8,1024,256]{2,1,0:T(8,128)(2,1)S(1)}) custom-call(s32[196]{0:T(256)S(1)} %get-tuple-element.33.jobs_ref, bf16[6,200,128]{2,1,0:T(8,128)(2,1)S(1)} %collective-permute-done.3.got_ref, bf16[2,256,1024]{2,1,0:T(8,128)(2,1)S(1)} %get-tuple-element.37.s_ref, ...), custom_call_target="tpu_custom_call", output_to_operand_aliasing={{1}: (5, {})} | custom-call | flops 500000000 | bytes 1000000 | tf_op jit(solution)/shard_map/pallas_call | solution.py:422
  26.8 2.0 %collective-permute-done.2.got_ref = bf16[6,200,128]{2,1,0:T(8,128)(2,1)S(1)} collective-permute-done((bf16[6,200,128]{2,1,0:T(8,128)(2,1)S(1)}, bf16[6,200,128]{2,1,0:T(8,128)(2,1)S(1)}, u32[]{:S(2)}, u32[]{:S(2)}) %collective-permute-start.2) | collective-permute-done | bytes 307232 | tf_op jit(solution)/shard_map/ppermute | solution.py:321
  28.8 1.8 %shard_map.70 = (bf16[8,200,128]{2,1,0:T(8,128)(2,1)}, bf16[8,1024,256]{2,1,0:T(8,128)(2,1)S(1)}) custom-call(s32[196]{0:T(256)S(1)} %get-tuple-element.33.jobs_ref, bf16[6,200,128]{2,1,0:T(8,128)(2,1)S(1)} %collective-permute-done.2.got_ref, bf16[2,256,1024]{2,1,0:T(8,128)(2,1)S(1)} %get-tuple-element.37.s_ref, ...), custom_call_target="tpu_custom_call", output_to_operand_aliasing={{1}: (7, {})} | custom-call | flops 500000000 | bytes 1000000 | tf_op jit(solution)/shard_map/pallas_call | solution.py:433
  (1 shorter events, 0.0 us)
Async XLA Ops:
  1.2 11.5 %collective-permute-start = (bf16[4,200,128]{2,1,0:T(8,128)(2,1)S(1)}, bf16[4,200,128]{2,1,0:T(8,128)(2,1)S(1)}, u32[]{:S(2)}, u32[]{:S(2)}) collective-permute-start(bf16[4,200,128]{2,1,0:T(8,128)(2,1)S(1)} %get-tuple-element.35), channel_id=1, source_target_pairs={{1,2},{3,4},{5,6},{7,8},{9,10},{11,12},{13,14},{2,1},{4,3},{6,5},{... | collective-permute-start | bytes 614408 | tf_op jit(solution)/shard_map/ppermute | solution.py:316
  6.1 8.4 %collective-permute-start.1 = (bf16[4,200,128]{2,1,0:T(8,128)(2,1)S(1)}, bf16[4,200,128]{2,1,0:T(8,128)(2,1)S(1)}, u32[]{:S(2)}, u32[]{:S(2)}) collective-permute-start(bf16[4,200,128]{2,1,0:T(8,128)(2,1)S(1)} %get-tuple-element.36), channel_id=1, source_target_pairs={{0,1},{2,3},{4,5},{6,7},{8,9},{10,11},{12,13},{14,15},{1,0},{3,2},... | collective-permute-start | bytes 614408 | tf_op jit(solution)/shard_map/ppermute | solution.py:316
  16.3 9.4 %collective-permute-start.3 = (bf16[6,200,128]{2,1,0:T(8,128)(2,1)S(1)}, bf16[6,200,128]{2,1,0:T(8,128)(2,1)S(1)}, u32[]{:S(2)}, u32[]{:S(2)}) collective-permute-start(bf16[6,200,128]{2,1,0:T(8,128)(2,1)S(1)} %get-tuple-element.48), channel_id=1, source_target_pairs={{16,0},{32,16},{48,32},{64,48},{80,64},{96,80},{112,96},{128,112},... | collective-permute-start | bytes 921608 | tf_op jit(solution)/shard_map/ppermute | solution.py:321
  18.2 10.5 %collective-permute-start.2 = (bf16[6,200,128]{2,1,0:T(8,128)(2,1)S(1)}, bf16[6,200,128]{2,1,0:T(8,128)(2,1)S(1)}, u32[]{:S(2)}, u32[]{:S(2)}) collective-permute-start(bf16[6,200,128]{2,1,0:T(8,128)(2,1)S(1)} %get-tuple-element.42), channel_id=1, source_target_pairs={{0,16},{16,32},{32,48},{48,64},{64,80},{80,96},{96,112},{112,128},... | collective-permute-start | bytes 921608 | tf_op jit(solution)/shard_map/ppermute | solution.py:321

commit v5 on v4

--- a/solution.py
+++ b/solution.py
@@ -233,24 +233,36 @@
 
 
 def rim_kernel(
-    jobs_ref, g_ref, from_b, from_a, s_ref, t_ref, x_old, down_ref, up_ref, x, part, lhs, low, rows, held, sem
+    jobs_ref, g_ref, from_b, from_a, s_ref, t_ref, x_old, cross_ref, near_ref, x, part, lhs, low, rows, held, sem
 ):
     lists = Lists(jobs_ref, held, sem)
+    halos = []
     for at, atom in enumerate((0, 1, 6, 7)):
-        ref = up_ref if atom >= 6 else down_ref
-        halo = halo_of(from_a, from_b, atom)
-        ref[at % 2] = g_ref[atom]
-        ref[2 + at % 2] = halo
-        shift_atom(g_ref[atom], halo, s_ref, atom // 4, lhs.at[at], low.at[at], store_in(x, atom))
+        halos.append(halo_of(from_a, from_b, atom))
+        shift_atom(g_ref[atom], halos[at], s_ref, atom // 4, lhs.at[at], low.at[at], store_in(x, atom))
     part[...] = jnp.zeros(part.shape, F32)
     run_jobs(lists.ready(), 1, 4, t_ref, x, part)
-    for at in range(4):
-        ref = up_ref if at >= 2 else down_ref
-        ref[4 + at % 2] = unfold(part[at], rows.at[at]).astype(BF)
+    odd = lax.axis_index("atom") % 2
+
+    def fill(ref, side):
+        for j in range(2):
+            ref[j] = g_ref[6 * side + j]
+            ref[2 + j] = halos[2 * side + j]
+            ref[4 + j] = unfold(part[2 * side + j], rows.at[2 * side + j]).astype(BF)
+
+    @pl.when(odd == 1)
+    def _():
+        fill(cross_ref, 1)
+        fill(near_ref, 0)
+
+    @pl.when(odd == 0)
+    def _():
+        fill(cross_ref, 0)
+        fill(near_ref, 1)
 
 
 def early_kernel(
-    jobs_ref, g_ref, from_b, from_a, s_ref, t_ref, x_old, up_old, inner_ref, rim_ref, x, up_ref, acc, lhs, low, rows, held, sem
+    jobs_ref, g_ref, from_b, from_a, s_ref, t_ref, x_old, cross_old, inner_ref, rim_ref, x, cross_ref, acc, lhs, low, rows, held, sem
 ):
     @pl.when(lax.axis_index("atom") % 2 == 1)
     def _():
@@ -259,7 +271,7 @@
 
 
 def late_kernel(
-    jobs_ref, g_ref, from_b, from_a, s_ref, t_ref, x_old, inner_old, rim_old, inner_ref, rim_ref, x, acc, lhs, low, rows, held, sem
+    jobs_ref, g_ref, from_b, from_a, s_ref, t_ref, x_old, inner_old, rim_old, near_old, inner_ref, rim_ref, x, near_ref, acc, lhs, low, rows, held, sem
 ):
     @pl.when(lax.axis_index("atom") % 2 == 0)
     def _():
@@ -278,34 +290,29 @@
         rim_ref[j] = acc[j if j < 2 else j + 4]
 
 
-def upper_kernel(jobs_ref, got_ref, s_ref, t_ref, rim_ref, x_old, out_ref, x, acc, lhs, low, rows, held, sem):
-    lists = Lists(jobs_ref, held, sem)
-    for j in range(2):
-        shift_atom(got_ref[j], got_ref[2 + j], s_ref, 0, lhs.at[j], low.at[j], store_in(x, 2 + j))
-    acc[0:2] = rim_ref[2:4]
-    run_jobs(lists.ready(), 3, 4, t_ref, x, acc)
-    for j in range(2):
-        out_ref[j] = (unfold(acc[j], rows.at[j]) + got_ref[4 + j].astype(F32)).astype(BF)
-
-
-def lower_kernel(
-    jobs_ref, got_ref, s_ref, t_ref, rim_ref, inner_ref, upper_ref, x_old, out_ref, x, acc, done, lhs, low, rows, held, sem, sems
+def final_kernel(
+    jobs_ref, cross_ref, near_ref, s_ref, t_ref, rim_ref, inner_ref, x_old, out_ref, x, acc, done, lhs, low, rows, held, sem, sems
 ):
     lists = Lists(jobs_ref, held, sem)
-    copies = [
-        pltpu.make_async_copy(inner_ref, out_ref.at[2:6], sems.at[0]),
-        pltpu.make_async_copy(upper_ref, out_ref.at[6:8], sems.at[1]),
-        pltpu.make_async_copy(done, out_ref.at[0:2], sems.at[2]),
-    ]
-    copies[0].start()
-    copies[1].start()
-    for j in range(2):
-        shift_atom(got_ref[j], got_ref[2 + j], s_ref, 1, lhs.at[j], low.at[j], store_in(x, j))
-    acc[0:2] = rim_ref[0:2]
-    run_jobs(lists.ready(), 2, 4, t_ref, x, acc)
-    for j in range(2):
-        done[j] = (unfold(acc[j], rows.at[j]) + got_ref[4 + j].astype(F32)).astype(BF)
-    copies[2].start()
+    odd = lax.axis_index("atom") % 2
+    early = pltpu.make_async_copy(inner_ref, out_ref.at[2:6], sems.at[0])
+    early.start()
+    sides = ((1 - odd, near_ref), (odd, cross_ref))
+    for n, (side, ref) in enumerate(sides):
+        for j in range(2):
+            at = 2 * n + j
+            shift_atom(ref[j], ref[2 + j], s_ref, 1 - side, lhs.at[at], low.at[at], store_in(x, 2 * side + j))
+            acc[3 * n + j] = rim_ref[2 * side + j]
+    held = lists.ready()
+    copies = [early]
+    for n, (side, ref) in enumerate(sides):
+        run_jobs(held, 2 + side, 4, t_ref, x, acc.at[pl.ds(3 * n, 3)])
+        for j in range(2):
+            at = 2 * n + j
+            done[at] = (unfold(acc[3 * n + j], rows.at[at]) + ref[4 + j].astype(F32)).astype(BF)
+        copy = pltpu.make_async_copy(done.at[pl.ds(2 * n, 2)], out_ref.at[pl.ds(6 * side, 2)], sems.at[1 + n])
+        copy.start()
+        copies.append(copy)
     for copy in copies:
         copy.wait()
 
@@ -314,11 +321,6 @@
     count = lax.axis_size(axis)
     pairs = [(i, i + 1) for i in range(start, count - 1, 2)]
     return lax.ppermute(value, axis, pairs + [(b, a) for a, b in pairs])
-
-
-def step_of(value, axis, by):
-    count = lax.axis_size(axis)
-    return lax.ppermute(value, axis, [(i, i + by) for i in range(count) if 0 <= i + by < count])
 
 
 def call(kernel, outs, scratch, flops, moved, specs, out_specs, aliases={}):
@@ -382,7 +384,7 @@
         dma(()),
     ]
     payload = shape((6, slab, e_dev), BF)
-    down, up, x = call(
+    cross, near, x = call(
         rim_kernel,
         (payload, payload, shifted),
         [pltpu.VMEM((5, ROWS, 256), F32)] + spare,
@@ -392,11 +394,10 @@
         (VMEM, VMEM, VMEM),
         {6: 2},
     )(jobs, g, from_b, from_a, s, t, x)
-    above = step_of(down, "atom", -1)
     inner = shape((4, slab, e_dev), BF)
     rim = shape((4, ROWS, 256), F32)
     sums = pltpu.VMEM((9, ROWS, 256), F32)
-    inner, rim, x, up = call(
+    inner, rim, x, cross = call(
         early_kernel,
         (inner, rim, shifted, payload),
         [sums] + spare,
@@ -405,41 +406,30 @@
         [VMEM] * 8,
         (VMEM,) * 4,
         {6: 2, 7: 3},
-    )(jobs, g, from_b, from_a, s, t, x, up)
-    below = step_of(up, "atom", 1)
-    inner, rim, x = call(
+    )(jobs, g, from_b, from_a, s, t, x, cross)
+    cross = swap(cross, "atom", 1)
+    inner, rim, x, near = call(
         late_kernel,
-        (shape(inner.shape, BF), shape(rim.shape, F32), shifted),
+        (shape(inner.shape, BF), shape(rim.shape, F32), shifted, payload),
         [sums] + spare,
         int(3e9),
         int(1e6),
-        [VMEM] * 9,
-        (VMEM,) * 3,
-        {7: 0, 8: 1, 6: 2},
-    )(jobs, g, from_b, from_a, s, t, x, inner, rim)
-
-    sums = pltpu.VMEM((3, ROWS, 256), F32)
-    upper, x = call(
-        upper_kernel,
-        (shape((2, slab, e_dev), BF), shifted),
-        [sums] + spare,
-        int(5e8),
-        int(1e6),
-        [VMEM] * 6,
-        (VMEM, VMEM),
-        {5: 1},
-    )(jobs, above, s, t, rim, x)
+        [VMEM] * 10,
+        (VMEM,) * 4,
+        {7: 0, 8: 1, 6: 2, 9: 3},
+    )(jobs, g, from_b, from_a, s, t, x, inner, rim, near)
+    near = swap(near, "atom", 0)
 
     return call(
-        lower_kernel,
+        final_kernel,
         (shape((atoms, slab, e_dev), BF), shifted),
-        [sums, pltpu.VMEM((2, slab, e_dev), BF)] + spare + [dma((3,))],
-        int(5e8),
+        [pltpu.VMEM((6, ROWS, 256), F32), pltpu.VMEM((4, slab, e_dev), BF)] + spare + [dma((3,))],
+        int(1e9),
         int(1e6),
         [VMEM] * 8,
         (HBM, VMEM),
         {7: 1},
-    )(jobs, below, s, t, rim, inner, upper, x)[0]
+    )(jobs, cross, near, s, t, rim, inner, x)[0]
 
 
 def solution(mesh):

time: 30.7 us -> 30.8 us (level)
  the two profiles are of different devices: /device:TPU:344 before, /device:TPU:249 now
where the time goes in v5:
time: 30.8 us; the launch traced here: 30.6 us
  Pallas kernels  13.3 us (43%)
  starting transfers between devices  13 us (42%)
  waiting for transfers between devices  3.55 us (12%)
  between operations  0.73 us (2%)
    ppermute x4, starting transfers between devices, swap(): return lax.ppermute(value, axis, pairs + [(b, a) for a, b in pairs])  13 us
    pallas_call x1, Pallas kernels, per_device(): call(build_kernel, (shape((2 * SLOTS, ROWS, DEPTH), BF), shape((2, 256, D...  4.2 us
    ppermute x4, waiting for transfers between devices, swap(): return lax.ppermute(value, axis, pairs + [(b, a) for a, b in pairs])  3.55 us
    pallas_call x1, Pallas kernels, per_device(): call(final_kernel, (shape((atoms, slab, e_dev), BF), shifted), [pltpu.VME...  3.02 us
    pallas_call x1, Pallas kernels, per_device(): call(early_kernel, (inner, rim, shifted, payload), [sums] + spare, int(30...  2.51 us
    pallas_call x1, Pallas kernels, per_device(): call(rim_kernel, (payload, payload, shifted), [pltpu.VMEM((5, ROWS, 256),...  2.34 us
    pallas_call x1, Pallas kernels, per_device(): call(pack_kernel, (half, half) + tuple((shape(v.shape, v.dtype) for v in...  1.2 us
  transfers between devices with their start and end apart: 4, of which 2 were waited for; matrix products, arithmetic and copies ran while one was open for 0% of the time, Pallas kernels for 14%

profile of v5, /device:TPU:249, one launch (start us, length us, event | category | flops | bytes accessed | tf_op | source)
XLA Modules:
  0.0 30.6 jit_solution(2699118390960188536)
XLA Ops:
  0.0 1.2 %shard_map.64 = (bf16[4,200,128]{2,1,0:T(8,128)(2,1)S(1)}, bf16[4,200,128]{2,1,0:T(8,128)(2,1)S(1)}, bf16[8,200,128]{2,1,0:T(8,128)(2,1)S(1)}, bf16[16,800]{1,0:...) custom-call(bf16[8,200,128]{2,1,0:T(8,128)(2,1)} %g_hbm.1, bf16[16,800]{1,0:T(8,128)(2,1)} %coup_hbm.1, ...), custom_call_target="tpu_custom_call" | custom-call | flops 1000000 | bytes 1000000 | tf_op jit(solution)/shard_map/pallas_call | solution.py:347
  1.2 4.6 %collective-permute-start = (bf16[4,200,128]{2,1,0:T(8,128)(2,1)S(1)}, bf16[4,200,128]{2,1,0:T(8,128)(2,1)S(1)}, u32[]{:S(2)}, u32[]{:S(2)}) collective-permute-start(bf16[4,200,128]{2,1,0:T(8,128)(2,1)S(1)} %get-tuple-element.34), channel_id=1, source_target_pairs={{1,2},{3,4},{5,6},{7,8},{9,10},{11,12},{13,14},{2,1},{4,3},{6,5},{... | collective-permute-start | bytes 614408 | tf_op jit(solution)/shard_map/ppermute | solution.py:323
  5.8 1.9 %collective-permute-start.1 = (bf16[4,200,128]{2,1,0:T(8,128)(2,1)S(1)}, bf16[4,200,128]{2,1,0:T(8,128)(2,1)S(1)}, u32[]{:S(2)}, u32[]{:S(2)}) collective-permute-start(bf16[4,200,128]{2,1,0:T(8,128)(2,1)S(1)} %get-tuple-element.35), channel_id=1, source_target_pairs={{0,1},{2,3},{4,5},{6,7},{8,9},{10,11},{12,13},{14,15},{1,0},{3,2},... | collective-permute-start | bytes 614408 | tf_op jit(solution)/shard_map/ppermute | solution.py:323
  8.4 4.2 %shard_map.65 = (bf16[32,104,1024]{2,1,0:T(8,128)(2,1)S(1)}, bf16[2,256,1024]{2,1,0:T(8,128)(2,1)S(1)}, s32[196]{0:T(256)S(1)}, bf16[8,1024,256]{2,1,0:T(8,128)(2,1)S(1)}) custom-call(s32[1]{0:T(128)S(6)} %copy.23.cnt_ref, s32[2,16]{1,0:T(2,128)S(1)} %get-tuple-element.28.pairs_in, f32[8]{0:T(128)S(1)} %get-tuple-element.29.occ_in, ...), custom_call_target="tpu_custom_call" | custom-call | flops 3000000000 | bytes 8000000 | tf_op jit(solution)/shard_map/pallas_call | solution.py:360
  12.6 0.0 collective-permute-done.from_b
  12.6 0.7 %collective-permute-done.1.from_a = bf16[4,200,128]{2,1,0:T(8,128)(2,1)S(1)} collective-permute-done((bf16[4,200,128]{2,1,0:T(8,128)(2,1)S(1)}, bf16[4,200,128]{2,1,0:T(8,128)(2,1)S(1)}, u32[]{:S(2)}, u32[]{:S(2)}) %collective-permute-start.1) | collective-permute-done | bytes 204832 | tf_op jit(solution)/shard_map/ppermute | solution.py:323
  13.3 2.3 %shard_map.66 = (bf16[6,200,128]{2,1,0:T(8,128)(2,1)S(1)}, bf16[6,200,128]{2,1,0:T(8,128)(2,1)S(1)}, bf16[8,1024,256]{2,1,0:T(8,128)(2,1)S(1)}) custom-call(s32[196]{0:T(256)S(1)} %get-tuple-element.32.jobs_ref, bf16[8,200,128]{2,1,0:T(8,128)(2,1)S(1)} %get-tuple-element.33.g_ref, ...), custom_call_target="tpu_custom_call", output_to_operand_aliasing={{2}: (6, {})} | custom-call | flops 1000000000 | bytes 1000000 | tf_op jit(solution)/shard_map/pallas_call | solution.py:387
  15.7 2.5 %shard_map.67 = (bf16[4,200,128]{2,1,0:T(8,128)(2,1)S(1)}, f32[4,104,256]{2,1,0:T(8,128)S(1)}, bf16[8,1024,256]{2,1,0:T(8,128)(2,1)S(1)}, bf16[6,200,128]{2,1,0:T(8,128)(2,1)S(1)}) custom-call(s32[196]{0:T(256)S(1)} %get-tuple-element.32.jobs_ref, bf16[8,200,128]{2,1,0:T(8,128)(2,1)S(1)} %get-tuple-element.33.g_ref, ...), custom_call_target="tpu_custom_call", output_to_operand_aliasing={{2}: (6, {}), {3}: (7, {})} | custom-call | flops 3000000000 | bytes 1000000 | tf_op jit(solution)/shard_map/pallas_call | solution.py:400
  18.2 3.5 %collective-permute-start.2 = (bf16[6,200,128]{2,1,0:T(8,128)(2,1)S(1)}, bf16[6,200,128]{2,1,0:T(8,128)(2,1)S(1)}, u32[]{:S(2)}, u32[]{:S(2)}) collective-permute-start(bf16[6,200,128]{2,1,0:T(8,128)(2,1)S(1)} %get-tuple-element.41), channel_id=1, source_target_pairs={{16,32},{48,64},{80,96},{112,128},{144,160},{176,192},{208,224},{2... | collective-permute-start | bytes 921608 | tf_op jit(solution)/shard_map/ppermute | solution.py:323
  21.7 3.0 %collective-permute-start.3 = (bf16[6,200,128]{2,1,0:T(8,128)(2,1)S(1)}, bf16[6,200,128]{2,1,0:T(8,128)(2,1)S(1)}, u32[]{:S(2)}, u32[]{:S(2)}) collective-permute-start(bf16[6,200,128]{2,1,0:T(8,128)(2,1)S(1)} %get-tuple-element.46), channel_id=1, source_target_pairs={{0,16},{32,48},{64,80},{96,112},{128,144},{160,176},{192,208},{224... | collective-permute-start | bytes 921608 | tf_op jit(solution)/shard_map/ppermute | solution.py:323
  24.7 2.8 %collective-permute-done.2.cross_ref = bf16[6,200,128]{2,1,0:T(8,128)(2,1)S(1)} collective-permute-done((bf16[6,200,128]{2,1,0:T(8,128)(2,1)S(1)}, bf16[6,200,128]{2,1,0:T(8,128)(2,1)S(1)}, u32[]{:S(2)}, u32[]{:S(2)}) %collective-permute-start.2) | collective-permute-done | bytes 307232 | tf_op jit(solution)/shard_map/ppermute | solution.py:323
  27.6 0.0 collective-permute-done.3.near_ref
  27.6 3.0 %shard_map.69 = (bf16[8,200,128]{2,1,0:T(8,128)(2,1)}, bf16[8,1024,256]{2,1,0:T(8,128)(2,1)S(1)}) custom-call(s32[196]{0:T(256)S(1)} %get-tuple-element.32.jobs_ref, bf16[6,200,128]{2,1,0:T(8,128)(2,1)S(1)} %collective-permute-done.2.cross_ref, bf16[6,200,128]{2,1,0:T(8,128)(2,1)S(1)} %collective-permute-done.3.near_ref, ...), custom_call_target="tpu_custom_call", output_to_operand_aliasing={{1}: (7, {})} | custom-call | flops 1000000000 | bytes 1000000 | tf_op jit(solution)/shard_map/pallas_call | solution.py:423
  (1 shorter events, 0.0 us)
Async XLA Ops:
  1.2 11.4 %collective-permute-start = (bf16[4,200,128]{2,1,0:T(8,128)(2,1)S(1)}, bf16[4,200,128]{2,1,0:T(8,128)(2,1)S(1)}, u32[]{:S(2)}, u32[]{:S(2)}) collective-permute-start(bf16[4,200,128]{2,1,0:T(8,128)(2,1)S(1)} %get-tuple-element.34), channel_id=1, source_target_pairs={{1,2},{3,4},{5,6},{7,8},{9,10},{11,12},{13,14},{2,1},{4,3},{6,5},{... | collective-permute-start | bytes 614408 | tf_op jit(solution)/shard_map/ppermute | solution.py:323
  5.8 7.5 %collective-permute-start.1 = (bf16[4,200,128]{2,1,0:T(8,128)(2,1)S(1)}, bf16[4,200,128]{2,1,0:T(8,128)(2,1)S(1)}, u32[]{:S(2)}, u32[]{:S(2)}) collective-permute-start(bf16[4,200,128]{2,1,0:T(8,128)(2,1)S(1)} %get-tuple-element.35), channel_id=1, source_target_pairs={{0,1},{2,3},{4,5},{6,7},{8,9},{10,11},{12,13},{14,15},{1,0},{3,2},... | collective-permute-start | bytes 614408 | tf_op jit(solution)/shard_map/ppermute | solution.py:323
  18.2 9.4 %collective-permute-start.2 = (bf16[6,200,128]{2,1,0:T(8,128)(2,1)S(1)}, bf16[6,200,128]{2,1,0:T(8,128)(2,1)S(1)}, u32[]{:S(2)}, u32[]{:S(2)}) collective-permute-start(bf16[6,200,128]{2,1,0:T(8,128)(2,1)S(1)} %get-tuple-element.41), channel_id=1, source_target_pairs={{16,32},{48,64},{80,96},{112,128},{144,160},{176,192},{208,224},{2... | collective-permute-start | bytes 921608 | tf_op jit(solution)/shard_map/ppermute | solution.py:323
  21.7 5.8 %collective-permute-start.3 = (bf16[6,200,128]{2,1,0:T(8,128)(2,1)S(1)}, bf16[6,200,128]{2,1,0:T(8,128)(2,1)S(1)}, u32[]{:S(2)}, u32[]{:S(2)}) collective-permute-start(bf16[6,200,128]{2,1,0:T(8,128)(2,1)S(1)} %get-tuple-element.46), channel_id=1, source_target_pairs={{0,16},{32,48},{64,80},{96,112},{128,144},{160,176},{192,208},{224... | collective-permute-start | bytes 921608 | tf_op jit(solution)/shard_map/ppermute | solution.py:323

commit v6 on v5

--- a/solution.py
+++ b/solution.py
@@ -261,25 +261,10 @@
         fill(near_ref, 1)
 
 
-def early_kernel(
-    jobs_ref, g_ref, from_b, from_a, s_ref, t_ref, x_old, cross_old, inner_ref, rim_ref, x, cross_ref, acc, lhs, low, rows, held, sem
+def local_kernel(
+    jobs_ref, g_ref, from_b, from_a, s_ref, t_ref, x_old, inner_ref, rim_ref, x, acc, lhs, low, rows, held, sem
 ):
-    @pl.when(lax.axis_index("atom") % 2 == 1)
-    def _():
-        lists = Lists(jobs_ref, held, sem)
-        local_terms(lists, g_ref, from_b, from_a, s_ref, t_ref, inner_ref, rim_ref, x, acc, lhs, low, rows)
-
-
-def late_kernel(
-    jobs_ref, g_ref, from_b, from_a, s_ref, t_ref, x_old, inner_old, rim_old, near_old, inner_ref, rim_ref, x, near_ref, acc, lhs, low, rows, held, sem
-):
-    @pl.when(lax.axis_index("atom") % 2 == 0)
-    def _():
-        lists = Lists(jobs_ref, held, sem)
-        local_terms(lists, g_ref, from_b, from_a, s_ref, t_ref, inner_ref, rim_ref, x, acc, lhs, low, rows)
-
-
-def local_terms(lists, g_ref, from_b, from_a, s_ref, t_ref, inner_ref, rim_ref, x, acc, lhs, low, rows):
+    lists = Lists(jobs_ref, held, sem)
     for at, atom in enumerate((2, 3, 4, 5)):
         halo = halo_of(from_a, from_b, atom)
         shift_atom(g_ref[atom], halo, s_ref, atom // 4, lhs.at[at], low.at[at], store_in(x, atom))
@@ -394,31 +379,18 @@
         (VMEM, VMEM, VMEM),
         {6: 2},
     )(jobs, g, from_b, from_a, s, t, x)
-    inner = shape((4, slab, e_dev), BF)
-    rim = shape((4, ROWS, 256), F32)
-    sums = pltpu.VMEM((9, ROWS, 256), F32)
-    inner, rim, x, cross = call(
-        early_kernel,
-        (inner, rim, shifted, payload),
-        [sums] + spare,
+    cross = swap(cross, "atom", 1)
+    near = swap(near, "atom", 0)
+    inner, rim, x = call(
+        local_kernel,
+        (shape((4, slab, e_dev), BF), shape((4, ROWS, 256), F32), shifted),
+        [pltpu.VMEM((9, ROWS, 256), F32)] + spare,
         int(3e9),
         int(1e6),
-        [VMEM] * 8,
-        (VMEM,) * 4,
-        {6: 2, 7: 3},
-    )(jobs, g, from_b, from_a, s, t, x, cross)
-    cross = swap(cross, "atom", 1)
-    inner, rim, x, near = call(
-        late_kernel,
-        (shape(inner.shape, BF), shape(rim.shape, F32), shifted, payload),
-        [sums] + spare,
-        int(3e9),
-        int(1e6),
-        [VMEM] * 10,
-        (VMEM,) * 4,
-        {7: 0, 8: 1, 6: 2, 9: 3},
-    )(jobs, g, from_b, from_a, s, t, x, inner, rim, near)
-    near = swap(near, "atom", 0)
+        [VMEM] * 7,
+        (VMEM,) * 3,
+        {6: 2},
+    )(jobs, g, from_b, from_a, s, t, x)
 
     return call(
         final_kernel,

time: 30.8 us -> 29.9 us (0.971)
  the two profiles are of different devices: /device:TPU:249 before, /device:TPU:121 now
where the time goes in v6:
time: 29.9 us; the launch traced here: 29.7 us
  starting transfers between devices  14.4 us (48%)
  Pallas kernels  13 us (43%)
  waiting for transfers between devices  1.53 us (5%)
  between operations  0.72 us (2%)
    ppermute x4, starting transfers between devices, swap(): return lax.ppermute(value, axis, pairs + [(b, a) for a, b in pairs])  14.4 us
    pallas_call x1, Pallas kernels, per_device(): call(build_kernel, (shape((2 * SLOTS, ROWS, DEPTH), BF), shape((2, 256, D...  4.37 us
    pallas_call x1, Pallas kernels, per_device(): call(final_kernel, (shape((atoms, slab, e_dev), BF), shifted), [pltpu.VME...  3.49 us
    pallas_call x1, Pallas kernels, per_device(): call(rim_kernel, (payload, payload, shifted), [pltpu.VMEM((5, ROWS, 256),...  2.29 us
    pallas_call x1, Pallas kernels, per_device(): call(local_kernel, (shape((4, slab, e_dev), BF), shape((4, ROWS, 256), F3...  1.62 us
    ppermute x4, waiting for transfers between devices, swap(): return lax.ppermute(value, axis, pairs + [(b, a) for a, b in pairs])  1.53 us
    pallas_call x1, Pallas kernels, per_device(): call(pack_kernel, (half, half) + tuple((shape(v.shape, v.dtype) for v in...  1.2 us
  transfers between devices with their start and end apart: 4, of which 2 were waited for; matrix products, arithmetic and copies ran while one was open for 0% of the time, Pallas kernels for 20%

profile of v6, /device:TPU:121, one launch (start us, length us, event | category | flops | bytes accessed | tf_op | source)
XLA Modules:
  0.0 29.7 jit_solution(16909682476400412117)
XLA Ops:
  0.0 1.2 %shard_map.64 = (bf16[4,200,128]{2,1,0:T(8,128)(2,1)S(1)}, bf16[4,200,128]{2,1,0:T(8,128)(2,1)S(1)}, bf16[8,200,128]{2,1,0:T(8,128)(2,1)S(1)}, bf16[16,800]{1,0:...) custom-call(bf16[8,200,128]{2,1,0:T(8,128)(2,1)} %g_hbm.1, bf16[16,800]{1,0:T(8,128)(2,1)} %coup_hbm.1, ...), custom_call_target="tpu_custom_call" | custom-call | flops 1000000 | bytes 1000000 | tf_op jit(solution)/shard_map/pallas_call | solution.py:332
  1.2 4.6 %collective-permute-start = (bf16[4,200,128]{2,1,0:T(8,128)(2,1)S(1)}, bf16[4,200,128]{2,1,0:T(8,128)(2,1)S(1)}, u32[]{:S(2)}, u32[]{:S(2)}) collective-permute-start(bf16[4,200,128]{2,1,0:T(8,128)(2,1)S(1)} %get-tuple-element.29), channel_id=1, source_target_pairs={{1,2},{3,4},{5,6},{7,8},{9,10},{11,12},{13,14},{2,1},{4,3},{6,5},{... | collective-permute-start | bytes 614408 | tf_op jit(solution)/shard_map/ppermute | solution.py:308
  5.8 1.9 %collective-permute-start.1 = (bf16[4,200,128]{2,1,0:T(8,128)(2,1)S(1)}, bf16[4,200,128]{2,1,0:T(8,128)(2,1)S(1)}, u32[]{:S(2)}, u32[]{:S(2)}) collective-permute-start(bf16[4,200,128]{2,1,0:T(8,128)(2,1)S(1)} %get-tuple-element.30), channel_id=1, source_target_pairs={{0,1},{2,3},{4,5},{6,7},{8,9},{10,11},{12,13},{14,15},{1,0},{3,2},... | collective-permute-start | bytes 614408 | tf_op jit(solution)/shard_map/ppermute | solution.py:308
  8.4 4.4 %shard_map.65 = (bf16[32,104,1024]{2,1,0:T(8,128)(2,1)S(1)}, bf16[2,256,1024]{2,1,0:T(8,128)(2,1)S(1)}, s32[196]{0:T(256)S(1)}, bf16[8,1024,256]{2,1,0:T(8,128)(2,1)S(1)}) custom-call(s32[1]{0:T(128)S(6)} %copy.13.cnt_ref, s32[2,16]{1,0:T(2,128)S(1)} %get-tuple-element.23.pairs_in, f32[8]{0:T(128)S(1)} %get-tuple-element.24.occ_in, ...), custom_call_target="tpu_custom_call" | custom-call | flops 3000000000 | bytes 8000000 | tf_op jit(solution)/shard_map/pallas_call | solution.py:345
  12.7 0.0 collective-permute-done.from_b
  12.7 0.6 %collective-permute-done.1.from_a = bf16[4,200,128]{2,1,0:T(8,128)(2,1)S(1)} collective-permute-done((bf16[4,200,128]{2,1,0:T(8,128)(2,1)S(1)}, bf16[4,200,128]{2,1,0:T(8,128)(2,1)S(1)}, u32[]{:S(2)}, u32[]{:S(2)}) %collective-permute-start.1) | collective-permute-done | bytes 204832 | tf_op jit(solution)/shard_map/ppermute | solution.py:308
  13.3 2.3 %shard_map.66 = (bf16[6,200,128]{2,1,0:T(8,128)(2,1)S(1)}, bf16[6,200,128]{2,1,0:T(8,128)(2,1)S(1)}, bf16[8,1024,256]{2,1,0:T(8,128)(2,1)S(1)}) custom-call(s32[196]{0:T(256)S(1)} %get-tuple-element.27.jobs_ref, bf16[8,200,128]{2,1,0:T(8,128)(2,1)S(1)} %get-tuple-element.28.g_ref, ...), custom_call_target="tpu_custom_call", output_to_operand_aliasing={{2}: (6, {})} | custom-call | flops 1000000000 | bytes 1000000 | tf_op jit(solution)/shard_map/pallas_call | solution.py:372
  15.6 6.0 %collective-permute-start.2 = (bf16[6,200,128]{2,1,0:T(8,128)(2,1)S(1)}, bf16[6,200,128]{2,1,0:T(8,128)(2,1)S(1)}, u32[]{:S(2)}, u32[]{:S(2)}) collective-permute-start(bf16[6,200,128]{2,1,0:T(8,128)(2,1)S(1)} %get-tuple-element.34), channel_id=1, source_target_pairs={{16,32},{48,64},{80,96},{112,128},{144,160},{176,192},{208,224},{2... | collective-permute-start | bytes 921608 | tf_op jit(solution)/shard_map/ppermute | solution.py:308
  21.6 1.9 %collective-permute-start.3 = (bf16[6,200,128]{2,1,0:T(8,128)(2,1)S(1)}, bf16[6,200,128]{2,1,0:T(8,128)(2,1)S(1)}, u32[]{:S(2)}, u32[]{:S(2)}) collective-permute-start(bf16[6,200,128]{2,1,0:T(8,128)(2,1)S(1)} %get-tuple-element.35), channel_id=1, source_target_pairs={{0,16},{32,48},{64,80},{96,112},{128,144},{160,176},{192,208},{224... | collective-permute-start | bytes 921608 | tf_op jit(solution)/shard_map/ppermute | solution.py:308
  23.6 1.6 %shard_map.67 = (bf16[4,200,128]{2,1,0:T(8,128)(2,1)S(1)}, f32[4,104,256]{2,1,0:T(8,128)S(1)}, bf16[8,1024,256]{2,1,0:T(8,128)(2,1)S(1)}) custom-call(s32[196]{0:T(256)S(1)} %get-tuple-element.27.jobs_ref, bf16[8,200,128]{2,1,0:T(8,128)(2,1)S(1)} %get-tuple-element.28.g_ref, ...), custom_call_target="tpu_custom_call", output_to_operand_aliasing={{2}: (6, {})} | custom-call | flops 3000000000 | bytes 1000000 | tf_op jit(solution)/shard_map/pallas_call | solution.py:384
  25.2 1.0 %collective-permute-done.2.cross_ref = bf16[6,200,128]{2,1,0:T(8,128)(2,1)S(1)} collective-permute-done((bf16[6,200,128]{2,1,0:T(8,128)(2,1)S(1)}, bf16[6,200,128]{2,1,0:T(8,128)(2,1)S(1)}, u32[]{:S(2)}, u32[]{:S(2)}) %collective-permute-start.2) | collective-permute-done | bytes 307232 | tf_op jit(solution)/shard_map/ppermute | solution.py:308
  26.2 0.0 collective-permute-done.3.near_ref
  26.2 3.5 %shard_map.68 = (bf16[8,200,128]{2,1,0:T(8,128)(2,1)}, bf16[8,1024,256]{2,1,0:T(8,128)(2,1)S(1)}) custom-call(s32[196]{0:T(256)S(1)} %get-tuple-element.27.jobs_ref, bf16[6,200,128]{2,1,0:T(8,128)(2,1)S(1)} %collective-permute-done.2.cross_ref, bf16[6,200,128]{2,1,0:T(8,128)(2,1)S(1)} %collective-permute-done.3.near_ref, ...), custom_call_target="tpu_custom_call", output_to_operand_aliasing={{1}: (7, {})} | custom-call | flops 1000000000 | bytes 1000000 | tf_op jit(solution)/shard_map/pallas_call | solution.py:395
Async XLA Ops:
  1.2 11.5 %collective-permute-start = (bf16[4,200,128]{2,1,0:T(8,128)(2,1)S(1)}, bf16[4,200,128]{2,1,0:T(8,128)(2,1)S(1)}, u32[]{:S(2)}, u32[]{:S(2)}) collective-permute-start(bf16[4,200,128]{2,1,0:T(8,128)(2,1)S(1)} %get-tuple-element.29), channel_id=1, source_target_pairs={{1,2},{3,4},{5,6},{7,8},{9,10},{11,12},{13,14},{2,1},{4,3},{6,5},{... | collective-permute-start | bytes 614408 | tf_op jit(solution)/shard_map/ppermute | solution.py:308
  5.8 7.5 %collective-permute-start.1 = (bf16[4,200,128]{2,1,0:T(8,128)(2,1)S(1)}, bf16[4,200,128]{2,1,0:T(8,128)(2,1)S(1)}, u32[]{:S(2)}, u32[]{:S(2)}) collective-permute-start(bf16[4,200,128]{2,1,0:T(8,128)(2,1)S(1)} %get-tuple-element.30), channel_id=1, source_target_pairs={{0,1},{2,3},{4,5},{6,7},{8,9},{10,11},{12,13},{14,15},{1,0},{3,2},... | collective-permute-start | bytes 614408 | tf_op jit(solution)/shard_map/ppermute | solution.py:308
  15.6 10.6 %collective-permute-start.2 = (bf16[6,200,128]{2,1,0:T(8,128)(2,1)S(1)}, bf16[6,200,128]{2,1,0:T(8,128)(2,1)S(1)}, u32[]{:S(2)}, u32[]{:S(2)}) collective-permute-start(bf16[6,200,128]{2,1,0:T(8,128)(2,1)S(1)} %get-tuple-element.34), channel_id=1, source_target_pairs={{16,32},{48,64},{80,96},{112,128},{144,160},{176,192},{208,224},{2... | collective-permute-start | bytes 921608 | tf_op jit(solution)/shard_map/ppermute | solution.py:308
  21.6 4.5 %collective-permute-start.3 = (bf16[6,200,128]{2,1,0:T(8,128)(2,1)S(1)}, bf16[6,200,128]{2,1,0:T(8,128)(2,1)S(1)}, u32[]{:S(2)}, u32[]{:S(2)}) collective-permute-start(bf16[6,200,128]{2,1,0:T(8,128)(2,1)S(1)} %get-tuple-element.35), channel_id=1, source_target_pairs={{0,16},{32,48},{64,80},{96,112},{128,144},{160,176},{192,208},{224... | collective-permute-start | bytes 921608 | tf_op jit(solution)/shard_map/ppermute | solution.py:308

commit v7 on v6

--- a/solution.py
+++ b/solution.py
@@ -29,20 +29,20 @@
     return lax.broadcasted_iota(I32, shape, dim)
 
 
-def pack_kernel(g_hbm, coup_hbm, pairs_hbm, occ_hbm, off_hbm, to_a, to_b, g, coup, pairs, occ, off, sems):
+def pack_kernel(g_hbm, coup_hbm, pairs_hbm, occ_hbm, off_hbm, first, second, g, coup, pairs, occ, off, sems):
     half = ATOMS // 2
     moves = ((g_hbm, g), (coup_hbm, coup), (pairs_hbm, pairs), (occ_hbm, occ), (off_hbm, off))
     copies = [pltpu.make_async_copy(src, dst, sems.at[i]) for i, (src, dst) in enumerate(moves)]
     for copy in copies:
         copy.start()
     odd = lax.axis_index("energy") % 2
-    pick = (iota((SLAB, LANES), 1) // KMAX) == odd
+    pick = (iota((SLAB, LANES), 1) // KMAX) == (odd + 1 + lax.axis_index("atom")) % 2
     copies[0].wait()
     for x in range(half):
         turned = pltpu.roll(g[x + half * odd].astype(F32), KMAX, 1).astype(BF)
         kept = g[x + half - half * odd]
-        to_a[x] = jnp.where(pick, turned, kept)
-        to_b[x] = jnp.where(pick, kept, turned)
+        first[x] = jnp.where(pick, turned, kept)
+        second[x] = jnp.where(pick, kept, turned)
     for copy in copies[1:]:
         copy.wait()
 
@@ -156,17 +156,16 @@
     odd = lax.axis_index("energy") % 2
     e_in = iota((2 * LANES, LANES), 0)
     e_out = iota((2 * LANES, LANES), 1)
-    left_first = jnp.where(e_in < 128, e_in, jnp.where(e_in < 192, e_in - 192, e_in - 64))
-    right_first = jnp.where(e_in < 128, e_in, jnp.where(e_in < 192, e_in, e_in - 256))
-    orders = (jnp.where(odd == 1, left_first, right_first), jnp.where(odd == 1, right_first, left_first))
+    away = jnp.where(e_in < 128, e_in, jnp.where(e_in < 192, e_in - 192, e_in - 64)) - e_out
     for m in range(MODES):
         occ = occ_ref[m]
         step = off_ref[m]
-        for which in range(2):
-            away = orders[which] - e_out
-            s_ref[which, :, m * LANES : (m + 1) * LANES] = jnp.where(
-                away == -step, occ, jnp.where(away == step, occ + 1.0, 0.0)
-            ).astype(BF)
+        band = jnp.where(away == -step, occ, jnp.where(away == step, occ + 1.0, 0.0)).astype(BF)
+        cols = slice(m * LANES, (m + 1) * LANES)
+        s_ref[1 - odd, :, cols] = band
+        s_ref[odd, 0:128, cols] = band[0:128]
+        s_ref[odd, 128:192, cols] = band[192:256]
+        s_ref[odd, 192:256, cols] = band[128:192]
     send.wait()
 
 
@@ -188,11 +187,11 @@
                 )
 
 
-def halo_of(from_a, from_b, x):
-    left = iota((SLAB, LANES), 1) < KMAX
-    a = from_a[x % 4]
-    b = from_b[x % 4]
-    return jnp.where(left, a, b) if x < 4 else jnp.where(left, b, a)
+def halo_of(first, second, x):
+    pick = iota((SLAB, LANES), 1) // KMAX == 1 - lax.axis_index("atom") % 2
+    a = first[x % 4]
+    b = second[x % 4]
+    return jnp.where(pick, a, b) if x < 4 else jnp.where(pick, b, a)
 
 
 def store_in(x_ref, at):
@@ -233,12 +232,12 @@
 
 
 def rim_kernel(
-    jobs_ref, g_ref, from_b, from_a, s_ref, t_ref, x_old, cross_ref, near_ref, x, part, lhs, low, rows, held, sem
+    jobs_ref, g_ref, first, second, s_ref, t_ref, x_old, cross_ref, near_ref, x, part, lhs, low, rows, held, sem
 ):
     lists = Lists(jobs_ref, held, sem)
     halos = []
     for at, atom in enumerate((0, 1, 6, 7)):
-        halos.append(halo_of(from_a, from_b, atom))
+        halos.append(halo_of(first, second, atom))
         shift_atom(g_ref[atom], halos[at], s_ref, atom // 4, lhs.at[at], low.at[at], store_in(x, atom))
     part[...] = jnp.zeros(part.shape, F32)
     run_jobs(lists.ready(), 1, 4, t_ref, x, part)
@@ -262,11 +261,11 @@
 
 
 def local_kernel(
-    jobs_ref, g_ref, from_b, from_a, s_ref, t_ref, x_old, inner_ref, rim_ref, x, acc, lhs, low, rows, held, sem
+    jobs_ref, g_ref, first, second, s_ref, t_ref, x_old, inner_ref, rim_ref, x, acc, lhs, low, rows, held, sem
 ):
     lists = Lists(jobs_ref, held, sem)
     for at, atom in enumerate((2, 3, 4, 5)):
-        halo = halo_of(from_a, from_b, atom)
+        halo = halo_of(first, second, atom)
         shift_atom(g_ref[atom], halo, s_ref, atom // 4, lhs.at[at], low.at[at], store_in(x, atom))
     acc[...] = jnp.zeros(acc.shape, F32)
     run_jobs(lists.ready(), 0, 8, t_ref, x, acc)
@@ -308,6 +307,15 @@
     return lax.ppermute(value, axis, pairs + [(b, a) for a, b in pairs])
 
 
+def mixed_swap(value, start):
+    parts, count = lax.axis_size("atom"), lax.axis_size("energy")
+    pairs = []
+    for part in range(parts):
+        for i in range((start + part) % 2, count - 1, 2):
+            pairs.append((part * count + i, part * count + i + 1))
+    return lax.ppermute(value, ("atom", "energy"), pairs + [(b, a) for a, b in pairs])
+
+
 def call(kernel, outs, scratch, flops, moved, specs, out_specs, aliases={}):
     return pl.pallas_call(
         kernel,
@@ -329,7 +337,7 @@
 
     half = shape((atoms // 2, slab, e_dev), BF)
     taken = (green, coupling, pairs, occupation, offsets)
-    to_a, to_b, g, coup, pairs, occ, off = call(
+    first, second, g, coup, pairs, occ, off = call(
         pack_kernel,
         (half, half) + tuple(shape(v.shape, v.dtype) for v in taken),
         [dma((5,))],
@@ -338,8 +346,8 @@
         [HBM] * 5,
         (VMEM,) * 7,
     )(*[pltpu.with_memory_space_constraint(v, pltpu.HBM) for v in taken])
-    from_b = swap(to_b, "energy", 1)
-    from_a = swap(to_a, "energy", 0)
+    first = mixed_swap(first, 1)
+    second = mixed_swap(second, 0)
 
     shifted = shape((ATOMS, DEPTH, 256), BF)
     t, s, jobs, x = call(
@@ -378,7 +386,7 @@
         [VMEM] * 7,
         (VMEM, VMEM, VMEM),
         {6: 2},
-    )(jobs, g, from_b, from_a, s, t, x)
+    )(jobs, g, first, second, s, t, x)
     cross = swap(cross, "atom", 1)
     near = swap(near, "atom", 0)
     inner, rim, x = call(
@@ -390,7 +398,7 @@
         [VMEM] * 7,
         (VMEM,) * 3,
         {6: 2},
-    )(jobs, g, from_b, from_a, s, t, x)
+    )(jobs, g, first, second, s, t, x)
 
     return call(
         final_kernel,

time: 29.9 us -> 29.2 us (0.977)
  waiting for transfers between devices: 1.53 us -> 0.13 us
  Pallas kernels: 13 us -> 13.5 us
    ppermute x0 -> x2, starting transfers between devices: none -> 7.02 us  [mixed_swap(): lax.ppermute(value, ('atom', 'energy'), pairs + [(b, a) for a, b in pairs])]
    ppermute x4 -> x2, starting transfers between devices: 14.4 us -> 7.47 us  [swap(): return lax.ppermute(value, axis, pairs + [(b, a) for a, b in pairs])]
    ppermute x4 -> x2, waiting for transfers between devices: 1.53 us -> 0.12 us  [swap(): return lax.ppermute(value, axis, pairs + [(b, a) for a, b in pairs])]
    pallas_call x1, Pallas kernels: 1.62 us -> 2.47 us  [per_device(): call(local_kernel, (shape((4, slab, e_dev), BF), shape((4, ROWS, 256), F3...]
    pallas_call x1, Pallas kernels: 3.49 us -> 2.99 us  [per_device(): call(final_kernel, (shape((atoms, slab, e_dev), BF), shifted), [pltpu.VME...]
  transfers between devices with their start and end apart: 4 -> 4, of which waited for: 2 -> 1; matrix products, arithmetic and copies ran while one was open for 0% -> 0% of each run, Pallas kernels for 20% -> 24%
where the time goes in v7:
time: 29.2 us; the launch traced here: 28.8 us
  starting transfers between devices  14.5 us (50%)
  Pallas kernels  13.5 us (46%)
  between operations  0.73 us (2%)
    ppermute x2, starting transfers between devices, swap(): return lax.ppermute(value, axis, pairs + [(b, a) for a, b in pairs])  7.47 us
    ppermute x2, starting transfers between devices, mixed_swap(): lax.ppermute(value, ('atom', 'energy'), pairs + [(b, a) for a, b in pairs])  7.02 us
    pallas_call x1, Pallas kernels, per_device(): call(build_kernel, (shape((2 * SLOTS, ROWS, DEPTH), BF), shape((2, 256, D...  4.54 us
    pallas_call x1, Pallas kernels, per_device(): call(final_kernel, (shape((atoms, slab, e_dev), BF), shifted), [pltpu.VME...  2.99 us
    pallas_call x1, Pallas kernels, per_device(): call(local_kernel, (shape((4, slab, e_dev), BF), shape((4, ROWS, 256), F3...  2.47 us
    pallas_call x1, Pallas kernels, per_device(): call(rim_kernel, (payload, payload, shifted), [pltpu.VMEM((5, ROWS, 256),...  2.29 us
    pallas_call x1, Pallas kernels, per_device(): call(pack_kernel, (half, half) + tuple((shape(v.shape, v.dtype) for v in...  1.2 us
  transfers between devices with their start and end apart: 4, of which 1 were waited for; matrix products, arithmetic and copies ran while one was open for 0% of the time, Pallas kernels for 24%

profile of v7, /device:TPU:121, one launch (start us, length us, event | category | flops | bytes accessed | tf_op | source)
XLA Modules:
  0.0 28.8 jit_solution(8326342466355159392)
XLA Ops:
  0.0 1.2 %shard_map.64 = (bf16[4,200,128]{2,1,0:T(8,128)(2,1)S(1)}, bf16[4,200,128]{2,1,0:T(8,128)(2,1)S(1)}, bf16[8,200,128]{2,1,0:T(8,128)(2,1)S(1)}, bf16[16,800]{1,0:...) custom-call(bf16[8,200,128]{2,1,0:T(8,128)(2,1)} %g_hbm.1, bf16[16,800]{1,0:T(8,128)(2,1)} %coup_hbm.1, ...), custom_call_target="tpu_custom_call" | custom-call | flops 1000000 | bytes 1000000 | tf_op jit(solution)/shard_map/pallas_call | solution.py:340
  1.2 3.1 %collective-permute-start = (bf16[4,200,128]{2,1,0:T(8,128)(2,1)S(1)}, bf16[4,200,128]{2,1,0:T(8,128)(2,1)S(1)}, u32[]{:S(2)}, u32[]{:S(2)}) collective-permute-start(bf16[4,200,128]{2,1,0:T(8,128)(2,1)S(1)} %get-tuple-element.29), channel_id=1, source_target_pairs={{1,2},{3,4},{5,6},{7,8},{9,10},{11,12},{13,14},{16,17},{18,19},{20... | collective-permute-start | bytes 614408 | tf_op jit(solution)/shard_map/ppermute | solution.py:316
  4.3 3.9 %collective-permute-start.1 = (bf16[4,200,128]{2,1,0:T(8,128)(2,1)S(1)}, bf16[4,200,128]{2,1,0:T(8,128)(2,1)S(1)}, u32[]{:S(2)}, u32[]{:S(2)}) collective-permute-start(bf16[4,200,128]{2,1,0:T(8,128)(2,1)S(1)} %get-tuple-element.30), channel_id=1, source_target_pairs={{0,1},{2,3},{4,5},{6,7},{8,9},{10,11},{12,13},{14,15},{17,18},{19,... | collective-permute-start | bytes 614408 | tf_op jit(solution)/shard_map/ppermute | solution.py:316
  8.9 4.5 %shard_map.65 = (bf16[32,104,1024]{2,1,0:T(8,128)(2,1)S(1)}, bf16[2,256,1024]{2,1,0:T(8,128)(2,1)S(1)}, s32[196]{0:T(256)S(1)}, bf16[8,1024,256]{2,1,0:T(8,128)(2,1)S(1)}) custom-call(s32[1]{0:T(128)S(6)} %copy.13.cnt_ref, s32[2,16]{1,0:T(2,128)S(1)} %get-tuple-element.23.pairs_in, f32[8]{0:T(128)S(1)} %get-tuple-element.24.occ_in, ...), custom_call_target="tpu_custom_call" | custom-call | flops 3000000000 | bytes 8000000 | tf_op jit(solution)/shard_map/pallas_call | solution.py:353
  13.4 0.0 collective-permute-done.first
  13.5 0.0 collective-permute-done.1.second
  13.5 2.3 %shard_map.66 = (bf16[6,200,128]{2,1,0:T(8,128)(2,1)S(1)}, bf16[6,200,128]{2,1,0:T(8,128)(2,1)S(1)}, bf16[8,1024,256]{2,1,0:T(8,128)(2,1)S(1)}) custom-call(s32[196]{0:T(256)S(1)} %get-tuple-element.27.jobs_ref, bf16[8,200,128]{2,1,0:T(8,128)(2,1)S(1)} %get-tuple-element.28.g_ref, ...), custom_call_target="tpu_custom_call", output_to_operand_aliasing={{2}: (6, {})} | custom-call | flops 1000000000 | bytes 1000000 | tf_op jit(solution)/shard_map/pallas_call | solution.py:380
  15.8 5.5 %collective-permute-start.2 = (bf16[6,200,128]{2,1,0:T(8,128)(2,1)S(1)}, bf16[6,200,128]{2,1,0:T(8,128)(2,1)S(1)}, u32[]{:S(2)}, u32[]{:S(2)}) collective-permute-start(bf16[6,200,128]{2,1,0:T(8,128)(2,1)S(1)} %get-tuple-element.34), channel_id=1, source_target_pairs={{16,32},{48,64},{80,96},{112,128},{144,160},{176,192},{208,224},{2... | collective-permute-start | bytes 921608 | tf_op jit(solution)/shard_map/ppermute | solution.py:307
  21.3 1.9 %collective-permute-start.3 = (bf16[6,200,128]{2,1,0:T(8,128)(2,1)S(1)}, bf16[6,200,128]{2,1,0:T(8,128)(2,1)S(1)}, u32[]{:S(2)}, u32[]{:S(2)}) collective-permute-start(bf16[6,200,128]{2,1,0:T(8,128)(2,1)S(1)} %get-tuple-element.35), channel_id=1, source_target_pairs={{0,16},{32,48},{64,80},{96,112},{128,144},{160,176},{192,208},{224... | collective-permute-start | bytes 921608 | tf_op jit(solution)/shard_map/ppermute | solution.py:307
  23.2 2.5 %shard_map.67 = (bf16[4,200,128]{2,1,0:T(8,128)(2,1)S(1)}, f32[4,104,256]{2,1,0:T(8,128)S(1)}, bf16[8,1024,256]{2,1,0:T(8,128)(2,1)S(1)}) custom-call(s32[196]{0:T(256)S(1)} %get-tuple-element.27.jobs_ref, bf16[8,200,128]{2,1,0:T(8,128)(2,1)S(1)} %get-tuple-element.28.g_ref, ...), custom_call_target="tpu_custom_call", output_to_operand_aliasing={{2}: (6, {})} | custom-call | flops 3000000000 | bytes 1000000 | tf_op jit(solution)/shard_map/pallas_call | solution.py:392
  25.7 0.1 collective-permute-done.2.cross_ref
  25.8 0.0 collective-permute-done.3.near_ref
  25.8 3.0 %shard_map.68 = (bf16[8,200,128]{2,1,0:T(8,128)(2,1)}, bf16[8,1024,256]{2,1,0:T(8,128)(2,1)S(1)}) custom-call(s32[196]{0:T(256)S(1)} %get-tuple-element.27.jobs_ref, bf16[6,200,128]{2,1,0:T(8,128)(2,1)S(1)} %collective-permute-done.2.cross_ref, bf16[6,200,128]{2,1,0:T(8,128)(2,1)S(1)} %collective-permute-done.3.near_ref, ...), custom_call_target="tpu_custom_call", output_to_operand_aliasing={{1}: (7, {})} | custom-call | flops 1000000000 | bytes 1000000 | tf_op jit(solution)/shard_map/pallas_call | solution.py:403
Async XLA Ops:
  1.2 12.2 %collective-permute-start = (bf16[4,200,128]{2,1,0:T(8,128)(2,1)S(1)}, bf16[4,200,128]{2,1,0:T(8,128)(2,1)S(1)}, u32[]{:S(2)}, u32[]{:S(2)}) collective-permute-start(bf16[4,200,128]{2,1,0:T(8,128)(2,1)S(1)} %get-tuple-element.29), channel_id=1, source_target_pairs={{1,2},{3,4},{5,6},{7,8},{9,10},{11,12},{13,14},{16,17},{18,19},{20... | collective-permute-start | bytes 614408 | tf_op jit(solution)/shard_map/ppermute | solution.py:316
  4.3 9.1 %collective-permute-start.1 = (bf16[4,200,128]{2,1,0:T(8,128)(2,1)S(1)}, bf16[4,200,128]{2,1,0:T(8,128)(2,1)S(1)}, u32[]{:S(2)}, u32[]{:S(2)}) collective-permute-start(bf16[4,200,128]{2,1,0:T(8,128)(2,1)S(1)} %get-tuple-element.30), channel_id=1, source_target_pairs={{0,1},{2,3},{4,5},{6,7},{8,9},{10,11},{12,13},{14,15},{17,18},{19,... | collective-permute-start | bytes 614408 | tf_op jit(solution)/shard_map/ppermute | solution.py:316
  15.8 10.1 %collective-permute-start.2 = (bf16[6,200,128]{2,1,0:T(8,128)(2,1)S(1)}, bf16[6,200,128]{2,1,0:T(8,128)(2,1)S(1)}, u32[]{:S(2)}, u32[]{:S(2)}) collective-permute-start(bf16[6,200,128]{2,1,0:T(8,128)(2,1)S(1)} %get-tuple-element.34), channel_id=1, source_target_pairs={{16,32},{48,64},{80,96},{112,128},{144,160},{176,192},{208,224},{2... | collective-permute-start | bytes 921608 | tf_op jit(solution)/shard_map/ppermute | solution.py:307
  21.3 4.5 %collective-permute-start.3 = (bf16[6,200,128]{2,1,0:T(8,128)(2,1)S(1)}, bf16[6,200,128]{2,1,0:T(8,128)(2,1)S(1)}, u32[]{:S(2)}, u32[]{:S(2)}) collective-permute-start(bf16[6,200,128]{2,1,0:T(8,128)(2,1)S(1)} %get-tuple-element.35), channel_id=1, source_target_pairs={{0,16},{32,48},{64,80},{96,112},{128,144},{160,176},{192,208},{224... | collective-permute-start | bytes 921608 | tf_op jit(solution)/shard_map/ppermute | solution.py:307

commit v8 on v7

--- a/solution.py
+++ b/solution.py
@@ -1,3 +1,5 @@
+import functools
+
 import jax
 import jax.numpy as jnp
 from jax import lax
@@ -61,23 +63,23 @@
             x_ref[x, m * LANES + 96 : (m + 1) * LANES, :] = jnp.zeros((32, 256), BF)
 
     def listed(s, carry):
-        near, far, down, up = carry
+        near, down, up, far = carry
         first = pairs_ref[0, s] - base
         second = pairs_ref[1, s] - base
         local = jnp.where((second >= 0) & (second < ATOMS), 1, 0)
         below = jnp.where(second < 0, 1, 0)
-        out = jnp.where(second < 0, second + 2, second - 6)
+        above = 1 - local - below
         jobs_ref[near] = s + 64 * second + 4096 * first
         jobs_ref[near + 1] = s + SLOTS + 64 * first + 4096 * second
-        jobs_ref[LISTS + far] = s + SLOTS + 64 * first + 4096 * out
-        jobs_ref[2 * LISTS + down] = s + 64 * out + 4096 * first
-        jobs_ref[3 * LISTS + up] = s + 64 * out + 4096 * (first - 6)
-        return near + 2 * local, far + 1 - local, down + below, up + 1 - local - below
+        jobs_ref[LISTS + down] = s + SLOTS + 64 * first + 4096 * (second + 2)
+        jobs_ref[2 * LISTS + up] = s + SLOTS + 64 * first + 4096 * (second - ATOMS)
+        jobs_ref[3 * LISTS + far] = s + 64 * (second + 2 - 8 * above) + 4096 * (first - 4 * above)
+        return near + 2 * local, down + below, up + above, far + 1 - local
 
     for copy in copies:
         copy.wait()
     counted = lax.fori_loop(0, count, listed, (jnp.int32(0),) * 4)
-    for kind, (many, spare) in enumerate(zip(counted, (ATOMS, 4, 2, 2))):
+    for kind, (many, spare) in enumerate(zip(counted, (ATOMS, 2, 2, 4))):
         for j in range(8):
             jobs_ref[kind * LISTS + many + j] = 4096 * spare
         jobs_ref[4 * LISTS + kind] = many
@@ -232,32 +234,21 @@
 
 
 def rim_kernel(
-    jobs_ref, g_ref, first, second, s_ref, t_ref, x_old, cross_ref, near_ref, x, part, lhs, low, rows, held, sem
+    near, jobs_ref, g_ref, first, second, s_ref, t_ref, x_old, pay_ref, x, part, lhs, low, rows, held, sem
 ):
     lists = Lists(jobs_ref, held, sem)
-    halos = []
-    for at, atom in enumerate((0, 1, 6, 7)):
-        halos.append(halo_of(first, second, atom))
-        shift_atom(g_ref[atom], halos[at], s_ref, atom // 4, lhs.at[at], low.at[at], store_in(x, atom))
+    side = (near + lax.axis_index("atom")) % 2
+    pick = iota((SLAB, LANES), 1) // KMAX == 1 - near
+    for j in range(2):
+        center = g_ref[6 * side + j]
+        halo = jnp.where(pick, first[2 * side + j], second[2 * side + j])
+        pay_ref[j] = center
+        pay_ref[2 + j] = halo
+        shift_atom(center, halo, s_ref, side, lhs.at[j], low.at[j], store_in(x, 6 * side + j))
     part[...] = jnp.zeros(part.shape, F32)
-    run_jobs(lists.ready(), 1, 4, t_ref, x, part)
-    odd = lax.axis_index("atom") % 2
-
-    def fill(ref, side):
-        for j in range(2):
-            ref[j] = g_ref[6 * side + j]
-            ref[2 + j] = halos[2 * side + j]
-            ref[4 + j] = unfold(part[2 * side + j], rows.at[2 * side + j]).astype(BF)
-
-    @pl.when(odd == 1)
-    def _():
-        fill(cross_ref, 1)
-        fill(near_ref, 0)
-
-    @pl.when(odd == 0)
-    def _():
-        fill(cross_ref, 0)
-        fill(near_ref, 1)
+    run_jobs(lists.ready(), 1 + side, 4, t_ref, x, part)
+    for j in range(2):
+        pay_ref[4 + j] = unfold(part[j], rows.at[j]).astype(BF)
 
 
 def local_kernel(
@@ -286,14 +277,13 @@
         for j in range(2):
             at = 2 * n + j
             shift_atom(ref[j], ref[2 + j], s_ref, 1 - side, lhs.at[at], low.at[at], store_in(x, 2 * side + j))
-            acc[3 * n + j] = rim_ref[2 * side + j]
-    held = lists.ready()
+    acc[0:4] = rim_ref[...]
+    run_jobs(lists.ready(), 3, 4, t_ref, x, acc)
     copies = [early]
     for n, (side, ref) in enumerate(sides):
-        run_jobs(held, 2 + side, 4, t_ref, x, acc.at[pl.ds(3 * n, 3)])
         for j in range(2):
             at = 2 * n + j
-            done[at] = (unfold(acc[3 * n + j], rows.at[at]) + ref[4 + j].astype(F32)).astype(BF)
+            done[at] = (unfold(acc[2 * side + j], rows.at[at]) + ref[4 + j].astype(F32)).astype(BF)
         copy = pltpu.make_async_copy(done.at[pl.ds(2 * n, 2)], out_ref.at[pl.ds(6 * side, 2)], sems.at[1 + n])
         copy.start()
         copies.append(copy)
@@ -377,18 +367,20 @@
         dma(()),
     ]
     payload = shape((6, slab, e_dev), BF)
-    cross, near, x = call(
-        rim_kernel,
-        (payload, payload, shifted),
-        [pltpu.VMEM((5, ROWS, 256), F32)] + spare,
-        int(1e9),
-        int(1e6),
-        [VMEM] * 7,
-        (VMEM, VMEM, VMEM),
-        {6: 2},
-    )(jobs, g, first, second, s, t, x)
-    cross = swap(cross, "atom", 1)
-    near = swap(near, "atom", 0)
+    swapped = []
+    for near in range(2):
+        pay, x = call(
+            functools.partial(rim_kernel, near),
+            (payload, shifted),
+            [pltpu.VMEM((3, ROWS, 256), F32)] + spare,
+            int(5e8),
+            int(1e6),
+            [VMEM] * 7,
+            (VMEM, VMEM),
+            {6: 1},
+        )(jobs, g, first, second, s, t, x)
+        swapped.append(swap(pay, "atom", 1 - near))
+    cross, near = swapped
     inner, rim, x = call(
         local_kernel,
         (shape((4, slab, e_dev), BF), shape((4, ROWS, 256), F32), shifted),
@@ -403,7 +395,7 @@
     return call(
         final_kernel,
         (shape((atoms, slab, e_dev), BF), shifted),
-        [pltpu.VMEM((6, ROWS, 256), F32), pltpu.VMEM((4, slab, e_dev), BF)] + spare + [dma((3,))],
+        [pltpu.VMEM((5, ROWS, 256), F32), pltpu.VMEM((4, slab, e_dev), BF)] + spare + [dma((3,))],
         int(1e9),
         int(1e6),
         [VMEM] * 8,

time: 29.2 us -> 28.9 us (0.990)
  the two profiles are of different devices: /device:TPU:121 before, /device:TPU:248 now
where the time goes in v8:
time: 28.9 us; the launch traced here: 28.7 us
  starting transfers between devices  13.9 us (48%)
  Pallas kernels  13.8 us (48%)
  between operations  0.74 us (3%)
  waiting for transfers between devices  0.32 us (1%)
    ppermute x2, starting transfers between devices, swap(): return lax.ppermute(value, axis, pairs + [(b, a) for a, b in pairs])  7.06 us
    ppermute x2, starting transfers between devices, mixed_swap(): lax.ppermute(value, ('atom', 'energy'), pairs + [(b, a) for a, b in pairs])  6.8 us
    pallas_call x1, Pallas kernels, per_device(): call(build_kernel, (shape((2 * SLOTS, ROWS, DEPTH), BF), shape((2, 256, D...  4.71 us
    pallas_call x1, Pallas kernels, per_device(): call(local_kernel, (shape((4, slab, e_dev), BF), shape((4, ROWS, 256), F3...  3.27 us
    pallas_call x1, Pallas kernels, per_device(): call(final_kernel, (shape((atoms, slab, e_dev), BF), shifted), [pltpu.VME...  2.42 us
    pallas_call x2, Pallas kernels, per_device(): call(functools.partial(rim_kernel, near), (payload, shifted), [pltpu.VMEM...  2.2 us
    pallas_call x1, Pallas kernels, per_device(): call(pack_kernel, (half, half) + tuple((shape(v.shape, v.dtype) for v in...  1.2 us
  transfers between devices with their start and end apart: 4, of which 1 were waited for; matrix products, arithmetic and copies ran while one was open for 0% of the time, Pallas kernels for 32%

profile of v8, /device:TPU:248, one launch (start us, length us, event | category | flops | bytes accessed | tf_op | source)
XLA Modules:
  0.0 28.7 jit_solution(2728002279590175046)
XLA Ops:
  0.0 1.2 %shard_map.64 = (bf16[4,200,128]{2,1,0:T(8,128)(2,1)S(1)}, bf16[4,200,128]{2,1,0:T(8,128)(2,1)S(1)}, bf16[8,200,128]{2,1,0:T(8,128)(2,1)S(1)}, bf16[16,800]{1,0:...) custom-call(bf16[8,200,128]{2,1,0:T(8,128)(2,1)} %g_hbm.1, bf16[16,800]{1,0:T(8,128)(2,1)} %coup_hbm.1, ...), custom_call_target="tpu_custom_call" | custom-call | flops 1000000 | bytes 1000000 | tf_op jit(solution)/shard_map/pallas_call | solution.py:330
  1.2 4.8 %collective-permute-start = (bf16[4,200,128]{2,1,0:T(8,128)(2,1)S(1)}, bf16[4,200,128]{2,1,0:T(8,128)(2,1)S(1)}, u32[]{:S(2)}, u32[]{:S(2)}) collective-permute-start(bf16[4,200,128]{2,1,0:T(8,128)(2,1)S(1)} %get-tuple-element.30), channel_id=1, source_target_pairs={{1,2},{3,4},{5,6},{7,8},{9,10},{11,12},{13,14},{16,17},{18,19},{20... | collective-permute-start | bytes 614408 | tf_op jit(solution)/shard_map/ppermute | solution.py:306
  6.1 2.0 %collective-permute-start.1 = (bf16[4,200,128]{2,1,0:T(8,128)(2,1)S(1)}, bf16[4,200,128]{2,1,0:T(8,128)(2,1)S(1)}, u32[]{:S(2)}, u32[]{:S(2)}) collective-permute-start(bf16[4,200,128]{2,1,0:T(8,128)(2,1)S(1)} %get-tuple-element.31), channel_id=1, source_target_pairs={{0,1},{2,3},{4,5},{6,7},{8,9},{10,11},{12,13},{14,15},{17,18},{19,... | collective-permute-start | bytes 614408 | tf_op jit(solution)/shard_map/ppermute | solution.py:306
  8.7 4.7 %shard_map.65 = (bf16[32,104,1024]{2,1,0:T(8,128)(2,1)S(1)}, bf16[2,256,1024]{2,1,0:T(8,128)(2,1)S(1)}, s32[196]{0:T(256)S(1)}, bf16[8,1024,256]{2,1,0:T(8,128)(2,1)S(1)}) custom-call(s32[1]{0:T(128)S(6)} %copy.15.cnt_ref, s32[2,16]{1,0:T(2,128)S(1)} %get-tuple-element.24.pairs_in, f32[8]{0:T(128)S(1)} %get-tuple-element.25.occ_in, ...), custom_call_target="tpu_custom_call" | custom-call | flops 3000000000 | bytes 8000000 | tf_op jit(solution)/shard_map/pallas_call | solution.py:343
  13.4 0.0 collective-permute-done.first
  13.4 0.3 %collective-permute-done.1.second = bf16[4,200,128]{2,1,0:T(8,128)(2,1)S(1)} collective-permute-done((bf16[4,200,128]{2,1,0:T(8,128)(2,1)S(1)}, bf16[4,200,128]{2,1,0:T(8,128)(2,1)S(1)}, u32[]{:S(2)}, u32[]{:S(2)}) %collective-permute-start.1) | collective-permute-done | bytes 204832 | tf_op jit(solution)/shard_map/ppermute | solution.py:306
  13.7 1.1 %shard_map.66 = (bf16[6,200,128]{2,1,0:T(8,128)(2,1)S(1)}, bf16[8,1024,256]{2,1,0:T(8,128)(2,1)S(1)}) custom-call(s32[196]{0:T(256)S(1)} %get-tuple-element.28.jobs_ref, bf16[8,200,128]{2,1,0:T(8,128)(2,1)S(1)} %get-tuple-element.29.g_ref, bf16[4,200,128]{2,1,0:T(8,128)(2,1)S(1)} %collective-permute-done.first, ...), custom_call_target="tpu_custom_call", output_to_operand_aliasing={{1}: (6, {})} | custom-call | flops 500000000 | bytes 1000000 | tf_op jit(solution)/shard_map/pallas_call | solution.py:372
  14.8 1.9 %collective-permute-start.2 = (bf16[6,200,128]{2,1,0:T(8,128)(2,1)S(1)}, bf16[6,200,128]{2,1,0:T(8,128)(2,1)S(1)}, u32[]{:S(2)}, u32[]{:S(2)}) collective-permute-start(bf16[6,200,128]{2,1,0:T(8,128)(2,1)S(1)} %get-tuple-element.35), channel_id=1, source_target_pairs={{16,32},{48,64},{80,96},{112,128},{144,160},{176,192},{208,224},{2... | collective-permute-start | bytes 921608 | tf_op jit(solution)/shard_map/ppermute | solution.py:297
  16.7 1.1 %shard_map.67 = (bf16[6,200,128]{2,1,0:T(8,128)(2,1)S(1)}, bf16[8,1024,256]{2,1,0:T(8,128)(2,1)S(1)}) custom-call(s32[196]{0:T(256)S(1)} %get-tuple-element.28.jobs_ref, bf16[8,200,128]{2,1,0:T(8,128)(2,1)S(1)} %get-tuple-element.29.g_ref, bf16[4,200,128]{2,1,0:T(8,128)(2,1)S(1)} %collective-permute-done.first, ...), custom_call_target="tpu_custom_call", output_to_operand_aliasing={{1}: (6, {})} | custom-call | flops 500000000 | bytes 1000000 | tf_op jit(solution)/shard_map/pallas_call | solution.py:372
  17.9 5.1 %collective-permute-start.3 = (bf16[6,200,128]{2,1,0:T(8,128)(2,1)S(1)}, bf16[6,200,128]{2,1,0:T(8,128)(2,1)S(1)}, u32[]{:S(2)}, u32[]{:S(2)}) collective-permute-start(bf16[6,200,128]{2,1,0:T(8,128)(2,1)S(1)} %get-tuple-element.37), channel_id=1, source_target_pairs={{0,16},{32,48},{64,80},{96,112},{128,144},{160,176},{192,208},{224... | collective-permute-start | bytes 921608 | tf_op jit(solution)/shard_map/ppermute | solution.py:297
  23.0 3.3 %shard_map.68 = (bf16[4,200,128]{2,1,0:T(8,128)(2,1)S(1)}, f32[4,104,256]{2,1,0:T(8,128)S(1)}, bf16[8,1024,256]{2,1,0:T(8,128)(2,1)S(1)}) custom-call(s32[196]{0:T(256)S(1)} %get-tuple-element.28.jobs_ref, bf16[8,200,128]{2,1,0:T(8,128)(2,1)S(1)} %get-tuple-element.29.g_ref, ...), custom_call_target="tpu_custom_call", output_to_operand_aliasing={{2}: (6, {})} | custom-call | flops 3000000000 | bytes 1000000 | tf_op jit(solution)/shard_map/pallas_call | solution.py:384
  26.3 0.0 collective-permute-done.2.cross_ref
  26.3 0.0 collective-permute-done.3.near_ref
  26.3 2.4 %shard_map.69 = (bf16[8,200,128]{2,1,0:T(8,128)(2,1)}, bf16[8,1024,256]{2,1,0:T(8,128)(2,1)S(1)}) custom-call(s32[196]{0:T(256)S(1)} %get-tuple-element.28.jobs_ref, bf16[6,200,128]{2,1,0:T(8,128)(2,1)S(1)} %collective-permute-done.2.cross_ref, bf16[6,200,128]{2,1,0:T(8,128)(2,1)S(1)} %collective-permute-done.3.near_ref, ...), custom_call_target="tpu_custom_call", output_to_operand_aliasing={{1}: (7, {})} | custom-call | flops 1000000000 | bytes 1000000 | tf_op jit(solution)/shard_map/pallas_call | solution.py:395
Async XLA Ops:
  1.2 12.2 %collective-permute-start = (bf16[4,200,128]{2,1,0:T(8,128)(2,1)S(1)}, bf16[4,200,128]{2,1,0:T(8,128)(2,1)S(1)}, u32[]{:S(2)}, u32[]{:S(2)}) collective-permute-start(bf16[4,200,128]{2,1,0:T(8,128)(2,1)S(1)} %get-tuple-element.30), channel_id=1, source_target_pairs={{1,2},{3,4},{5,6},{7,8},{9,10},{11,12},{13,14},{16,17},{18,19},{20... | collective-permute-start | bytes 614408 | tf_op jit(solution)/shard_map/ppermute | solution.py:306
  6.1 7.7 %collective-permute-start.1 = (bf16[4,200,128]{2,1,0:T(8,128)(2,1)S(1)}, bf16[4,200,128]{2,1,0:T(8,128)(2,1)S(1)}, u32[]{:S(2)}, u32[]{:S(2)}) collective-permute-start(bf16[4,200,128]{2,1,0:T(8,128)(2,1)S(1)} %get-tuple-element.31), channel_id=1, source_target_pairs={{0,1},{2,3},{4,5},{6,7},{8,9},{10,11},{12,13},{14,15},{17,18},{19,... | collective-permute-start | bytes 614408 | tf_op jit(solution)/shard_map/ppermute | solution.py:306
  14.8 11.5 %collective-permute-start.2 = (bf16[6,200,128]{2,1,0:T(8,128)(2,1)S(1)}, bf16[6,200,128]{2,1,0:T(8,128)(2,1)S(1)}, u32[]{:S(2)}, u32[]{:S(2)}) collective-permute-start(bf16[6,200,128]{2,1,0:T(8,128)(2,1)S(1)} %get-tuple-element.35), channel_id=1, source_target_pairs={{16,32},{48,64},{80,96},{112,128},{144,160},{176,192},{208,224},{2... | collective-permute-start | bytes 921608 | tf_op jit(solution)/shard_map/ppermute | solution.py:297
  17.9 8.4 %collective-permute-start.3 = (bf16[6,200,128]{2,1,0:T(8,128)(2,1)S(1)}, bf16[6,200,128]{2,1,0:T(8,128)(2,1)S(1)}, u32[]{:S(2)}, u32[]{:S(2)}) collective-permute-start(bf16[6,200,128]{2,1,0:T(8,128)(2,1)S(1)} %get-tuple-element.37), channel_id=1, source_target_pairs={{0,16},{32,48},{64,80},{96,112},{128,144},{160,176},{192,208},{224... | collective-permute-start | bytes 921608 | tf_op jit(solution)/shard_map/ppermute | solution.py:297
